TPU v7x, 256 devices: a whole 4x4x8 slice. The times are simulated.
256 devices in a mesh: inplane: 8 (over x_hi, y), row: 32 (over x_lo, z, core).
Axes of the slice: x: 4 (x_hi: 2, x_lo: 2; x = x_hi * 2 + x_lo), y: 4, z: 8, core: 2. Of those that a mesh axis runs over, the one named last changes fastest.
Arguments:
- amplitudes: float32 [1024, 1024], P('row'), may hold values from -6 to 6
- previous: float32 [1024, 1024], P('row'), may hold values from -6 to 6
- coupling: bfloat16 [1024, 1024, 1024], P('inplane', 'row'), may hold values from -0.1875 to 0.1875
- stiffness: float32 [1024], replicated, may hold values from 0.01 to 3
- airy_scale: float32 [1024], P('inplane'), may hold values from 256 to 2560
- damping: float32 [1024], replicated, may hold values from 0.01 to 0.5
- strike_mode: int32 [1024], P('row'), may hold values from 0 to 1023
- strike_offset: int32 [1024], P('row'), may hold values from 0 to 127
Outputs:
- next_amplitudes: float32 [1024, 1024], P('row')
- airy: float32 [1024, 1024], P(None, 'inplane')
All inputs are finite; a program needn't handle non-finite values.
Results may differ from a plain program's by a relative error of at most 0.0047.
Values may be sent and summed in bfloat16 or wider, within the bound.
No kernel may reach another device: no remote copies, remote signals or barrier semaphores. Data moves between devices by JAX's collectives and lax.ppermute only.
A program may use at most 128 MiB of HBM per device.

v0:
```python
import jax
import jax.numpy as jnp
from jax import lax
from jax.sharding import PartitionSpec as P

STRIKE_LEN = 64


def shards(
    amplitudes, previous, coupling, stiffness, airy_scale, damping, strike_mode, strike_offset
):
    slab_modes, row_modes, width = coupling.shape
    flat = coupling.reshape(slab_modes * row_modes, width)
    first_row = lax.axis_index("row") * row_modes
    rounded = amplitudes.astype(jnp.bfloat16)
    gathered = lax.all_gather(rounded, "row", axis=0, tiled=True)
    inner = lax.dot_general(
        flat, gathered, (((1,), (1,)), ((), ())), preferred_element_type=jnp.float32
    )
    inner = inner.reshape(slab_modes, row_modes, gathered.shape[0])
    columns = lax.dynamic_slice_in_dim(gathered, first_row, row_modes, 1).astype(jnp.float32).T
    inner, airy_cols = (inner, jnp.sum(inner * columns[None, :, :], axis=1))
    airy = lax.psum(airy_cols.T, "row") / airy_scale[None, :]
    weights = airy.T
    partial_force = jnp.sum(weights[:, None, :] * inner, axis=0).T
    summed = lax.psum(partial_force, "inplane")
    force = lax.all_to_all(summed, "row", split_axis=0, concat_axis=1, tiled=True)
    offset = strike_offset.astype(jnp.float32)
    pulse = jnp.where(
        strike_offset <= STRIKE_LEN, 2.0 * (1.0 - jnp.cos(jnp.pi * offset / STRIKE_LEN)), 0.0
    )
    modes = jnp.arange(width, dtype=jnp.int32)
    excite = jnp.where(modes[None, :] == strike_mode[:, None], pulse[:, None], 0.0)
    result = (
        2.0 * amplitudes - (1.0 - damping) * previous - stiffness * amplitudes - force + excite
    ) / (1.0 + damping)
    return (result, airy)


def solution(mesh):
    return jax.shard_map(
        shards,
        mesh=mesh,
        in_specs=(
            P("row", None),
            P("row", None),
            P("inplane", "row", None),
            P(),
            P("inplane"),
            P(),
            P("row"),
            P("row"),
        ),
        out_specs=(P("row", None), P(None, "inplane")),
        check_vma=False,
    )
```

profile of v0, /device:TPU:2, one launch (start us, length us, event | category | flops | bytes accessed | tf_op | source)
XLA Modules:
  0.0 458.8 jit_solution(15962825775076068463)
XLA Ops:
  7.2 0.0 all-gather.2.cloned.1.call-start
  7.2 1.5 convert_element_type.7
  8.8 0.0 all-gather.2.cloned.1.call-update
  8.8 0.0 all-reduce.3.cloned.1.call-start
  8.8 68.8 %all-gather.2.cloned.1.call-done = bf16[1024,1024]{1,0:T(8,128)(2,1)} async-done(((bf16[32,1024]{1,0:T(8,128)(2,1)}), bf16[1024,1024]{1,0:T(8,128)(2,1)}) %all-gather.2.cloned.1.call-update) | async-done | bytes 2097168 | tf_op jit(solution)/shard_map/all_gather | solution.py:16
  77.6 1.1 convert_bitcast_fusion
  78.7 0.2 copy.21
  78.9 29.6 %multiply_reduce_fusion.1 = (f32[128,1024]{1,0:T(8,128)}, f32[128,32,1024]{2,0,1:T(8,128)}) fusion(f32[32,1024]{1,0:T(8,128)S(1)} %copy.21, bf16[1024,1024]{1,0:T(8,128)(2,1)} %all-gather.2.cloned.1.call-done, bf16[128,32,1024]{2,1,0:T(8,128)(2,1)} %param.10), kind=kOutput, calls=%fused_computation.1 | convolution fusion | flops 8598192128 | bytes 27918336 | tf_op jit(solution)/shard_map/dot_general | solution.py:17
  108.5 0.0 all-reduce.3.cloned.1.call-update
  108.5 0.2 all-reduce.5.cloned.1.call-start
  108.7 221.4 %all-reduce.3.cloned.1.call-done = f32[1024,128]{0,1:T(8,128)} async-done(((f32[1024,128]{0,1:T(8,128)}), f32[1024,128]{0,1:T(8,128)}) %all-reduce.3.cloned.1.call-update) | async-done | bytes 524304 | tf_op jit(solution)/shard_map/psum | solution.py:23
  330.2 1.1 fusion.3
  331.3 0.0 copy-start.4
  331.3 0.0 copy-start.7
  331.4 0.0 copy-start.1
  331.4 0.0 copy-start.6
  331.4 8.2 %multiply_reduce_fusion = f32[32,1024]{1,0:T(8,128)S(1)} fusion(f32[128,32,1024]{2,0,1:T(8,128)} %get-tuple-element.7, f32[128,1024]{1,0:T(8,128)S(1)} %fusion.3), kind=kLoop, calls=%fused_computation | loop fusion | flops 8355840 | bytes 17432576 | tf_op jit(solution)/shard_map/reduce_sum | solution.py:25
  339.6 1.0 all_to_all.14
  340.6 0.0 all-reduce.5.cloned.1.call-update
  340.6 89.0 %all-reduce.5.cloned.1.call-done = f32[32,32,32]{1,0,2:T(8,128)} async-done(((f32[32,32,32]{1,0,2:T(8,128)}), f32[32,32,32]{1,0,2:T(8,128)}) %all-reduce.5.cloned.1.call-update) | async-done | bytes 131088 | tf_op jit(solution)/shard_map/psum | solution.py:26
  429.7 1.3 copy.31
  431.0 0.9 reshape.20
  431.9 8.6 %all-to-all-start = ((f32[32,1,1024]{2,1,0:T(1,128)}), f32[32,1,1024]{2,1,0:T(1,128)S(1)}, u32[]{:S(2)}, u32[]{:S(2)}) async-start(f32[32,1,1024]{2,1,0:T(1,128)} %reshape.20), calls=%async_computation | async-start | bytes 262144 | tf_op jit(solution)/shard_map/all_to_all | solution.py:27
  440.6 0.1 broadcast_divide_fusion
  440.7 1.0 copy.24
  441.7 8.0 %all-to-all-done = f32[32,1,1024]{2,1,0:T(1,128)S(1)} async-done(((f32[32,1,1024]{2,1,0:T(1,128)}), f32[32,1,1024]{2,1,0:T(1,128)S(1)}, u32[]{:S(2)}, u32[]{:S(2)}) %all-to-all-start) | async-done | bytes 131104 | tf_op jit(solution)/shard_map/all_to_all | solution.py:27
  449.7 0.5 broadcast.16
  450.2 0.9 reduce
  451.2 0.2 reshape.21
  451.3 0.2 copy.25
  451.5 0.0 copy-done.2
  451.5 0.7 add_divide_fusion
  (13 shorter events, 0.1 us)
Async XLA Ops:
  7.2 70.5 %all-gather.2.cloned.1.call-start = ((), (), s32[]{:S(2)}) async-start(), calls=%async_computation.1 | async-start | bytes 2162688 | tf_op jit(solution)/shard_map/all_gather | solution.py:16
  8.8 321.4 %all-reduce.3.cloned.1.call-start = ((), (), s32[]{:S(2)}) async-start(), calls=%async_computation.2 | async-start | bytes 1048576 | tf_op jit(solution)/shard_map/psum | solution.py:23
  78.9 251.3 %copy-start.5 = (f32[128]{0:T(128)S(1)}, f32[128]{0:T(128)}, u32[]{:S(2)}) copy-start(f32[128]{0:T(128)} %param.12) | copy-start | bytes 1540
  108.5 321.1 %all-reduce.5.cloned.1.call-start = ((), (), s32[]{:S(2)}) async-start(), calls=%async_computation.3 | async-start | bytes 1048576 | tf_op jit(solution)/shard_map/psum | solution.py:26
  331.3 9.3 %copy-start.4 = (f32[1024]{0:T(1024)S(1)}, f32[1024]{0:T(1024)}, u32[]{:S(2)}) copy-start(f32[1024]{0:T(1024)} %param.13) | copy-start | bytes 12292
  331.3 109.2 %copy-start.7 = (s32[32]{0:T(128)S(1)}, s32[32]{0:T(128)}, u32[]{:S(2)}) copy-start(s32[32]{0:T(128)} %param.15) | copy-start | bytes 388
  331.3 109.3 %copy-start = (f32[1024,128]{0,1:T(8,128)S(1)}, f32[1024,128]{0,1:T(8,128)}, u32[]{:S(2)}) copy-start(f32[1024,128]{0,1:T(8,128)} %all-reduce.3.cloned.1.call-done) | copy-start | bytes 1572868
  331.4 120.2 %copy-start.1 = (f32[32,1024]{1,0:T(8,128)S(1)}, f32[32,1024]{1,0:T(8,128)}, u32[]{:S(2)}) copy-start(f32[32,1024]{1,0:T(8,128)} %param.8) | copy-start | bytes 393220
  331.4 120.1 %copy-start.2 = (f32[32,1024]{1,0:T(8,128)S(1)}, f32[32,1024]{1,0:T(8,128)}, u32[]{:S(2)}) copy-start(f32[32,1024]{1,0:T(8,128)} %param.9) | copy-start | bytes 393220
  331.4 120.1 %copy-start.3 = (f32[1024]{0:T(1024)S(1)}, f32[1024]{0:T(1024)}, u32[]{:S(2)}) copy-start(f32[1024]{0:T(1024)} %param.11) | copy-start | bytes 12292
  331.4 120.1 %copy-start.6 = (s32[32]{0:T(128)S(1)}, s32[32]{0:T(128)}, u32[]{:S(2)}) copy-start(s32[32]{0:T(128)} %param.14) | copy-start | bytes 388
  431.9 17.8 %all-to-all-start = ((f32[32,1,1024]{2,1,0:T(1,128)}), f32[32,1,1024]{2,1,0:T(1,128)S(1)}, u32[]{:S(2)}, u32[]{:S(2)}) async-start(f32[32,1,1024]{2,1,0:T(1,128)} %reshape.20), calls=%async_computation | async-start | bytes 262144 | tf_op jit(solution)/shard_map/all_to_all | solution.py:27
Sparse Core Ops, SparseCore 0:
  10.4 67.1 all-gather.1
  108.6 221.4 all-reduce.2
  340.7 88.8 all-reduce.4
where the time goes:
time: 460 us; the launch traced here: 459 us
  waiting for transfers between devices  387 us (84%)
  matrix products  29.6 us (6%)
  between operations  13.9 us (3%)
  other arithmetic  13.8 us (3%)
  starting transfers between devices  8.94 us (2%)
  local copies, waits for them, and re-layouts  5.29 us (1%)
    psum x1, waiting for transfers between devices, shards(): airy = lax.psum(airy_cols.T, 'row') / airy_scale[None, :]  221 us
    psum x1, waiting for transfers between devices, shards(): summed = lax.psum(partial_force, 'inplane')  89 us
    all_gather x1, waiting for transfers between devices, shards(): gathered = lax.all_gather(rounded, 'row', axis=0, tiled=True)  68.8 us
    dot_general x1, matrix products, shards(): lax.dot_general(flat, gathered, (((1,), (1,)), ((), ())), preferred_eleme...  29.6 us
  transfers between devices with their start and end apart: 4, of which 4 were waited for; matrix products, arithmetic and copies ran while one was open for 0% of the time, Pallas kernels for 0%

commit v1 on v0

v1 whole, which is shorter than its diff:
```python
import functools

import jax
import jax.numpy as jnp
from jax import lax
from jax.experimental import pallas as pl
from jax.experimental.pallas import tpu as pltpu
from jax.sharding import Mesh, PartitionSpec as P

STRIKE_LEN = 64
AXES = ("xh", "y", "xl", "z", "c")
SIZES = (2, 4, 2, 8, 2)
INPLANE = ("xh", "y")
ROW = ("xl", "z", "c")
SAME = ("xl", "z")
N_IN = 8
N_SAME = 16
BF = jnp.bfloat16
F32 = jnp.float32


def inner_kernel(row_ref, tensor_ref, cases_ref, inner_ref, part_ref, turned):
    blocks, cases, depth = cases_ref.shape
    slabs, rows, width = tensor_ref.shape

    @pl.when(pl.program_id(0) == 0)
    def _():
        for i in range(blocks):
            turned[i * depth : (i + 1) * depth, :] = cases_ref[i].T

    start = pl.multiple_of(row_ref[0] * rows, rows)
    columns = turned[pl.ds(start, rows), :].astype(F32)
    inner = jnp.dot(
        tensor_ref[...].reshape(slabs * rows, width), turned[...], preferred_element_type=F32
    ).reshape(slabs, rows, cases)
    inner_ref[...] = inner.astype(BF)
    part_ref[...] = jnp.sum(inner * columns[None], axis=1)


def inner_products(row, coupling, cases, slabs=32):
    n_k, rows, width = coupling.shape
    blocks, n_c, depth = cases.shape
    return pl.pallas_call(
        inner_kernel,
        grid_spec=pltpu.PrefetchScalarGridSpec(
            num_scalar_prefetch=1,
            grid=(n_k // slabs,),
            in_specs=[
                pl.BlockSpec((slabs, rows, width), lambda k, r: (k, 0, 0)),
                pl.BlockSpec((blocks, n_c, depth), lambda k, r: (0, 0, 0)),
            ],
            out_specs=[
                pl.BlockSpec((slabs, rows, n_c), lambda k, r: (k, 0, 0)),
                pl.BlockSpec((slabs, n_c), lambda k, r: (k, 0)),
            ],
            scratch_shapes=[pltpu.VMEM((width, n_c), BF)],
        ),
        out_shape=[
            jax.ShapeDtypeStruct((n_k, rows, n_c), BF),
            jax.ShapeDtypeStruct((n_k, n_c), F32),
        ],
        cost_estimate=pl.CostEstimate(
            flops=2 * n_k * rows * width * n_c, bytes_accessed=12 << 20, transcendentals=0
        ),
        compiler_params=pltpu.CompilerParams(vmem_limit_bytes=40 << 20),
        name="inner_products",
    )(row, coupling, cases)


def force_kernel(airy_ref, inner_ref, out_ref, total):
    slabs, rows, n_c = inner_ref.shape
    step = pl.program_id(0)
    acc = jnp.zeros((rows, n_c), F32)
    for k in range(slabs):
        acc = acc + airy_ref[k : k + 1, :].astype(F32) * inner_ref[k].astype(F32)

    @pl.when(step == 0)
    def _():
        total[...] = acc

    @pl.when(step > 0)
    def _():
        total[...] += acc

    @pl.when(step == pl.num_programs(0) - 1)
    def _():
        for g in range(n_c // 32):
            out_ref[g] = jnp.concatenate(
                [total[8 * a : 8 * a + 8, 32 * g : 32 * g + 32] for a in range(4)], axis=1
            ).astype(out_ref.dtype)


def forces(airy, inner, slabs=32):
    n_k, rows, n_c = inner.shape
    return pl.pallas_call(
        force_kernel,
        grid=(n_k // slabs,),
        in_specs=[
            pl.BlockSpec((slabs, n_c), lambda k: (k, 0)),
            pl.BlockSpec((slabs, rows, n_c), lambda k: (k, 0, 0)),
        ],
        out_specs=pl.BlockSpec((n_c // 32, 8, 128), lambda k: (0, 0, 0)),
        out_shape=jax.ShapeDtypeStruct((n_c // 32, 8, 128), BF),
        scratch_shapes=[pltpu.VMEM((rows, n_c), F32)],
        cost_estimate=pl.CostEstimate(
            flops=2 * n_k * rows * n_c, bytes_accessed=4 << 20, transcendentals=0
        ),
        compiler_params=pltpu.CompilerParams(vmem_limit_bytes=32 << 20),
        name="forces",
    )(airy, inner)


def final_kernel(parts_ref, base_ref, damping_ref, out_ref):
    total = parts_ref[0].astype(F32)
    for i in range(1, parts_ref.shape[0]):
        total = total + parts_ref[i].astype(F32)
    spread = jnp.concatenate([total[:, :, 32 * a : 32 * a + 32] for a in range(4)], axis=1)
    force = spread.reshape(1024, 32).T
    out_ref[...] = (base_ref[...] - force) / (1.0 + damping_ref[...])


def final_step(parts, base, damping):
    return pl.pallas_call(
        final_kernel,
        out_shape=jax.ShapeDtypeStruct(base.shape, F32),
        compiler_params=pltpu.CompilerParams(vmem_limit_bytes=16 << 20),
        name="final_step",
    )(parts, base, damping)


def exchange(x, axes):
    return lax.all_to_all(x, axes, split_axis=0, concat_axis=0, tiled=True)


def spread(x, axes, n):
    return exchange(jnp.broadcast_to(x[None], (n, *x.shape)), axes)


def swap(x):
    return lax.ppermute(x, "c", [(0, 1), (1, 0)])


def shards(
    amplitudes, previous, coupling, stiffness, airy_scale, damping, strike_mode, strike_offset
):
    n_k, rows, width = coupling.shape
    core = lax.axis_index("c")
    inplane = lax.axis_index(INPLANE)
    same = lax.axis_index(SAME)
    row = lax.axis_index(ROW)
    depth = width // N_IN

    rounded = amplitudes.astype(BF)
    piece = lax.dynamic_slice_in_dim(rounded, inplane * depth, depth, 1)
    slab = spread(piece, SAME, N_SAME).reshape(N_SAME * rows, depth)
    own = spread(slab, INPLANE, N_IN)
    other = swap(own)

    index = row.astype(jnp.int32).reshape(1)
    inner_own, part_own = inner_products(index, coupling, own)
    inner_other, part_other = inner_products(index, coupling, other)

    part = part_own + swap(part_other.astype(BF)).astype(F32)
    per = n_k // N_SAME
    n_half = part.shape[1]
    shares = exchange(part.astype(BF).reshape(N_SAME, per, n_half), SAME)
    scale = lax.dynamic_slice_in_dim(airy_scale, same * per, per, 0)
    summed = jnp.sum(shares.astype(F32), axis=0) / scale[:, None]
    airy_own = spread(summed.astype(BF), SAME, N_SAME).reshape(n_k, n_half)
    airy_other = swap(airy_own)

    force_own = forces(airy_own, inner_own)
    force_other = forces(airy_other, inner_other)

    def by_core(mine, theirs):
        first = jnp.where(core == 0, mine, theirs)
        second = jnp.where(core == 0, theirs, mine)
        return jnp.stack([first, second], axis=1)

    messages = by_core(force_own, force_other).reshape(2 * N_SAME, 8, 128)
    arrived = exchange(messages, ROW)
    parts = spread(arrived, INPLANE, N_IN)

    offset = strike_offset.astype(F32)
    pulse = jnp.where(
        strike_offset <= STRIKE_LEN, 2.0 * (1.0 - jnp.cos(jnp.pi * offset / STRIKE_LEN)), 0.0
    )
    modes = jnp.arange(width, dtype=jnp.int32)
    excite = jnp.where(modes[None, :] == strike_mode[:, None], pulse[:, None], 0.0)
    base = 2.0 * amplitudes - (1.0 - damping) * previous - stiffness * amplitudes + excite
    result = final_step(parts, base, damping[None, :])

    airy = by_core(
        airy_own.T.reshape(N_SAME, rows, n_k), airy_other.T.reshape(N_SAME, rows, n_k)
    ).reshape(2 * N_SAME * rows, n_k)
    return (result, airy.astype(F32))


def solution(mesh):
    fine = Mesh(mesh.devices.reshape(SIZES), AXES)
    return jax.shard_map(
        shards,
        mesh=fine,
        in_specs=(
            P(ROW, None),
            P(ROW, None),
            P(INPLANE, ROW, None),
            P(),
            P(INPLANE),
            P(),
            P(ROW),
            P(ROW),
        ),
        out_specs=(P(ROW, None), P(None, INPLANE)),
        check_vma=False,
    )
```

time: 460 us -> 123 us (0.27)
  waiting for transfers between devices: 387 us -> 35.6 us
  blocking collectives: 0 us -> 38.9 us
  matrix products: 29.6 us -> 0 us
  Pallas kernels: 0 us -> 14.1 us
  between operations: 13.9 us -> 0.9 us
  other arithmetic: 13.8 us -> 1.03 us
  starting transfers between devices: 8.94 us -> 18.2 us
  local copies, waits for them, and re-layouts: 5.29 us -> 13.9 us
    psum x2 -> x0, waiting for transfers between devices: 310 us -> none  [the longest x1 221 us: shards(): airy = lax.psum(airy_cols.T, 'row') / airy_scale[None, :]]
    all_gather x1 -> x0, waiting for transfers between devices: 68.8 us -> none  [shards(): gathered = lax.all_gather(rounded, 'row', axis=0, tiled=True)]
    all_to_all x0 -> x2, blocking collectives: none -> 38.9 us  [exchange(): return lax.all_to_all(x, axes, split_axis=0, concat_axis=0, tiled=True)]
    dot_general x1 -> x0, matrix products: 29.6 us -> none  [shards(): lax.dot_general(flat, gathered, (((1,), (1,)), ((), ())), preferred_eleme...]
    all_to_all x1 -> x4, waiting for transfers between devices: 7.96 us -> 32.9 us  [exchange(): return lax.all_to_all(x, axes, split_axis=0, concat_axis=0, tiled=True)]
    pallas_call x0 -> x5, Pallas kernels: none -> 14.1 us  [the longest x2 10.9 us: inner_products(): pl.pallas_call(inner_kernel, grid_spec=pltpu.PrefetchScalarGridSpec(num_s...]
    all_to_all x1 -> x4, starting transfers between devices: 8.64 us -> 18 us  [exchange(): return lax.all_to_all(x, axes, split_axis=0, concat_axis=0, tiled=True)]
    reduce_sum x1, other arithmetic: 8.21 us -> 0.02 us  [shards(): summed = jnp.sum(shares.astype(F32), axis=0) / scale[:, None]]
  transfers between devices with their start and end apart: 4 -> 7, of which waited for: 4 -> 5; matrix products, arithmetic and copies ran while one was open for 0% -> 1% of each run, Pallas kernels for 0% -> 5%
where the time goes in v1:
time: 123 us
  blocking collectives  38.9 us (32%)
  waiting for transfers between devices  35.6 us (29%)
  starting transfers between devices  18.2 us (15%)
  Pallas kernels  14.1 us (11%)
  local copies, waits for them, and re-layouts  13.9 us (11%)
    all_to_all x2, blocking collectives, exchange(): return lax.all_to_all(x, axes, split_axis=0, concat_axis=0, tiled=True)  38.9 us
    all_to_all x4, waiting for transfers between devices, exchange(): return lax.all_to_all(x, axes, split_axis=0, concat_axis=0, tiled=True)  32.9 us
    all_to_all x4, starting transfers between devices, exchange(): return lax.all_to_all(x, axes, split_axis=0, concat_axis=0, tiled=True)  18 us
    pallas_call x2, Pallas kernels, inner_products(): pl.pallas_call(inner_kernel, grid_spec=pltpu.PrefetchScalarGridSpec(num_s...  10.9 us
    unnamed x24, local copies, waits for them, and re-layouts  9.69 us
    ppermute x3, waiting for transfers between devices, swap(): return lax.ppermute(x, 'c', [(0, 1), (1, 0)])  2.66 us
  transfers between devices with their start and end apart: 7, of which 5 were waited for; matrix products, arithmetic and copies ran while one was open for 1% of the time, Pallas kernels for 5%

profile of v1, /device:TPU:2, one launch (start us, length us, event | category | flops | bytes accessed | tf_op | source)
XLA Modules:
  0.0 122.6 jit_solution(11455598039291381154)
XLA Ops:
  0.6 0.7 dynamic-slice_convert_fusion
  1.4 17.3 %all_to_all.30 = bf16[16,32,128]{2,1,0:T(8,128)(2,1)S(1)} all-to-all(bf16[16,32,128]{2,1,0:T(8,128)(2,1)S(1)} %broadcast_in_dim.24), channel_id=1, replica_groups=mesh['xh'=2,'y'=4,'xl'=2,'z'=8,'c'=2] {'xl','z'}, dimensions={0} | all-to-all | bytes 262144 | tf_op jit(solution)/shard_map/all_to_all | solution.py:132
  18.7 0.1 broadcast_in_dim.30
  18.8 21.6 %all_to_all.31.cases_ref = bf16[8,512,128]{2,1,0:T(8,128)(2,1)S(1)} all-to-all(bf16[8,512,128]{2,1,0:T(8,128)(2,1)S(1)} %broadcast_in_dim.30), channel_id=1, replica_groups=mesh['xh'=2,'y'=4,'xl'=2,'z'=8,'c'=2] {'xh','y'}, dimensions={0} | all-to-all | bytes 2097152 | tf_op jit(solution)/shard_map/all_to_all | solution.py:132
  40.4 2.7 %collective-permute-done.cases_ref = bf16[8,512,128]{2,1,0:T(8,128)(2,1)S(1)} collective-permute-done((bf16[8,512,128]{2,1,0:T(8,128)(2,1)S(1)}, bf16[8,512,128]{2,1,0:T(8,128)(2,1)S(1)}, u32[]{:S(2)}, u32[]{:S(2)}) %collective-permute-start) | collective-permute-done | bytes 1048608 | tf_op jit(solution)/shard_map/ppermute | solution.py:140
  43.1 3.4 %copy-done.5 = bf16[128,32,1024]{2,1,0:T(8,128)(2,1)S(1)} copy-done((bf16[128,32,1024]{2,1,0:T(8,128)(2,1)S(1)}, bf16[128,32,1024]{2,1,0:T(8,128)(2,1)}, u32[]{:S(2)}) %copy-start.5) | copy-done | bytes 8388632
  46.5 5.5 %inner_products.3 = (bf16[128,32,512]{2,1,0:T(8,128)(2,1)S(1)}, f32[128,512]{1,0:T(8,128)S(1)}) custom-call(s32[1]{0:T(128)} %bitcast.row_ref, bf16[128,32,1024]{2,1,0:T(8,128)(2,1)S(1)} %copy-done.5, bf16[8,512,128]{2,1,0:T(8,128)(2,1)S(1)} %collective-permute-done.cases_ref), custom_call_target="tpu_custom_call" | custom-call | flops 4294967296 | bytes 12582912 | tf_op jit(solution)/shard_map/inner_products/pallas_call | solution.py:43
  52.0 1.9 %copy-done = bf16[128,32,512]{2,1,0:T(8,128)(2,1)} copy-done((bf16[128,32,512]{2,1,0:T(8,128)(2,1)}, bf16[128,32,512]{2,1,0:T(8,128)(2,1)S(1)}, u32[]{:S(2)}) %copy-start) | copy-done | bytes 4194328
  53.9 0.2 collective-permute-start.1
  54.1 5.5 %inner_products.2 = (bf16[128,32,512]{2,1,0:T(8,128)(2,1)S(1)}, f32[128,512]{1,0:T(8,128)S(1)}) custom-call(s32[1]{0:T(128)} %bitcast.row_ref, bf16[128,32,1024]{2,1,0:T(8,128)(2,1)S(1)} %copy-done.5, bf16[8,512,128]{2,1,0:T(8,128)(2,1)S(1)} %all_to_all.31.cases_ref), custom_call_target="tpu_custom_call" | custom-call | flops 4294967296 | bytes 12582912 | tf_op jit(solution)/shard_map/inner_products/pallas_call | solution.py:43
  59.6 2.0 %copy-done.2 = bf16[128,32,512]{2,1,0:T(8,128)(2,1)} copy-done((bf16[128,32,512]{2,1,0:T(8,128)(2,1)}, bf16[128,32,512]{2,1,0:T(8,128)(2,1)S(1)}, u32[]{:S(2)}) %copy-start.2) | copy-done | bytes 4194328
  61.6 0.7 fusion
  62.3 5.1 %all-to-all-start.2 = ((bf16[16,8,512]{2,1,0:T(8,128)(2,1)}), bf16[16,8,512]{2,1,0:T(8,128)(2,1)S(1)}, u32[]{:S(2)}, u32[]{:S(2)}) async-start(bf16[16,8,512]{2,1,0:T(8,128)(2,1)} %fusion), calls=%async_computation.2 | async-start | bytes 262144 | tf_op jit(solution)/shard_map/all_to_all | solution.py:132
  67.3 0.1 dynamic_slice.7
  67.4 7.9 %all-to-all-done.2 = bf16[16,8,512]{2,1,0:T(8,128)(2,1)S(1)} async-done(((bf16[16,8,512]{2,1,0:T(8,128)(2,1)}), bf16[16,8,512]{2,1,0:T(8,128)(2,1)S(1)}, u32[]{:S(2)}, u32[]{:S(2)}) %all-to-all-start.2) | async-done | bytes 131104 | tf_op jit(solution)/shard_map/all_to_all | solution.py:132
  75.4 0.7 broadcast_in_dim.31
  76.0 4.7 %all-to-all-start.3 = ((bf16[16,8,512]{2,1,0:T(8,128)(2,1)}), bf16[16,8,512]{2,1,0:T(8,128)(2,1)S(1)}, u32[]{:S(2)}, u32[]{:S(2)}) async-start(bf16[16,8,512]{2,1,0:T(8,128)(2,1)} %broadcast_in_dim.31), calls=%async_computation.3 | async-start | bytes 262144 | tf_op jit(solution)/shard_map/all_to_all | solution.py:132
  80.8 7.6 %all-to-all-done.3 = bf16[16,8,512]{2,1,0:T(8,128)(2,1)S(1)} async-done(((bf16[16,8,512]{2,1,0:T(8,128)(2,1)}), bf16[16,8,512]{2,1,0:T(8,128)(2,1)S(1)}, u32[]{:S(2)}, u32[]{:S(2)}) %all-to-all-start.3) | async-done | bytes 131104 | tf_op jit(solution)/shard_map/all_to_all | solution.py:132
  88.3 2.3 %copy-done.3 = bf16[128,32,512]{2,1,0:T(8,128)(2,1)S(1)} copy-done((bf16[128,32,512]{2,1,0:T(8,128)(2,1)S(1)}, bf16[128,32,512]{2,1,0:T(8,128)(2,1)}, u32[]{:S(2)}) %copy-start.3) | copy-done | bytes 4194328
  90.7 1.1 forces.2
  91.8 1.1 forces.3
  93.0 0.6 copy.14
  93.6 4.7 %all-to-all-start.4 = ((bf16[32,8,128]{2,1,0:T(8,128)(2,1)}), bf16[32,8,128]{2,1,0:T(8,128)(2,1)S(1)}, u32[]{:S(2)}, u32[]{:S(2)}) async-start(bf16[32,8,128]{2,1,0:T(8,128)(2,1)} %bitcast.6), calls=%async_computation.4 | async-start | bytes 131072 | tf_op jit(solution)/shard_map/all_to_all | solution.py:132
  98.4 7.7 %all-to-all-done.4 = bf16[32,8,128]{2,1,0:T(8,128)(2,1)S(1)} async-done(((bf16[32,8,128]{2,1,0:T(8,128)(2,1)}), bf16[32,8,128]{2,1,0:T(8,128)(2,1)S(1)}, u32[]{:S(2)}, u32[]{:S(2)}) %all-to-all-start.4) | async-done | bytes 65568 | tf_op jit(solution)/shard_map/all_to_all | solution.py:132
  106.1 0.9 broadcast_in_dim.54
  107.0 3.5 %all-to-all-start.5 = ((bf16[8,32,8,128]{3,2,1,0:T(8,128)(2,1)}), bf16[8,32,8,128]{3,2,1,0:T(8,128)(2,1)S(1)}, u32[]{:S(2)}, u32[]{:S(2)}) async-start(bf16[8,32,8,128]{3,2,1,0:T(8,128)(2,1)} %broadcast_in_dim.54), calls=%async_computation.5 | async-start | bytes 1048576 | tf_op jit(solution)/shard_map/all_to_all | solution.py:132
  110.6 0.1 select_add_fusion.base_ref
  110.7 0.1 copy.16
  110.8 0.1 copy.15
  111.0 0.8 copy.17
  111.8 9.8 %all-to-all-done.5.parts_ref = bf16[8,32,8,128]{3,2,1,0:T(8,128)(2,1)S(1)} async-done(((bf16[8,32,8,128]{3,2,1,0:T(8,128)(2,1)}), bf16[8,32,8,128]{3,2,1,0:T(8,128)(2,1)S(1)}, u32[]{:S(2)}, u32[]{:S(2)}) %all-to-all-start.5) | async-done | bytes 524320 | tf_op jit(solution)/shard_map/all_to_all | solution.py:132
  121.6 1.0 final_step.1
  (34 shorter events, 0.3 us)
Async XLA Ops:
  40.4 2.7 %collective-permute-start = (bf16[8,512,128]{2,1,0:T(8,128)(2,1)S(1)}, bf16[8,512,128]{2,1,0:T(8,128)(2,1)S(1)}, u32[]{:S(2)}, u32[]{:S(2)}) collective-permute-start(bf16[8,512,128]{2,1,0:T(8,128)(2,1)S(1)} %all_to_all.31.cases_ref), channel_id=1, source_target_pairs={{0,1},{1,0},{2,3},{3,2},{4,5},{5,4},{6,7},{7,6},{8,9},{9,8},{10,11... | collective-permute-start | bytes 3145736 | tf_op jit(solution)/shard_map/ppermute | solution.py:140
  43.1 3.4 %copy-start.5 = (bf16[128,32,1024]{2,1,0:T(8,128)(2,1)S(1)}, bf16[128,32,1024]{2,1,0:T(8,128)(2,1)}, u32[]{:S(2)}) copy-start(bf16[128,32,1024]{2,1,0:T(8,128)(2,1)} %tensor_ref.3) | copy-start | bytes 25165828
  51.9 1.9 %copy-start = (bf16[128,32,512]{2,1,0:T(8,128)(2,1)}, bf16[128,32,512]{2,1,0:T(8,128)(2,1)S(1)}, u32[]{:S(2)}) copy-start(bf16[128,32,512]{2,1,0:T(8,128)(2,1)S(1)} %get-tuple-element.9.inner_ref) | copy-start | bytes 12582916
  53.9 13.4 %copy-start.10 = (f32[128]{0:T(128)S(1)}, f32[128]{0:T(128)}, u32[]{:S(2)}) copy-start(f32[128]{0:T(128)} %param.12) | copy-start | bytes 1540
  53.9 34.4 %copy-start.4 = (f32[1024]{0:T(1024)S(1)}, f32[1024]{0:T(1024)}, u32[]{:S(2)}) copy-start(f32[1024]{0:T(1024)} %param.13) | copy-start | bytes 12292
  53.9 7.7 %collective-permute-start.1 = (bf16[128,512]{1,0:T(8,128)(2,1)S(1)}, bf16[128,512]{1,0:T(8,128)(2,1)S(1)}, u32[]{:S(2)}, u32[]{:S(2)}) collective-permute-start(bf16[128,512]{1,0:T(8,128)(2,1)S(1)} %convert_element_type.32), channel_id=1, source_target_pairs={{0,1},{1,0},{2,3},{3,2},{4,5},{5,4},{6,7},{7,6},{8,9},{9,8},{10,11... | collective-permute-start | bytes 393224 | tf_op jit(solution)/shard_map/ppermute | solution.py:140
  59.6 2.0 %copy-start.2 = (bf16[128,32,512]{2,1,0:T(8,128)(2,1)}, bf16[128,32,512]{2,1,0:T(8,128)(2,1)S(1)}, u32[]{:S(2)}) copy-start(bf16[128,32,512]{2,1,0:T(8,128)(2,1)S(1)} %get-tuple-element.8.inner_ref) | copy-start | bytes 12582916
  62.3 13.0 %all-to-all-start.2 = ((bf16[16,8,512]{2,1,0:T(8,128)(2,1)}), bf16[16,8,512]{2,1,0:T(8,128)(2,1)S(1)}, u32[]{:S(2)}, u32[]{:S(2)}) async-start(bf16[16,8,512]{2,1,0:T(8,128)(2,1)} %fusion), calls=%async_computation.2 | async-start | bytes 262144 | tf_op jit(solution)/shard_map/all_to_all | solution.py:132
  76.0 12.3 %all-to-all-start.3 = ((bf16[16,8,512]{2,1,0:T(8,128)(2,1)}), bf16[16,8,512]{2,1,0:T(8,128)(2,1)S(1)}, u32[]{:S(2)}, u32[]{:S(2)}) async-start(bf16[16,8,512]{2,1,0:T(8,128)(2,1)} %broadcast_in_dim.31), calls=%async_computation.3 | async-start | bytes 262144 | tf_op jit(solution)/shard_map/all_to_all | solution.py:132
  88.3 3.5 %copy-start.1 = (bf16[128,32,512]{2,1,0:T(8,128)(2,1)S(1)}, bf16[128,32,512]{2,1,0:T(8,128)(2,1)}, u32[]{:S(2)}) copy-start(bf16[128,32,512]{2,1,0:T(8,128)(2,1)} %copy-done) | copy-start | bytes 12582916
  88.3 3.5 %collective-permute-start.2 = (bf16[128,512]{1,0:T(8,128)(2,1)S(1)}, bf16[128,512]{1,0:T(8,128)(2,1)S(1)}, u32[]{:S(2)}, u32[]{:S(2)}) collective-permute-start(bf16[128,512]{1,0:T(8,128)(2,1)S(1)} %bitcast.20), channel_id=1, source_target_pairs={{0,1},{1,0},{2,3},{3,2},{4,5},{5,4},{6,7},{7,6},{8,9},{9,8},{10,11... | collective-permute-start | bytes 393224 | tf_op jit(solution)/shard_map/ppermute | solution.py:140
  88.3 2.3 %copy-start.3 = (bf16[128,32,512]{2,1,0:T(8,128)(2,1)S(1)}, bf16[128,32,512]{2,1,0:T(8,128)(2,1)}, u32[]{:S(2)}) copy-start(bf16[128,32,512]{2,1,0:T(8,128)(2,1)} %copy-done.2) | copy-start | bytes 12582916
  90.7 7.7 %copy-start.11 = (s32[32]{0:T(128)S(1)}, s32[32]{0:T(128)}, u32[]{:S(2)}) copy-start(s32[32]{0:T(128)} %param.15) | copy-start | bytes 388
  91.8 18.7 %copy-start.6 = (f32[32,1024]{1,0:T(8,128)S(1)}, f32[32,1024]{1,0:T(8,128)}, u32[]{:S(2)}) copy-start(f32[32,1024]{1,0:T(8,128)} %param.8) | copy-start | bytes 393220
  91.8 18.7 %copy-start.7 = (f32[32,1024]{1,0:T(8,128)S(1)}, f32[32,1024]{1,0:T(8,128)}, u32[]{:S(2)}) copy-start(f32[32,1024]{1,0:T(8,128)} %param.9) | copy-start | bytes 393220
  91.8 18.7 %copy-start.8 = (f32[1024]{0:T(1024)S(1)}, f32[1024]{0:T(1024)}, u32[]{:S(2)}) copy-start(f32[1024]{0:T(1024)} %param.11) | copy-start | bytes 12292
  91.8 18.7 %copy-start.9 = (s32[32]{0:T(128)S(1)}, s32[32]{0:T(128)}, u32[]{:S(2)}) copy-start(s32[32]{0:T(128)} %param.14) | copy-start | bytes 388
  93.6 12.5 %all-to-all-start.4 = ((bf16[32,8,128]{2,1,0:T(8,128)(2,1)}), bf16[32,8,128]{2,1,0:T(8,128)(2,1)S(1)}, u32[]{:S(2)}, u32[]{:S(2)}) async-start(bf16[32,8,128]{2,1,0:T(8,128)(2,1)} %bitcast.6), calls=%async_computation.4 | async-start | bytes 131072 | tf_op jit(solution)/shard_map/all_to_all | solution.py:132
  107.0 14.6 %all-to-all-start.5 = ((bf16[8,32,8,128]{3,2,1,0:T(8,128)(2,1)}), bf16[8,32,8,128]{3,2,1,0:T(8,128)(2,1)S(1)}, u32[]{:S(2)}, u32[]{:S(2)}) async-start(bf16[8,32,8,128]{3,2,1,0:T(8,128)(2,1)} %broadcast_in_dim.54), calls=%async_computation.5 | async-start | bytes 1048576 | tf_op jit(solution)/shard_map/all_to_all | solution.py:132

commit v2 on v1

--- a/solution.py
+++ b/solution.py
@@ -14,6 +14,7 @@
 ROW = ("xl", "z", "c")
 SAME = ("xl", "z")
 N_IN = 8
+N_Y = 4
 N_SAME = 16
 BF = jnp.bfloat16
 F32 = jnp.float32
@@ -37,9 +38,10 @@
     part_ref[...] = jnp.sum(inner * columns[None], axis=1)
 
 
-def inner_products(row, coupling, cases, slabs=32):
+def inner_products(row, coupling, cases, first=0, n_c=512, slabs=32):
     n_k, rows, width = coupling.shape
-    blocks, n_c, depth = cases.shape
+    blocks, _, depth = cases.shape
+    at = first // n_c
     return pl.pallas_call(
         inner_kernel,
         grid_spec=pltpu.PrefetchScalarGridSpec(
@@ -47,7 +49,7 @@
             grid=(n_k // slabs,),
             in_specs=[
                 pl.BlockSpec((slabs, rows, width), lambda k, r: (k, 0, 0)),
-                pl.BlockSpec((blocks, n_c, depth), lambda k, r: (0, 0, 0)),
+                pl.BlockSpec((blocks, n_c, depth), lambda k, r: (0, at, 0)),
             ],
             out_specs=[
                 pl.BlockSpec((slabs, rows, n_c), lambda k, r: (k, 0, 0)),
@@ -56,58 +58,63 @@
             scratch_shapes=[pltpu.VMEM((width, n_c), BF)],
         ),
         out_shape=[
-            jax.ShapeDtypeStruct((n_k, rows, n_c), BF),
+            pltpu.HBM((n_k, rows, n_c), BF),
             jax.ShapeDtypeStruct((n_k, n_c), F32),
         ],
         cost_estimate=pl.CostEstimate(
             flops=2 * n_k * rows * width * n_c, bytes_accessed=12 << 20, transcendentals=0
         ),
-        compiler_params=pltpu.CompilerParams(vmem_limit_bytes=40 << 20),
+        compiler_params=pltpu.CompilerParams(vmem_limit_bytes=20 << 20),
         name="inner_products",
-    )(row, coupling, cases)
-
-
-def force_kernel(airy_ref, inner_ref, out_ref, total):
-    slabs, rows, n_c = inner_ref.shape
+    )(row, pltpu.with_memory_space_constraint(coupling, pltpu.HBM), cases)
+
+
+def force_kernel(airy_ref, *refs):
+    *inner_refs, out_ref, total = refs
     step = pl.program_id(0)
-    acc = jnp.zeros((rows, n_c), F32)
-    for k in range(slabs):
-        acc = acc + airy_ref[k : k + 1, :].astype(F32) * inner_ref[k].astype(F32)
-
-    @pl.when(step == 0)
-    def _():
-        total[...] = acc
-
-    @pl.when(step > 0)
-    def _():
-        total[...] += acc
+    first = 0
+    for inner_ref in inner_refs:
+        slabs, rows, n_c = inner_ref.shape
+        acc = jnp.zeros((rows, n_c), F32)
+        for k in range(slabs):
+            weight = airy_ref[k : k + 1, first : first + n_c].astype(F32)
+            acc = acc + weight * inner_ref[k].astype(F32)
+
+        @pl.when(step == 0)
+        def _():
+            total[:, first : first + n_c] = acc
+
+        @pl.when(step > 0)
+        def _():
+            total[:, first : first + n_c] += acc
+
+        first += n_c
 
     @pl.when(step == pl.num_programs(0) - 1)
     def _():
-        for g in range(n_c // 32):
+        for g in range(first // 32):
             out_ref[g] = jnp.concatenate(
                 [total[8 * a : 8 * a + 8, 32 * g : 32 * g + 32] for a in range(4)], axis=1
             ).astype(out_ref.dtype)
 
 
-def forces(airy, inner, slabs=32):
-    n_k, rows, n_c = inner.shape
+def forces(airy, inners, slabs=32):
+    n_k, rows, _ = inners[0].shape
+    n_c = airy.shape[1]
     return pl.pallas_call(
         force_kernel,
         grid=(n_k // slabs,),
-        in_specs=[
-            pl.BlockSpec((slabs, n_c), lambda k: (k, 0)),
-            pl.BlockSpec((slabs, rows, n_c), lambda k: (k, 0, 0)),
-        ],
+        in_specs=[pl.BlockSpec((slabs, n_c), lambda k: (k, 0))]
+        + [pl.BlockSpec((slabs, rows, i.shape[2]), lambda k: (k, 0, 0)) for i in inners],
         out_specs=pl.BlockSpec((n_c // 32, 8, 128), lambda k: (0, 0, 0)),
         out_shape=jax.ShapeDtypeStruct((n_c // 32, 8, 128), BF),
         scratch_shapes=[pltpu.VMEM((rows, n_c), F32)],
         cost_estimate=pl.CostEstimate(
             flops=2 * n_k * rows * n_c, bytes_accessed=4 << 20, transcendentals=0
         ),
-        compiler_params=pltpu.CompilerParams(vmem_limit_bytes=32 << 20),
+        compiler_params=pltpu.CompilerParams(vmem_limit_bytes=12 << 20),
         name="forces",
-    )(airy, inner)
+    )(airy, *[pltpu.with_memory_space_constraint(i, pltpu.HBM) for i in inners])
 
 
 def final_kernel(parts_ref, base_ref, damping_ref, out_ref):
@@ -145,21 +152,24 @@
 ):
     n_k, rows, width = coupling.shape
     core = lax.axis_index("c")
-    inplane = lax.axis_index(INPLANE)
     same = lax.axis_index(SAME)
     row = lax.axis_index(ROW)
-    depth = width // N_IN
+    depth = width // N_Y
 
     rounded = amplitudes.astype(BF)
-    piece = lax.dynamic_slice_in_dim(rounded, inplane * depth, depth, 1)
+    piece = lax.dynamic_slice_in_dim(rounded, lax.axis_index("y") * depth, depth, 1)
     slab = spread(piece, SAME, N_SAME).reshape(N_SAME * rows, depth)
-    own = spread(slab, INPLANE, N_IN)
+    own = spread(slab, "y", N_Y)
     other = swap(own)
 
     index = row.astype(jnp.int32).reshape(1)
-    inner_own, part_own = inner_products(index, coupling, own)
+    inner_own_a, part_own_a = inner_products(index, coupling, own, 0, 256)
+    other, part_own_a = lax.optimization_barrier((other, part_own_a))
     inner_other, part_other = inner_products(index, coupling, other)
-
+    own, part_other = lax.optimization_barrier((own, part_other))
+    inner_own_b, part_own_b = inner_products(index, coupling, own, 256, 256)
+
+    part_own = jnp.concatenate([part_own_a, part_own_b], axis=1)
     part = part_own + swap(part_other.astype(BF)).astype(F32)
     per = n_k // N_SAME
     n_half = part.shape[1]
@@ -169,17 +179,18 @@
     airy_own = spread(summed.astype(BF), SAME, N_SAME).reshape(n_k, n_half)
     airy_other = swap(airy_own)
 
-    force_own = forces(airy_own, inner_own)
-    force_other = forces(airy_other, inner_other)
+    force_other = forces(airy_other, [inner_other])
+    force_own = forces(airy_own, [inner_own_a, inner_own_b])
 
     def by_core(mine, theirs):
         first = jnp.where(core == 0, mine, theirs)
         second = jnp.where(core == 0, theirs, mine)
         return jnp.stack([first, second], axis=1)
 
-    messages = by_core(force_own, force_other).reshape(2 * N_SAME, 8, 128)
-    arrived = exchange(messages, ROW)
-    parts = spread(arrived, INPLANE, N_IN)
+    messages = by_core(force_own, swap(force_other))
+    everywhere = jnp.broadcast_to(messages[None], (N_IN, *messages.shape))
+    arrived = exchange(everywhere.reshape(N_IN * N_SAME, 16, 128), INPLANE + SAME)
+    parts = arrived.reshape(N_IN, 2 * N_SAME, 8, 128)
 
     offset = strike_offset.astype(F32)
     pulse = jnp.where(

time: 123 us -> 128 us (1.041)
  Pallas kernels: 14.1 us -> 30.2 us
  local copies, waits for them, and re-layouts: 13.9 us -> 2.94 us
  blocking collectives: 38.9 us -> 47.2 us
  waiting for transfers between devices: 35.6 us -> 28 us
  starting transfers between devices: 18.2 us -> 16.6 us
    pallas_call x2 -> x3, Pallas kernels: 10.9 us -> 22.4 us  [inner_products(): pl.pallas_call(inner_kernel, grid_spec=pltpu.PrefetchScalarGridSpec(num_s...]
    unnamed x24 -> x14, local copies, waits for them, and re-layouts: 9.69 us -> 0.04 us
    all_to_all x2 -> x3, blocking collectives: 38.9 us -> 47.2 us  [exchange(): return lax.all_to_all(x, axes, split_axis=0, concat_axis=0, tiled=True)]
    all_to_all x4 -> x2, waiting for transfers between devices: 32.9 us -> 26.6 us  [exchange(): return lax.all_to_all(x, axes, split_axis=0, concat_axis=0, tiled=True)]
    pallas_call x2, Pallas kernels: 2.2 us -> 6.83 us  [forces(): pl.pallas_call(force_kernel, grid=(n_k // slabs,), in_specs=[pl.BlockSpec...]
    all_to_all x4 -> x2, starting transfers between devices: 18 us -> 15.8 us  [exchange(): return lax.all_to_all(x, axes, split_axis=0, concat_axis=0, tiled=True)]
    broadcast_in_dim x4 -> x3, local copies, waits for them, and re-layouts: 1.71 us -> 0.1 us  [spread(): return exchange(jnp.broadcast_to(x[None], (n, *x.shape)), axes)]
    ppermute x3 -> x4, waiting for transfers between devices: 2.66 us -> 1.35 us  [swap(): return lax.ppermute(x, 'c', [(0, 1), (1, 0)])]
  transfers between devices with their start and end apart: 7 -> 6, of which waited for: 5 -> 3; matrix products, arithmetic and copies ran while one was open for 1% -> 1% of each run, Pallas kernels for 5% -> 13%
where the time goes in v2:
time: 128 us; the launch traced here: 127 us
  blocking collectives  47.2 us (37%)
  Pallas kernels  30.2 us (24%)
  waiting for transfers between devices  28 us (22%)
  starting transfers between devices  16.6 us (13%)
  local copies, waits for them, and re-layouts  2.94 us (2%)
    all_to_all x3, blocking collectives, exchange(): return lax.all_to_all(x, axes, split_axis=0, concat_axis=0, tiled=True)  47.2 us
    all_to_all x2, waiting for transfers between devices, exchange(): return lax.all_to_all(x, axes, split_axis=0, concat_axis=0, tiled=True)  26.6 us
    pallas_call x3, Pallas kernels, inner_products(): pl.pallas_call(inner_kernel, grid_spec=pltpu.PrefetchScalarGridSpec(num_s...  22.4 us
    all_to_all x2, starting transfers between devices, exchange(): return lax.all_to_all(x, axes, split_axis=0, concat_axis=0, tiled=True)  15.8 us
    pallas_call x2, Pallas kernels, forces(): pl.pallas_call(force_kernel, grid=(n_k // slabs,), in_specs=[pl.BlockSpec...  6.83 us
  transfers between devices with their start and end apart: 6, of which 3 were waited for; matrix products, arithmetic and copies ran while one was open for 1% of the time, Pallas kernels for 13%

profile of v2, /device:TPU:2, one launch (start us, length us, event | category | flops | bytes accessed | tf_op | source)
XLA Modules:
  0.0 126.8 jit_solution(5553611341711432667)
XLA Ops:
  0.6 0.8 dynamic-slice_convert_fusion
  1.4 19.2 %all_to_all.25 = bf16[16,32,256]{2,1,0:T(8,128)(2,1)S(1)} all-to-all(bf16[16,32,256]{2,1,0:T(8,128)(2,1)S(1)} %broadcast_in_dim.24), channel_id=1, replica_groups=mesh['xh'=2,'y'=4,'xl'=2,'z'=8,'c'=2] {'xl','z'}, dimensions={0} | all-to-all | bytes 524288 | tf_op jit(solution)/shard_map/all_to_all | solution.py:139
  20.6 0.1 broadcast_in_dim.30
  20.7 16.5 %all_to_all.26.cases_ref = bf16[4,512,256]{2,1,0:T(8,128)(2,1)S(1)} all-to-all(bf16[4,512,256]{2,1,0:T(8,128)(2,1)S(1)} %broadcast_in_dim.30), channel_id=1, replica_groups=mesh['xh'=2,'y'=4,'xl'=2,'z'=8,'c'=2] {'y'}, dimensions={0} | all-to-all | bytes 2097152 | tf_op jit(solution)/shard_map/all_to_all | solution.py:139
  37.2 6.7 %inner_products.3 = (bf16[128,32,256]{2,1,0:T(8,128)(2,1)}, f32[128,256]{1,0:T(8,128)S(1)}) custom-call(s32[1]{0:T(128)} %bitcast.1.row_ref, bf16[128,32,1024]{2,1,0:T(8,128)(2,1)} %tensor_ref.5, bf16[4,512,256]{2,1,0:T(8,128)(2,1)S(1)} %all_to_all.26.cases_ref), custom_call_target="tpu_custom_call" | custom-call | flops 2147483648 | bytes 12582912 | tf_op jit(solution)/shard_map/inner_products/pallas_call | solution.py:45
  43.9 8.9 %inner_products.4 = (bf16[128,32,512]{2,1,0:T(8,128)(2,1)}, f32[128,512]{1,0:T(8,128)S(1)}) custom-call(s32[1]{0:T(128)} %bitcast.1.row_ref, bf16[128,32,1024]{2,1,0:T(8,128)(2,1)} %tensor_ref.5, bf16[4,512,256]{2,1,0:T(8,128)(2,1)S(1)} %collective-permute-done.cases_ref), custom_call_target="tpu_custom_call" | custom-call | flops 4294967296 | bytes 12582912 | tf_op jit(solution)/shard_map/inner_products/pallas_call | solution.py:45
  52.8 0.0 copy-start.5
  52.8 0.6 collective-permute-start.1
  53.4 6.8 %inner_products.5 = (bf16[128,32,256]{2,1,0:T(8,128)(2,1)}, f32[128,256]{1,0:T(8,128)S(1)}) custom-call(s32[1]{0:T(128)} %bitcast.1.row_ref, bf16[128,32,1024]{2,1,0:T(8,128)(2,1)} %tensor_ref.5, bf16[4,512,256]{2,1,0:T(8,128)(2,1)S(1)} %all_to_all.26.cases_ref), custom_call_target="tpu_custom_call" | custom-call | flops 2147483648 | bytes 12582912 | tf_op jit(solution)/shard_map/inner_products/pallas_call | solution.py:45
  60.2 0.7 fusion.1
  60.9 7.5 %all-to-all-start.2 = ((bf16[16,8,512]{2,1,0:T(8,128)(2,1)}), bf16[16,8,512]{2,1,0:T(8,128)(2,1)S(1)}, u32[]{:S(2)}, u32[]{:S(2)}) async-start(bf16[16,8,512]{2,1,0:T(8,128)(2,1)} %fusion.1), calls=%async_computation.2 | async-start | bytes 262144 | tf_op jit(solution)/shard_map/all_to_all | solution.py:139
  68.4 0.1 dynamic_slice.7
  68.5 7.7 %all-to-all-done.2 = bf16[16,8,512]{2,1,0:T(8,128)(2,1)S(1)} async-done(((bf16[16,8,512]{2,1,0:T(8,128)(2,1)}), bf16[16,8,512]{2,1,0:T(8,128)(2,1)S(1)}, u32[]{:S(2)}, u32[]{:S(2)}) %all-to-all-start.2) | async-done | bytes 131104 | tf_op jit(solution)/shard_map/all_to_all | solution.py:139
  76.3 0.1 divide_convert_fusion
  76.4 11.5 %all_to_all.27 = bf16[16,8,512]{2,1,0:T(8,128)(2,1)S(1)} all-to-all(bf16[16,8,512]{2,1,0:T(8,128)(2,1)S(1)} %broadcast_in_dim.31), channel_id=1, replica_groups=mesh['xh'=2,'y'=4,'xl'=2,'z'=8,'c'=2] {'xl','z'}, dimensions={0} | all-to-all | bytes 262144 | tf_op jit(solution)/shard_map/all_to_all | solution.py:139
  87.9 1.3 %collective-permute-done.2.airy_ref = bf16[128,512]{1,0:T(8,128)(2,1)S(1)} collective-permute-done((bf16[128,512]{1,0:T(8,128)(2,1)S(1)}, bf16[128,512]{1,0:T(8,128)(2,1)S(1)}, u32[]{:S(2)}, u32[]{:S(2)}) %collective-permute-start.2) | collective-permute-done | bytes 131104 | tf_op jit(solution)/shard_map/ppermute | solution.py:147
  89.3 3.4 %forces.3 = bf16[16,8,128]{2,1,0:T(8,128)(2,1)S(1)} custom-call(bf16[128,512]{1,0:T(8,128)(2,1)S(1)} %collective-permute-done.2.airy_ref, bf16[128,32,512]{2,1,0:T(8,128)(2,1)} %get-tuple-element.21.refs_0_), custom_call_target="tpu_custom_call" | custom-call | flops 4194304 | bytes 4194304 | tf_op jit(solution)/shard_map/forces/pallas_call | solution.py:104
  92.7 0.0 copy-start.6
  92.7 0.0 copy-start
  92.7 0.0 copy-start.1
  92.7 0.0 copy-start.2
  92.8 0.0 copy-start.3
  92.8 0.2 collective-permute-start.3
  93.0 3.4 %forces.2 = bf16[16,8,128]{2,1,0:T(8,128)(2,1)S(1)} custom-call(bf16[128,512]{1,0:T(8,128)(2,1)S(1)} %bitcast.23, bf16[128,32,256]{2,1,0:T(8,128)(2,1)} %get-tuple-element.19.refs_0_, bf16[128,32,256]{2,1,0:T(8,128)(2,1)} %get-tuple-element.20.refs_1_), custom_call_target="tpu_custom_call" | custom-call | flops 4194304 | bytes 4194304 | tf_op jit(solution)/shard_map/forces/pallas_call | solution.py:104
  96.5 0.9 broadcast_in_dim.54
  97.3 8.2 %all-to-all-start.4 = ((bf16[128,16,128]{2,1,0:T(8,128)(2,1)}), bf16[128,16,128]{2,1,0:T(8,128)(2,1)S(1)}, u32[]{:S(2)}, u32[]{:S(2)}) async-start(bf16[128,16,128]{2,1,0:T(8,128)(2,1)} %bitcast.6), calls=%async_computation.4 | async-start | bytes 1048576 | tf_op jit(solution)/shard_map/all_to_all | solution.py:139
  105.7 0.1 select_add_fusion.base_ref
  105.8 0.1 copy.17
  106.0 0.1 copy.16
  106.1 0.8 copy.18
  107.0 18.9 %all-to-all-done.4 = bf16[128,16,128]{2,1,0:T(8,128)(2,1)S(1)} async-done(((bf16[128,16,128]{2,1,0:T(8,128)(2,1)}), bf16[128,16,128]{2,1,0:T(8,128)(2,1)S(1)}, u32[]{:S(2)}, u32[]{:S(2)}) %all-to-all-start.4) | async-done | bytes 524320 | tf_op jit(solution)/shard_map/all_to_all | solution.py:139
  125.8 1.0 final_step.1
  (24 shorter events, 0.3 us)
Async XLA Ops:
  37.2 6.8 %collective-permute-start = (bf16[4,512,256]{2,1,0:T(8,128)(2,1)S(1)}, bf16[4,512,256]{2,1,0:T(8,128)(2,1)S(1)}, u32[]{:S(2)}, u32[]{:S(2)}) collective-permute-start(bf16[4,512,256]{2,1,0:T(8,128)(2,1)S(1)} %all_to_all.26.cases_ref), channel_id=1, source_target_pairs={{0,1},{1,0},{2,3},{3,2},{4,5},{5,4},{6,7},{7,6},{8,9},{9,8},{10,11... | collective-permute-start | bytes 3145736 | tf_op jit(solution)/shard_map/ppermute | solution.py:147
  52.8 15.6 %copy-start.5 = (f32[128]{0:T(128)S(1)}, f32[128]{0:T(128)}, u32[]{:S(2)}) copy-start(f32[128]{0:T(128)} %param.12) | copy-start | bytes 1540
  52.8 7.4 %collective-permute-start.1 = (bf16[128,512]{1,0:T(8,128)(2,1)S(1)}, bf16[128,512]{1,0:T(8,128)(2,1)S(1)}, u32[]{:S(2)}, u32[]{:S(2)}) collective-permute-start(bf16[128,512]{1,0:T(8,128)(2,1)S(1)} %convert_element_type.32), channel_id=1, source_target_pairs={{0,1},{1,0},{2,3},{3,2},{4,5},{5,4},{6,7},{7,6},{8,9},{9,8},{10,11... | collective-permute-start | bytes 393224 | tf_op jit(solution)/shard_map/ppermute | solution.py:147
  60.9 15.4 %all-to-all-start.2 = ((bf16[16,8,512]{2,1,0:T(8,128)(2,1)}), bf16[16,8,512]{2,1,0:T(8,128)(2,1)S(1)}, u32[]{:S(2)}, u32[]{:S(2)}) async-start(bf16[16,8,512]{2,1,0:T(8,128)(2,1)} %fusion.1), calls=%async_computation.2 | async-start | bytes 262144 | tf_op jit(solution)/shard_map/all_to_all | solution.py:139
  87.9 1.3 %collective-permute-start.2 = (bf16[128,512]{1,0:T(8,128)(2,1)S(1)}, bf16[128,512]{1,0:T(8,128)(2,1)S(1)}, u32[]{:S(2)}, u32[]{:S(2)}) collective-permute-start(bf16[128,512]{1,0:T(8,128)(2,1)S(1)} %bitcast.22), channel_id=1, source_target_pairs={{0,1},{1,0},{2,3},{3,2},{4,5},{5,4},{6,7},{7,6},{8,9},{9,8},{10,11... | collective-permute-start | bytes 393224 | tf_op jit(solution)/shard_map/ppermute | solution.py:147
  92.7 12.9 %copy-start.6 = (s32[32]{0:T(128)S(1)}, s32[32]{0:T(128)}, u32[]{:S(2)}) copy-start(s32[32]{0:T(128)} %param.15) | copy-start | bytes 388
  92.7 12.9 %copy-start = (f32[1024]{0:T(1024)S(1)}, f32[1024]{0:T(1024)}, u32[]{:S(2)}) copy-start(f32[1024]{0:T(1024)} %param.13) | copy-start | bytes 12292
  92.7 12.9 %copy-start.1 = (f32[32,1024]{1,0:T(8,128)S(1)}, f32[32,1024]{1,0:T(8,128)}, u32[]{:S(2)}) copy-start(f32[32,1024]{1,0:T(8,128)} %param.8) | copy-start | bytes 393220
  92.7 12.9 %copy-start.2 = (f32[32,1024]{1,0:T(8,128)S(1)}, f32[32,1024]{1,0:T(8,128)}, u32[]{:S(2)}) copy-start(f32[32,1024]{1,0:T(8,128)} %param.9) | copy-start | bytes 393220
  92.8 12.9 %copy-start.3 = (f32[1024]{0:T(1024)S(1)}, f32[1024]{0:T(1024)}, u32[]{:S(2)}) copy-start(f32[1024]{0:T(1024)} %param.11) | copy-start | bytes 12292
  92.8 12.9 %copy-start.4 = (s32[32]{0:T(128)S(1)}, s32[32]{0:T(128)}, u32[]{:S(2)}) copy-start(s32[32]{0:T(128)} %param.14) | copy-start | bytes 388
  92.8 3.6 %collective-permute-start.3 = (bf16[16,8,128]{2,1,0:T(8,128)(2,1)S(1)}, bf16[16,8,128]{2,1,0:T(8,128)(2,1)S(1)}, u32[]{:S(2)}, u32[]{:S(2)}) collective-permute-start(bf16[16,8,128]{2,1,0:T(8,128)(2,1)S(1)} %forces.3), channel_id=1, source_target_pairs={{0,1},{1,0},{2,3},{3,2},{4,5},{5,4},{6,7},{7,6},{8,9},{9,8},{10,11... | collective-permute-start | bytes 98312 | tf_op jit(solution)/shard_map/ppermute | solution.py:147
  97.3 28.5 %all-to-all-start.4 = ((bf16[128,16,128]{2,1,0:T(8,128)(2,1)}), bf16[128,16,128]{2,1,0:T(8,128)(2,1)S(1)}, u32[]{:S(2)}, u32[]{:S(2)}) async-start(bf16[128,16,128]{2,1,0:T(8,128)(2,1)} %bitcast.6), calls=%async_computation.4 | async-start | bytes 1048576 | tf_op jit(solution)/shard_map/all_to_all | solution.py:139

commit v3 on v2

v3 whole, which is shorter than its diff:
```python
import functools

import jax
import jax.numpy as jnp
from jax import lax
from jax.experimental import pallas as pl
from jax.experimental.pallas import tpu as pltpu
from jax.sharding import Mesh, PartitionSpec as P

STRIKE_LEN = 64
AXES = ("xh", "y", "xl", "z", "c")
SIZES = (2, 4, 2, 8, 2)
INPLANE = ("xh", "y")
ROW = ("xl", "z", "c")
SAME = ("xl", "z")
N_IN = 8
N_Y = 4
N_SAME = 16
WIDE = 128
BF = jnp.bfloat16
F32 = jnp.float32


def inner_kernel(counts, row_ref, tensor_ref, *refs):
    n_in, blocks = sum(counts), len(counts)
    case_refs = refs[:n_in]
    inner_refs = refs[n_in : n_in + blocks]
    part_refs = refs[n_in + blocks : n_in + 2 * blocks]
    turned = refs[-1]
    slabs, rows, width = tensor_ref.shape

    @pl.when(pl.program_id(0) == 0)
    def _():
        at = 0
        for b, count in enumerate(counts):
            pieces = [case_refs[at + i][...] for i in range(count)]
            whole = pieces[0] if count == 1 else jnp.concatenate(pieces, axis=0)
            turned[:, b * WIDE : (b + 1) * WIDE] = whole.T
            at += count

    start = pl.multiple_of(row_ref[0] * rows, rows)
    columns = turned[pl.ds(start, rows), :].astype(F32)
    inner = jnp.dot(
        tensor_ref[...].reshape(slabs * rows, width), turned[...], preferred_element_type=F32
    ).reshape(slabs, rows, blocks * WIDE)
    for b in range(blocks):
        span = slice(b * WIDE, (b + 1) * WIDE)
        piece = inner[:, :, span]
        inner_refs[b][...] = piece.astype(BF)
        part = jnp.sum(piece * columns[None, :, span], axis=1)
        part_refs[b][...] = part.astype(part_refs[b].dtype)


def inner_products(row, coupling, groups, part_types, slabs=32):
    n_k, rows, width = coupling.shape
    counts = tuple(len(g) for g in groups)
    cases = [c for g in groups for c in g]
    blocks = len(groups)
    out = pl.pallas_call(
        functools.partial(inner_kernel, counts),
        grid_spec=pltpu.PrefetchScalarGridSpec(
            num_scalar_prefetch=1,
            grid=(n_k // slabs,),
            in_specs=[pl.BlockSpec((slabs, rows, width), lambda k, r: (k, 0, 0))]
            + [pl.BlockSpec(c.shape, lambda k, r: (0, 0)) for c in cases],
            out_specs=[pl.BlockSpec((slabs, rows, WIDE), lambda k, r: (k, 0, 0))] * blocks
            + [pl.BlockSpec((slabs, WIDE), lambda k, r: (k, 0))] * blocks,
            scratch_shapes=[pltpu.VMEM((width, blocks * WIDE), BF)],
        ),
        out_shape=[pltpu.HBM((n_k, rows, WIDE), BF)] * blocks
        + [jax.ShapeDtypeStruct((n_k, WIDE), t) for t in part_types],
        cost_estimate=pl.CostEstimate(
            flops=2 * n_k * rows * width * blocks * WIDE, bytes_accessed=10 << 20, transcendentals=0
        ),
        compiler_params=pltpu.CompilerParams(vmem_limit_bytes=24 << 20),
        name="inner_products",
    )(row, coupling, *cases)
    return out[:blocks], out[blocks:]


def combine_kernel(*refs):
    *sources, out_ref = refs
    half = len(sources) // 2
    for b in range(half):
        total = sources[b][...] + sources[half + b][...].astype(F32)
        out_ref[:, b * WIDE : (b + 1) * WIDE] = total.astype(BF)


def combine(mine, received):
    n_k = mine[0].shape[0]
    return pl.pallas_call(
        combine_kernel,
        out_shape=jax.ShapeDtypeStruct((n_k, WIDE * len(mine)), BF),
        compiler_params=pltpu.CompilerParams(vmem_limit_bytes=4 << 20),
        name="combine",
    )(*mine, *received)


def force_kernel(pair, place_ref, airy_ref, *refs):
    if pair:
        *inner_refs, mine_ref, out_ref, total = refs
    else:
        *inner_refs, out_ref, total = refs
    step = pl.program_id(0)
    slabs, rows, _ = inner_refs[0].shape
    y, core = place_ref[0], place_ref[1]

    for d, inner_ref in enumerate(inner_refs):
        acc = jnp.zeros((rows, WIDE), F32)
        for k in range(slabs):
            weight = airy_ref[k : k + 1, d * WIDE : (d + 1) * WIDE].astype(F32)
            acc = acc + weight * inner_ref[k].astype(F32)
        at = pl.ds(pl.multiple_of(((y + d) % N_Y) * rows, rows), rows)

        @pl.when(step == 0)
        def _():
            total[at, :] = acc

        @pl.when(step > 0)
        def _():
            total[at, :] += acc

    @pl.when(step == pl.num_programs(0) - 1)
    def _():
        turned = total[...].T.astype(BF).reshape(N_SAME, 8, WIDE)
        if pair:
            out_ref[:, core] = mine_ref[...]
            out_ref[:, 1 - core] = turned
        else:
            out_ref[...] = turned


def forces(place, airy, inners, mine=None, slabs=32):
    n_k, rows, _ = inners[0].shape
    pair = mine is not None
    shape = (N_SAME, 2, 8, WIDE) if pair else (N_SAME, 8, WIDE)
    extra = [mine] if pair else []
    return pl.pallas_call(
        functools.partial(force_kernel, pair),
        grid_spec=pltpu.PrefetchScalarGridSpec(
            num_scalar_prefetch=1,
            grid=(n_k // slabs,),
            in_specs=[pl.BlockSpec((slabs, airy.shape[1]), lambda k, s: (k, 0))]
            + [pl.BlockSpec((slabs, rows, WIDE), lambda k, s: (k, 0, 0))] * len(inners)
            + [pl.BlockSpec(m.shape, lambda k, s: (0, 0, 0)) for m in extra],
            out_specs=pl.BlockSpec(shape, lambda k, s: (0,) * len(shape)),
            scratch_shapes=[pltpu.VMEM((N_Y * rows, WIDE), F32)],
        ),
        out_shape=jax.ShapeDtypeStruct(shape, BF),
        cost_estimate=pl.CostEstimate(
            flops=2 * n_k * rows * airy.shape[1], bytes_accessed=4 << 20, transcendentals=0
        ),
        compiler_params=pltpu.CompilerParams(vmem_limit_bytes=12 << 20),
        name="forces",
    )(place, airy, *[pltpu.with_memory_space_constraint(i, pltpu.HBM) for i in inners], *extra)


def airy_kernel(place_ref, mine_ref, theirs_ref, out_ref):
    y, core = place_ref[0], place_ref[1]
    for source, at in ((mine_ref, core), (theirs_ref, 1 - core)):
        for d in range(N_Y):
            piece = source[:, d * WIDE : (d + 1) * WIDE].astype(F32).T
            out_ref[:, at, (y + d) % N_Y] = piece.reshape(N_SAME, 8, WIDE)


def airy_output(place, mine, theirs):
    full = pl.BlockSpec(mine.shape, lambda i, s: (0, 0))
    shape = (N_SAME, 2, N_Y, 8, WIDE)
    return pl.pallas_call(
        airy_kernel,
        grid_spec=pltpu.PrefetchScalarGridSpec(
            num_scalar_prefetch=1,
            grid=(1,),
            in_specs=[full, full],
            out_specs=pl.BlockSpec(shape, lambda i, s: (0,) * 5),
        ),
        out_shape=jax.ShapeDtypeStruct(shape, F32),
        cost_estimate=pl.CostEstimate(flops=1 << 20, bytes_accessed=1 << 20, transcendentals=0),
        compiler_params=pltpu.CompilerParams(vmem_limit_bytes=8 << 20),
        name="airy_output",
    )(place, mine, theirs)


def final_kernel(parts_ref, base_ref, damping_ref, out_ref):
    total = parts_ref[0].astype(F32)
    for i in range(1, parts_ref.shape[0]):
        total = total + parts_ref[i].astype(F32)
    scale = 1.0 + damping_ref[...]
    for a in range(4):
        rows = slice(8 * a, 8 * a + 8)
        force = jnp.concatenate(
            [total[r][:, 32 * a : 32 * a + 32] for r in range(2 * N_SAME)], axis=1
        )
        out_ref[rows, :] = (base_ref[rows, :] - force) / scale


def final_step(parts, base, damping):
    return pl.pallas_call(
        final_kernel,
        out_shape=jax.ShapeDtypeStruct(base.shape, F32),
        compiler_params=pltpu.CompilerParams(vmem_limit_bytes=16 << 20),
        name="final_step",
    )(parts, base, damping)


def exchange(x, axes):
    return lax.all_to_all(x, axes, split_axis=0, concat_axis=0, tiled=True)


def spread(x, axes, n):
    return exchange(jnp.broadcast_to(x[None], (n, *x.shape)), axes)


def swap(x):
    return lax.ppermute(x, "c", [(0, 1), (1, 0)])


def shift(x, by):
    return lax.ppermute(x, "y", [(i, (i + by) % N_Y) for i in range(N_Y)])


def after(x):
    return lax.optimization_barrier(x)


def shards(
    amplitudes, previous, coupling, stiffness, airy_scale, damping, strike_mode, strike_offset
):
    n_k, rows, width = coupling.shape
    y = lax.axis_index("y").astype(jnp.int32)
    core = lax.axis_index("c").astype(jnp.int32)
    same = lax.axis_index(SAME)
    row = lax.axis_index(ROW).astype(jnp.int32).reshape(1)
    place = jnp.stack([y, core])
    few = rows // N_Y

    piece = lax.dynamic_slice_in_dim(amplitudes, y * few, few, 0).astype(BF)
    b0 = spread(piece, SAME, N_SAME).reshape(WIDE, width)
    b3, b1 = shift(b0, 1), shift(b0, -1)
    o0 = swap(b0)
    (i0, j0), (p0, q0) = inner_products(row, coupling, [[b0], [o0]], [F32, BF])

    b1, b3, p0, q0 = after((b1, b3, p0, q0))
    b2a, b2b = shift(b3[: WIDE // 2], 1), shift(b1[WIDE // 2 :], -1)
    o1, o3 = swap(b1), swap(b3)
    (i1, i3), (p1, p3) = inner_products(row, coupling, [[b1], [b3]], [F32, F32])

    o1, o3, b2a, b2b, p1 = after((o1, o3, b2a, b2b, p1))
    o2a, o2b = swap(b2a), swap(b2b)
    (j1, j3), (q1, q3) = inner_products(row, coupling, [[o1], [o3]], [BF, BF])

    b2a, b2b, o2a, o2b, q1 = after((b2a, b2b, o2a, o2b, q1))
    (i2, j2), (p2, q2) = inner_products(row, coupling, [[b2a, b2b], [o2a, o2b]], [F32, BF])

    received = [swap(q) for q in (q0, q1, q2, q3)]
    part = combine([p0, p1, p2, p3], received)
    per = n_k // N_SAME
    n_half = part.shape[1]
    shares = exchange(part.reshape(N_SAME, per, n_half), SAME)
    scale = lax.dynamic_slice_in_dim(airy_scale, same * per, per, 0)
    summed = jnp.sum(shares.astype(F32), axis=0) / scale[:, None]
    airy_own = spread(summed.astype(BF), SAME, N_SAME).reshape(n_k, n_half)
    airy_other = swap(airy_own)

    force_own = forces(place, airy_own, [i0, i1, i2, i3])
    messages = forces(place, airy_other, [j0, j1, j2, j3], force_own)
    arrived = exchange(messages.reshape(2 * N_SAME, 8, WIDE), ROW)
    parts = spread(arrived, INPLANE, N_IN)
    airy = airy_output(place, airy_own, airy_other).reshape(2 * N_SAME * rows, n_k)

    offset = strike_offset.astype(F32)
    pulse = jnp.where(
        strike_offset <= STRIKE_LEN, 2.0 * (1.0 - jnp.cos(jnp.pi * offset / STRIKE_LEN)), 0.0
    )
    modes = jnp.arange(width, dtype=jnp.int32)
    excite = jnp.where(modes[None, :] == strike_mode[:, None], pulse[:, None], 0.0)
    base = 2.0 * amplitudes - (1.0 - damping) * previous - stiffness * amplitudes + excite
    result = final_step(parts, base, damping[None, :])
    return (result, airy)


def solution(mesh):
    fine = Mesh(mesh.devices.reshape(SIZES), AXES)
    return jax.shard_map(
        shards,
        mesh=fine,
        in_specs=(
            P(ROW, None),
            P(ROW, None),
            P(INPLANE, ROW, None),
            P(),
            P(INPLANE),
            P(),
            P(ROW),
            P(ROW),
        ),
        out_specs=(P(ROW, None), P(None, INPLANE)),
        check_vma=False,
    )
```

time: 128 us -> 117 us (0.914)
  blocking collectives: 47.2 us -> 30.9 us
  starting transfers between devices: 16.6 us -> 23.3 us
  Pallas kernels: 30.2 us -> 27.5 us
  local copies, waits for them, and re-layouts: 2.94 us -> 5.19 us
    all_to_all x3 -> x2, blocking collectives: 47.2 us -> 30.9 us  [exchange(): return lax.all_to_all(x, axes, split_axis=0, concat_axis=0, tiled=True)]
    ppermute x0 -> x4, starting transfers between devices: none -> 6.32 us  [shift(): return lax.ppermute(x, 'y', [(i, (i + by) % N_Y) for i in range(N_Y)])]
    unnamed x14 -> x16, local copies, waits for them, and re-layouts: 0.04 us -> 3.42 us
    pallas_call x5 -> x8, Pallas kernels: 29.2 us -> 26.6 us  [the longest x4 15.9 us: inner_products(): pl.pallas_call(functools.partial(inner_kernel, counts), grid_spec=pltpu.P...]
    ppermute x0 -> x4, waiting for transfers between devices: none -> 2.29 us  [shift(): return lax.ppermute(x, 'y', [(i, (i + by) % N_Y) for i in range(N_Y)])]
    all_to_all x2 -> x3, waiting for transfers between devices: 26.6 us -> 25 us  [exchange(): return lax.all_to_all(x, axes, split_axis=0, concat_axis=0, tiled=True)]
    ppermute x4 -> x10, starting transfers between devices: 0.83 us -> 2.21 us  [swap(): return lax.ppermute(x, 'c', [(0, 1), (1, 0)])]
    all_to_all x2 -> x3, starting transfers between devices: 15.8 us -> 14.7 us  [exchange(): return lax.all_to_all(x, axes, split_axis=0, concat_axis=0, tiled=True)]
  transfers between devices with their start and end apart: 6 -> 17, of which waited for: 3 -> 5; matrix products, arithmetic and copies ran while one was open for 1% -> 0% of each run, Pallas kernels for 13% -> 18%
where the time goes in v3:
time: 117 us; the launch traced here: 116 us
  blocking collectives  30.9 us (26%)
  waiting for transfers between devices  28.2 us (24%)
  Pallas kernels  27.5 us (24%)
  starting transfers between devices  23.3 us (20%)
  local copies, waits for them, and re-layouts  5.19 us (4%)
    all_to_all x2, blocking collectives, exchange(): return lax.all_to_all(x, axes, split_axis=0, concat_axis=0, tiled=True)  30.9 us
    all_to_all x3, waiting for transfers between devices, exchange(): return lax.all_to_all(x, axes, split_axis=0, concat_axis=0, tiled=True)  25 us
    pallas_call x4, Pallas kernels, inner_products(): pl.pallas_call(functools.partial(inner_kernel, counts), grid_spec=pltpu.P...  15.9 us
    all_to_all x3, starting transfers between devices, exchange(): return lax.all_to_all(x, axes, split_axis=0, concat_axis=0, tiled=True)  14.7 us
    pallas_call x2, Pallas kernels, forces(): pl.pallas_call(functools.partial(force_kernel, pair), grid_spec=pltpu.Pre...  8.54 us
    ppermute x4, starting transfers between devices, shift(): return lax.ppermute(x, 'y', [(i, (i + by) % N_Y) for i in range(N_Y)])  6.32 us
    unnamed x16, local copies, waits for them, and re-layouts  3.42 us
  transfers between devices with their start and end apart: 17, of which 5 were waited for; matrix products, arithmetic and copies ran while one was open for 0% of the time, Pallas kernels for 18%

profile of v3, /device:TPU:2, one launch (start us, length us, event | category | flops | bytes accessed | tf_op | source)
XLA Modules:
  0.0 116.2 jit_solution(17503976119425950416)
XLA Ops:
  0.6 0.8 dynamic-slice_convert_fusion
  1.4 19.2 %all_to_all.25 = bf16[16,8,1024]{2,1,0:T(8,128)(2,1)S(1)} all-to-all(bf16[16,8,1024]{2,1,0:T(8,128)(2,1)S(1)} %broadcast_in_dim.20), channel_id=1, replica_groups=mesh['xh'=2,'y'=4,'xl'=2,'z'=8,'c'=2] {'xl','z'}, dimensions={0} | all-to-all | bytes 524288 | tf_op jit(solution)/shard_map/all_to_all | solution.py:207
  20.6 3.0 %collective-permute-start = (bf16[128,1024]{1,0:T(8,128)(2,1)S(1)}, bf16[128,1024]{1,0:T(8,128)(2,1)S(1)}, u32[]{:S(2)}, u32[]{:S(2)}) collective-permute-start(bf16[128,1024]{1,0:T(8,128)(2,1)S(1)} %bitcast.13), channel_id=1, source_target_pairs={{0,96},{32,0},{64,32},{96,64},{1,97},{33,1},{65,33},{97,65},{2,98}... | collective-permute-start | bytes 786440 | tf_op jit(solution)/shard_map/ppermute | solution.py:219
  23.6 3.4 %copy-done = bf16[128,32,1024]{2,1,0:T(8,128)(2,1)S(1)} copy-done((bf16[128,32,1024]{2,1,0:T(8,128)(2,1)S(1)}, bf16[128,32,1024]{2,1,0:T(8,128)(2,1)}, u32[]{:S(2)}) %copy-start) | copy-done | bytes 8388632
  27.0 4.0 %inner_products.4 = (bf16[128,32,128]{2,1,0:T(8,128)(2,1)}, bf16[128,32,128]{2,1,0:T(8,128)(2,1)}, f32[128,128]{1,0:T(8,128)S(1)}, bf16[128,128]{1,0:T(8,128)(2,1)S(1)}) custom-call(s32[1]{0:T(128)} %bitcast.3.row_ref, bf16[128,32,1024]{2,1,0:T(8,128)(2,1)S(1)} %copy-done, bf16[128,1024]{1,0:T(8,128)(2,1)S(1)} %bitcast.15, ...), custom_call_target="tpu_custom_call" | custom-call | flops 2147483648 | bytes 10485760 | tf_op jit(solution)/shard_map/inner_products/pallas_call | solution.py:59
  31.0 2.3 %collective-permute-done.1.refs_1_ = bf16[128,1024]{1,0:T(8,128)(2,1)S(1)} collective-permute-done((bf16[128,1024]{1,0:T(8,128)(2,1)S(1)}, bf16[128,1024]{1,0:T(8,128)(2,1)S(1)}, u32[]{:S(2)}, u32[]{:S(2)}) %collective-permute-start.1) | collective-permute-done | bytes 262176 | tf_op jit(solution)/shard_map/ppermute | solution.py:219
  33.3 0.5 collective-permute-start.4
  33.8 0.1 collective-permute-start.5
  33.9 3.2 %collective-permute-start.6 = (bf16[64,1024]{1,0:T(8,128)(2,1)S(1)}, bf16[64,1024]{1,0:T(8,128)(2,1)S(1)}, u32[]{:S(2)}, u32[]{:S(2)}) collective-permute-start(bf16[64,1024]{1,0:T(8,128)(2,1)S(1)} %slice.7), channel_id=1, source_target_pairs={{0,96},{32,0},{64,32},{96,64},{1,97},{33,1},{65,33},{97,65},{2,98}... | collective-permute-start | bytes 393224 | tf_op jit(solution)/shard_map/ppermute | solution.py:219
  37.1 4.0 %inner_products.5 = (bf16[128,32,128]{2,1,0:T(8,128)(2,1)}, bf16[128,32,128]{2,1,0:T(8,128)(2,1)}, f32[128,128]{1,0:T(8,128)S(1)}, f32[128,128]{1,0:T(8,128)S(1)}) custom-call(s32[1]{0:T(128)} %bitcast.3.row_ref, bf16[128,32,1024]{2,1,0:T(8,128)(2,1)S(1)} %copy-done, bf16[128,1024]{1,0:T(8,128)(2,1)S(1)} %collective-permute-done.refs_0_, ...), custom_call_target="tpu_custom_call" | custom-call | flops 2147483648 | bytes 10485760 | tf_op jit(solution)/shard_map/inner_products/pallas_call | solution.py:59
  41.2 0.6 collective-permute-start.7
  41.8 0.1 collective-permute-start.8
  41.9 4.0 %inner_products.6 = (bf16[128,32,128]{2,1,0:T(8,128)(2,1)}, bf16[128,32,128]{2,1,0:T(8,128)(2,1)}, bf16[128,128]{1,0:T(8,128)(2,1)S(1)}, bf16[128,128]{1,0:T(8,128)(2,1)S(1)}) custom-call(s32[1]{0:T(128)} %bitcast.3.row_ref, bf16[128,32,1024]{2,1,0:T(8,128)(2,1)S(1)} %copy-done, bf16[128,1024]{1,0:T(8,128)(2,1)S(1)} %collective-permute-done.3.refs_0_, ...), custom_call_target="tpu_custom_call" | custom-call | flops 2147483648 | bytes 10485760 | tf_op jit(solution)/shard_map/inner_products/pallas_call | solution.py:59
  45.8 0.4 collective-permute-start.12
  46.3 0.2 collective-permute-start.10
  46.5 4.0 %inner_products.7 = (bf16[128,32,128]{2,1,0:T(8,128)(2,1)}, bf16[128,32,128]{2,1,0:T(8,128)(2,1)}, f32[128,128]{1,0:T(8,128)S(1)}, bf16[128,128]{1,0:T(8,128)(2,1)S(1)}) custom-call(s32[1]{0:T(128)} %bitcast.3.row_ref, bf16[128,32,1024]{2,1,0:T(8,128)(2,1)S(1)} %copy-done, bf16[64,1024]{1,0:T(8,128)(2,1)S(1)} %collective-permute-done.5.refs_0_, ...), custom_call_target="tpu_custom_call" | custom-call | flops 2147483648 | bytes 10485760 | tf_op jit(solution)/shard_map/inner_products/pallas_call | solution.py:59
  50.4 0.4 collective-permute-start.11
  50.9 0.8 collective-permute-done.11.refs_6_
  51.7 0.7 combine.1
  52.4 5.2 %all-to-all-start.1 = ((bf16[16,8,512]{2,1,0:T(8,128)(2,1)}), bf16[16,8,512]{2,1,0:T(8,128)(2,1)S(1)}, u32[]{:S(2)}, u32[]{:S(2)}) async-start(bf16[16,8,512]{2,1,0:T(8,128)(2,1)} %bitcast.4), calls=%async_computation.1 | async-start | bytes 262144 | tf_op jit(solution)/shard_map/all_to_all | solution.py:207
  57.7 7.9 %all-to-all-done.1 = bf16[16,8,512]{2,1,0:T(8,128)(2,1)S(1)} async-done(((bf16[16,8,512]{2,1,0:T(8,128)(2,1)}), bf16[16,8,512]{2,1,0:T(8,128)(2,1)S(1)}, u32[]{:S(2)}, u32[]{:S(2)}) %all-to-all-start.1) | async-done | bytes 131104 | tf_op jit(solution)/shard_map/all_to_all | solution.py:207
  65.7 11.7 %all_to_all.26 = bf16[16,8,512]{2,1,0:T(8,128)(2,1)S(1)} all-to-all(bf16[16,8,512]{2,1,0:T(8,128)(2,1)S(1)} %broadcast_in_dim.21), channel_id=1, replica_groups=mesh['xh'=2,'y'=4,'xl'=2,'z'=8,'c'=2] {'xl','z'}, dimensions={0} | all-to-all | bytes 262144 | tf_op jit(solution)/shard_map/all_to_all | solution.py:207
  77.5 4.0 %forces.2.refs_4_ = bf16[16,8,128]{2,1,0:T(8,128)(2,1)S(1)} custom-call(s32[2]{0:T(128)S(1)} %pad_add_fusion.place_ref, bf16[128,512]{1,0:T(8,128)(2,1)S(1)} %bitcast.10, bf16[128,32,128]{2,1,0:T(8,128)(2,1)} %get-tuple-element.58.refs_0_, bf16[128,32,128]{2,1,0:T(8,128)(2,1)} %get-tuple-element.59.refs_1_, bf16[128,32,128]{2,1,0:T(8,128)(2,1)} %get-tuple-element.60.refs_2_, ...), custom_call_target="tpu_custom_call" | custom-call | flops 4194304 | bytes 4194304 | tf_op jit(solution)/shard_map/forces/pallas_call | solution.py:138
  81.5 4.6 %forces.3 = bf16[16,2,8,128]{3,2,1,0:T(8,128)(2,1)} custom-call(s32[2]{0:T(128)S(1)} %pad_add_fusion.place_ref, bf16[128,512]{1,0:T(8,128)(2,1)S(1)} %collective-permute-done.13.airy_ref.theirs_ref, bf16[128,32,128]{2,1,0:T(8,128)(2,1)} %get-tuple-element.54.refs_0_, bf16[128,32,128]{2,1,0:T(8,128)(2,1)} %get-tuple-element.55.refs_1_, ...), custom_call_target="tpu_custom_call" | custom-call | flops 4194304 | bytes 4194304 | tf_op jit(solution)/shard_map/forces/pallas_call | solution.py:138
  86.0 4.7 %all-to-all-start.3 = ((bf16[32,8,128]{2,1,0:T(8,128)(2,1)}), bf16[32,8,128]{2,1,0:T(8,128)(2,1)S(1)}, u32[]{:S(2)}, u32[]{:S(2)}) async-start(bf16[32,8,128]{2,1,0:T(8,128)(2,1)} %bitcast.6), calls=%async_computation.3 | async-start | bytes 131072 | tf_op jit(solution)/shard_map/all_to_all | solution.py:207
  90.8 7.7 %all-to-all-done.3 = bf16[32,8,128]{2,1,0:T(8,128)(2,1)S(1)} async-done(((bf16[32,8,128]{2,1,0:T(8,128)(2,1)}), bf16[32,8,128]{2,1,0:T(8,128)(2,1)S(1)}, u32[]{:S(2)}, u32[]{:S(2)}) %all-to-all-start.3) | async-done | bytes 65568 | tf_op jit(solution)/shard_map/all_to_all | solution.py:207
  98.6 0.9 broadcast_in_dim.26
  99.4 4.8 %all-to-all-start.4 = ((bf16[8,32,8,128]{3,2,1,0:T(8,128)(2,1)}), bf16[8,32,8,128]{3,2,1,0:T(8,128)(2,1)S(1)}, u32[]{:S(2)}, u32[]{:S(2)}) async-start(bf16[8,32,8,128]{3,2,1,0:T(8,128)(2,1)} %broadcast_in_dim.26), calls=%async_computation.4 | async-start | bytes 1048576 | tf_op jit(solution)/shard_map/all_to_all | solution.py:207
  104.3 0.1 select_add_fusion.base_ref
  104.4 1.5 %airy_output.1 = f32[16,2,4,8,128]{4,3,2,1,0:T(8,128)} custom-call(s32[2]{0:T(128)S(1)} %pad_add_fusion.place_ref, bf16[128,512]{1,0:T(8,128)(2,1)S(1)} %bitcast.11, bf16[128,512]{1,0:T(8,128)(2,1)S(1)} %collective-permute-done.13.airy_ref.theirs_ref), custom_call_target="tpu_custom_call" | custom-call | flops 1048576 | bytes 1048576 | tf_op jit(solution)/shard_map/airy_output/pallas_call | solution.py:169
  105.9 9.4 %all-to-all-done.4.parts_ref = bf16[8,32,8,128]{3,2,1,0:T(8,128)(2,1)S(1)} async-done(((bf16[8,32,8,128]{3,2,1,0:T(8,128)(2,1)}), bf16[8,32,8,128]{3,2,1,0:T(8,128)(2,1)S(1)}, u32[]{:S(2)}, u32[]{:S(2)}) %all-to-all-start.4) | async-done | bytes 524320 | tf_op jit(solution)/shard_map/all_to_all | solution.py:207
  115.3 0.9 final_step.1
  (42 shorter events, 0.4 us)
Async XLA Ops:
  20.6 3.0 %collective-permute-start.2 = (bf16[128,1024]{1,0:T(8,128)(2,1)S(1)}, bf16[128,1024]{1,0:T(8,128)(2,1)S(1)}, u32[]{:S(2)}, u32[]{:S(2)}) collective-permute-start(bf16[128,1024]{1,0:T(8,128)(2,1)S(1)} %bitcast.12), channel_id=1, source_target_pairs={{0,1},{1,0},{2,3},{3,2},{4,5},{5,4},{6,7},{7,6},{8,9},{9,8},{10,11... | collective-permute-start | bytes 786440 | tf_op jit(solution)/shard_map/ppermute | solution.py:215
  20.6 10.4 %collective-permute-start = (bf16[128,1024]{1,0:T(8,128)(2,1)S(1)}, bf16[128,1024]{1,0:T(8,128)(2,1)S(1)}, u32[]{:S(2)}, u32[]{:S(2)}) collective-permute-start(bf16[128,1024]{1,0:T(8,128)(2,1)S(1)} %bitcast.13), channel_id=1, source_target_pairs={{0,96},{32,0},{64,32},{96,64},{1,97},{33,1},{65,33},{97,65},{2,98}... | collective-permute-start | bytes 786440 | tf_op jit(solution)/shard_map/ppermute | solution.py:219
  23.6 9.6 %collective-permute-start.1 = (bf16[128,1024]{1,0:T(8,128)(2,1)S(1)}, bf16[128,1024]{1,0:T(8,128)(2,1)S(1)}, u32[]{:S(2)}, u32[]{:S(2)}) collective-permute-start(bf16[128,1024]{1,0:T(8,128)(2,1)S(1)} %bitcast.14), channel_id=1, source_target_pairs={{0,32},{32,64},{64,96},{96,0},{1,33},{33,65},{65,97},{97,1},{2,34}... | collective-permute-start | bytes 786440 | tf_op jit(solution)/shard_map/ppermute | solution.py:219
  23.6 3.4 %copy-start = (bf16[128,32,1024]{2,1,0:T(8,128)(2,1)S(1)}, bf16[128,32,1024]{2,1,0:T(8,128)(2,1)}, u32[]{:S(2)}) copy-start(bf16[128,32,1024]{2,1,0:T(8,128)(2,1)} %tensor_ref.7) | copy-start | bytes 25165828
  33.3 7.9 %collective-permute-start.3 = (bf16[128,1024]{1,0:T(8,128)(2,1)S(1)}, bf16[128,1024]{1,0:T(8,128)(2,1)S(1)}, u32[]{:S(2)}, u32[]{:S(2)}) collective-permute-start(bf16[128,1024]{1,0:T(8,128)(2,1)S(1)} %collective-permute-done.refs_0_), channel_id=1, source_target_pairs={{0,1},{1,0},{2,3},{3,2},{4,5},{5,4},{6,7},{7,6},{8,9},{9,8},{10,11... | collective-permute-start | bytes 786440 | tf_op jit(solution)/shard_map/ppermute | solution.py:215
  33.3 7.9 %collective-permute-start.4 = (bf16[128,1024]{1,0:T(8,128)(2,1)S(1)}, bf16[128,1024]{1,0:T(8,128)(2,1)S(1)}, u32[]{:S(2)}, u32[]{:S(2)}) collective-permute-start(bf16[128,1024]{1,0:T(8,128)(2,1)S(1)} %collective-permute-done.1.refs_1_), channel_id=1, source_target_pairs={{0,1},{1,0},{2,3},{3,2},{4,5},{5,4},{6,7},{7,6},{8,9},{9,8},{10,11... | collective-permute-start | bytes 786440 | tf_op jit(solution)/shard_map/ppermute | solution.py:215
  33.8 7.3 %collective-permute-start.5 = (bf16[64,1024]{1,0:T(8,128)(2,1)S(1)}, bf16[64,1024]{1,0:T(8,128)(2,1)S(1)}, u32[]{:S(2)}, u32[]{:S(2)}) collective-permute-start(bf16[64,1024]{1,0:T(8,128)(2,1)S(1)} %slice.6), channel_id=1, source_target_pairs={{0,32},{32,64},{64,96},{96,0},{1,33},{33,65},{65,97},{97,1},{2,34}... | collective-permute-start | bytes 393224 | tf_op jit(solution)/shard_map/ppermute | solution.py:219
  33.9 7.2 %collective-permute-start.6 = (bf16[64,1024]{1,0:T(8,128)(2,1)S(1)}, bf16[64,1024]{1,0:T(8,128)(2,1)S(1)}, u32[]{:S(2)}, u32[]{:S(2)}) collective-permute-start(bf16[64,1024]{1,0:T(8,128)(2,1)S(1)} %slice.7), channel_id=1, source_target_pairs={{0,96},{32,0},{64,32},{96,64},{1,97},{33,1},{65,33},{97,65},{2,98}... | collective-permute-start | bytes 393224 | tf_op jit(solution)/shard_map/ppermute | solution.py:219
  37.1 13.7 %collective-permute-start.9 = (bf16[128,128]{1,0:T(8,128)(2,1)S(1)}, bf16[128,128]{1,0:T(8,128)(2,1)S(1)}, u32[]{:S(2)}, u32[]{:S(2)}) collective-permute-start(bf16[128,128]{1,0:T(8,128)(2,1)S(1)} %get-tuple-element.50), channel_id=1, source_target_pairs={{0,1},{1,0},{2,3},{3,2},{4,5},{5,4},{6,7},{7,6},{8,9},{9,8},{10,11... | collective-permute-start | bytes 98312 | tf_op jit(solution)/shard_map/ppermute | solution.py:215
  41.1 16.5 %copy-start.6 = (f32[128]{0:T(128)S(1)}, f32[128]{0:T(128)}, u32[]{:S(2)}) copy-start(f32[128]{0:T(128)} %param.12) | copy-start | bytes 1540
  41.2 5.1 %collective-permute-start.7 = (bf16[64,1024]{1,0:T(8,128)(2,1)S(1)}, bf16[64,1024]{1,0:T(8,128)(2,1)S(1)}, u32[]{:S(2)}, u32[]{:S(2)}) collective-permute-start(bf16[64,1024]{1,0:T(8,128)(2,1)S(1)} %collective-permute-done.5.refs_0_), channel_id=1, source_target_pairs={{0,1},{1,0},{2,3},{3,2},{4,5},{5,4},{6,7},{7,6},{8,9},{9,8},{10,11... | collective-permute-start | bytes 393224 | tf_op jit(solution)/shard_map/ppermute | solution.py:215
  41.8 4.5 %collective-permute-start.8 = (bf16[64,1024]{1,0:T(8,128)(2,1)S(1)}, bf16[64,1024]{1,0:T(8,128)(2,1)S(1)}, u32[]{:S(2)}, u32[]{:S(2)}) collective-permute-start(bf16[64,1024]{1,0:T(8,128)(2,1)S(1)} %collective-permute-done.6.refs_1_), channel_id=1, source_target_pairs={{0,1},{1,0},{2,3},{3,2},{4,5},{5,4},{6,7},{7,6},{8,9},{9,8},{10,11... | collective-permute-start | bytes 393224 | tf_op jit(solution)/shard_map/ppermute | solution.py:215
  45.8 5.1 %collective-permute-start.12 = (bf16[128,128]{1,0:T(8,128)(2,1)S(1)}, bf16[128,128]{1,0:T(8,128)(2,1)S(1)}, u32[]{:S(2)}, u32[]{:S(2)}) collective-permute-start(bf16[128,128]{1,0:T(8,128)(2,1)S(1)} %get-tuple-element.53), channel_id=1, source_target_pairs={{0,1},{1,0},{2,3},{3,2},{4,5},{5,4},{6,7},{7,6},{8,9},{9,8},{10,11... | collective-permute-start | bytes 98312 | tf_op jit(solution)/shard_map/ppermute | solution.py:215
  46.2 44.6 %copy-start.7 = (s32[32]{0:T(128)S(1)}, s32[32]{0:T(128)}, u32[]{:S(2)}) copy-start(s32[32]{0:T(128)} %param.15) | copy-start | bytes 388
  46.2 58.0 %copy-start.1 = (f32[1024]{0:T(1024)S(1)}, f32[1024]{0:T(1024)}, u32[]{:S(2)}) copy-start(f32[1024]{0:T(1024)} %param.13) | copy-start | bytes 12292
  46.2 58.0 %copy-start.2 = (f32[32,1024]{1,0:T(8,128)S(1)}, f32[32,1024]{1,0:T(8,128)}, u32[]{:S(2)}) copy-start(f32[32,1024]{1,0:T(8,128)} %param.8) | copy-start | bytes 393220
  46.2 58.0 %copy-start.3 = (f32[32,1024]{1,0:T(8,128)S(1)}, f32[32,1024]{1,0:T(8,128)}, u32[]{:S(2)}) copy-start(f32[32,1024]{1,0:T(8,128)} %param.9) | copy-start | bytes 393220
  46.3 58.0 %copy-start.4 = (f32[1024]{0:T(1024)S(1)}, f32[1024]{0:T(1024)}, u32[]{:S(2)}) copy-start(f32[1024]{0:T(1024)} %param.11) | copy-start | bytes 12292
  46.3 58.0 %copy-start.5 = (s32[32]{0:T(128)S(1)}, s32[32]{0:T(128)}, u32[]{:S(2)}) copy-start(s32[32]{0:T(128)} %param.14) | copy-start | bytes 388
  46.3 4.6 %collective-permute-start.10 = (bf16[128,128]{1,0:T(8,128)(2,1)S(1)}, bf16[128,128]{1,0:T(8,128)(2,1)S(1)}, u32[]{:S(2)}, u32[]{:S(2)}) collective-permute-start(bf16[128,128]{1,0:T(8,128)(2,1)S(1)} %get-tuple-element.51), channel_id=1, source_target_pairs={{0,1},{1,0},{2,3},{3,2},{4,5},{5,4},{6,7},{7,6},{8,9},{9,8},{10,11... | collective-permute-start | bytes 98312 | tf_op jit(solution)/shard_map/ppermute | solution.py:215
  50.4 1.3 %collective-permute-start.11 = (bf16[128,128]{1,0:T(8,128)(2,1)S(1)}, bf16[128,128]{1,0:T(8,128)(2,1)S(1)}, u32[]{:S(2)}, u32[]{:S(2)}) collective-permute-start(bf16[128,128]{1,0:T(8,128)(2,1)S(1)} %get-tuple-element.52), channel_id=1, source_target_pairs={{0,1},{1,0},{2,3},{3,2},{4,5},{5,4},{6,7},{7,6},{8,9},{9,8},{10,11... | collective-permute-start | bytes 98312 | tf_op jit(solution)/shard_map/ppermute | solution.py:215
  52.4 13.2 %all-to-all-start.1 = ((bf16[16,8,512]{2,1,0:T(8,128)(2,1)}), bf16[16,8,512]{2,1,0:T(8,128)(2,1)S(1)}, u32[]{:S(2)}, u32[]{:S(2)}) async-start(bf16[16,8,512]{2,1,0:T(8,128)(2,1)} %bitcast.4), calls=%async_computation.1 | async-start | bytes 262144 | tf_op jit(solution)/shard_map/all_to_all | solution.py:207
  77.4 4.0 %collective-permute-start.13 = (bf16[128,512]{1,0:T(8,128)(2,1)S(1)}, bf16[128,512]{1,0:T(8,128)(2,1)S(1)}, u32[]{:S(2)}, u32[]{:S(2)}) collective-permute-start(bf16[128,512]{1,0:T(8,128)(2,1)S(1)} %bitcast.9), channel_id=1, source_target_pairs={{0,1},{1,0},{2,3},{3,2},{4,5},{5,4},{6,7},{7,6},{8,9},{9,8},{10,11... | collective-permute-start | bytes 393224 | tf_op jit(solution)/shard_map/ppermute | solution.py:215
  86.0 12.5 %all-to-all-start.3 = ((bf16[32,8,128]{2,1,0:T(8,128)(2,1)}), bf16[32,8,128]{2,1,0:T(8,128)(2,1)S(1)}, u32[]{:S(2)}, u32[]{:S(2)}) async-start(bf16[32,8,128]{2,1,0:T(8,128)(2,1)} %bitcast.6), calls=%async_computation.3 | async-start | bytes 131072 | tf_op jit(solution)/shard_map/all_to_all | solution.py:207
  99.4 15.9 %all-to-all-start.4 = ((bf16[8,32,8,128]{3,2,1,0:T(8,128)(2,1)}), bf16[8,32,8,128]{3,2,1,0:T(8,128)(2,1)S(1)}, u32[]{:S(2)}, u32[]{:S(2)}) async-start(bf16[8,32,8,128]{3,2,1,0:T(8,128)(2,1)} %broadcast_in_dim.26), calls=%async_computation.4 | async-start | bytes 1048576 | tf_op jit(solution)/shard_map/all_to_all | solution.py:207

commit v4 on v3

--- a/solution.py
+++ b/solution.py
@@ -16,7 +16,9 @@
 N_IN = 8
 N_Y = 4
 N_SAME = 16
-WIDE = 128
+PARTS = 2
+FEW = 16
+WIDE = 256
 BF = jnp.bfloat16
 F32 = jnp.float32
 
@@ -103,14 +105,14 @@
         *inner_refs, out_ref, total = refs
     step = pl.program_id(0)
     slabs, rows, _ = inner_refs[0].shape
-    y, core = place_ref[0], place_ref[1]
+    half, core = place_ref[0], place_ref[1]
 
     for d, inner_ref in enumerate(inner_refs):
         acc = jnp.zeros((rows, WIDE), F32)
         for k in range(slabs):
             weight = airy_ref[k : k + 1, d * WIDE : (d + 1) * WIDE].astype(F32)
             acc = acc + weight * inner_ref[k].astype(F32)
-        at = pl.ds(pl.multiple_of(((y + d) % N_Y) * rows, rows), rows)
+        at = pl.ds(pl.multiple_of(((half + d) % PARTS) * rows, rows), rows)
 
         @pl.when(step == 0)
         def _():
@@ -122,7 +124,8 @@
 
     @pl.when(step == pl.num_programs(0) - 1)
     def _():
-        turned = total[...].T.astype(BF).reshape(N_SAME, 8, WIDE)
+        turned = total[...].T.reshape(N_SAME, FEW, PARTS * rows)
+        turned = jnp.concatenate([turned[:, :8], turned[:, 8:]], axis=2).astype(BF)
         if pair:
             out_ref[:, core] = mine_ref[...]
             out_ref[:, 1 - core] = turned
@@ -133,7 +136,7 @@
 def forces(place, airy, inners, mine=None, slabs=32):
     n_k, rows, _ = inners[0].shape
     pair = mine is not None
-    shape = (N_SAME, 2, 8, WIDE) if pair else (N_SAME, 8, WIDE)
+    shape = (N_SAME, 2, 8, 128) if pair else (N_SAME, 8, 128)
     extra = [mine] if pair else []
     return pl.pallas_call(
         functools.partial(force_kernel, pair),
@@ -144,7 +147,7 @@
             + [pl.BlockSpec((slabs, rows, WIDE), lambda k, s: (k, 0, 0))] * len(inners)
             + [pl.BlockSpec(m.shape, lambda k, s: (0, 0, 0)) for m in extra],
             out_specs=pl.BlockSpec(shape, lambda k, s: (0,) * len(shape)),
-            scratch_shapes=[pltpu.VMEM((N_Y * rows, WIDE), F32)],
+            scratch_shapes=[pltpu.VMEM((PARTS * rows, WIDE), F32)],
         ),
         out_shape=jax.ShapeDtypeStruct(shape, BF),
         cost_estimate=pl.CostEstimate(
@@ -152,20 +155,20 @@
         ),
         compiler_params=pltpu.CompilerParams(vmem_limit_bytes=12 << 20),
         name="forces",
-    )(place, airy, *[pltpu.with_memory_space_constraint(i, pltpu.HBM) for i in inners], *extra)
+    )(place, airy, *inners, *extra)
 
 
 def airy_kernel(place_ref, mine_ref, theirs_ref, out_ref):
-    y, core = place_ref[0], place_ref[1]
+    half, core = place_ref[0], place_ref[1]
     for source, at in ((mine_ref, core), (theirs_ref, 1 - core)):
-        for d in range(N_Y):
+        for d in range(PARTS):
             piece = source[:, d * WIDE : (d + 1) * WIDE].astype(F32).T
-            out_ref[:, at, (y + d) % N_Y] = piece.reshape(N_SAME, 8, WIDE)
+            out_ref[:, at, (half + d) % PARTS] = piece.reshape(N_SAME, FEW, piece.shape[1])
 
 
 def airy_output(place, mine, theirs):
     full = pl.BlockSpec(mine.shape, lambda i, s: (0, 0))
-    shape = (N_SAME, 2, N_Y, 8, WIDE)
+    shape = (N_SAME, 2, PARTS, FEW, mine.shape[0])
     return pl.pallas_call(
         airy_kernel,
         grid_spec=pltpu.PrefetchScalarGridSpec(
@@ -188,9 +191,8 @@
     scale = 1.0 + damping_ref[...]
     for a in range(4):
         rows = slice(8 * a, 8 * a + 8)
-        force = jnp.concatenate(
-            [total[r][:, 32 * a : 32 * a + 32] for r in range(2 * N_SAME)], axis=1
-        )
+        at = (a % 2) * 64 + (a // 2) * 32
+        force = jnp.concatenate([total[r][:, at : at + 32] for r in range(2 * N_SAME)], axis=1)
         out_ref[rows, :] = (base_ref[rows, :] - force) / scale
 
 
@@ -231,29 +233,23 @@
     core = lax.axis_index("c").astype(jnp.int32)
     same = lax.axis_index(SAME)
     row = lax.axis_index(ROW).astype(jnp.int32).reshape(1)
-    place = jnp.stack([y, core])
-    few = rows // N_Y
-
-    piece = lax.dynamic_slice_in_dim(amplitudes, y * few, few, 0).astype(BF)
+    half = y % PARTS
+    place = jnp.stack([half, core])
+
+    piece = lax.dynamic_slice_in_dim(amplitudes, half * FEW, FEW, 0).astype(BF)
     b0 = spread(piece, SAME, N_SAME).reshape(WIDE, width)
-    b3, b1 = shift(b0, 1), shift(b0, -1)
+    b1 = [shift(b0[: WIDE // 2], -1), shift(b0[WIDE // 2 :], 1)]
     o0 = swap(b0)
     (i0, j0), (p0, q0) = inner_products(row, coupling, [[b0], [o0]], [F32, BF])
 
-    b1, b3, p0, q0 = after((b1, b3, p0, q0))
-    b2a, b2b = shift(b3[: WIDE // 2], 1), shift(b1[WIDE // 2 :], -1)
-    o1, o3 = swap(b1), swap(b3)
-    (i1, i3), (p1, p3) = inner_products(row, coupling, [[b1], [b3]], [F32, F32])
-
-    o1, o3, b2a, b2b, p1 = after((o1, o3, b2a, b2b, p1))
-    o2a, o2b = swap(b2a), swap(b2b)
-    (j1, j3), (q1, q3) = inner_products(row, coupling, [[o1], [o3]], [BF, BF])
-
-    b2a, b2b, o2a, o2b, q1 = after((b2a, b2b, o2a, o2b, q1))
-    (i2, j2), (p2, q2) = inner_products(row, coupling, [[b2a, b2b], [o2a, o2b]], [F32, BF])
-
-    received = [swap(q) for q in (q0, q1, q2, q3)]
-    part = combine([p0, p1, p2, p3], received)
+    b1, p0, q0 = after((b1, p0, q0))
+    o1 = [swap(b) for b in b1]
+    (i1,), (p1,) = inner_products(row, coupling, [b1], [F32])
+
+    o1, p1 = after((o1, p1))
+    (j1,), (q1,) = inner_products(row, coupling, [o1], [BF])
+
+    part = combine([p0, p1], [swap(q0), swap(q1)])
     per = n_k // N_SAME
     n_half = part.shape[1]
     shares = exchange(part.reshape(N_SAME, per, n_half), SAME)
@@ -262,9 +258,9 @@
     airy_own = spread(summed.astype(BF), SAME, N_SAME).reshape(n_k, n_half)
     airy_other = swap(airy_own)
 
-    force_own = forces(place, airy_own, [i0, i1, i2, i3])
-    messages = forces(place, airy_other, [j0, j1, j2, j3], force_own)
-    arrived = exchange(messages.reshape(2 * N_SAME, 8, WIDE), ROW)
+    force_own = forces(place, airy_own, [i0, i1])
+    messages = forces(place, airy_other, [j0, j1], force_own)
+    arrived = exchange(messages.reshape(2 * N_SAME, 8, 128), ROW)
     parts = spread(arrived, INPLANE, N_IN)
     airy = airy_output(place, airy_own, airy_other).reshape(2 * N_SAME * rows, n_k)
 

time: 117 us -> 113 us (0.966)
  Pallas kernels: 27.5 us -> 21.7 us
  blocking collectives: 30.9 us -> 35.9 us
  starting transfers between devices: 23.3 us -> 20.8 us
  waiting for transfers between devices: 28.2 us -> 26 us
  local copies, waits for them, and re-layouts: 5.19 us -> 7.35 us
    all_to_all x2, blocking collectives: 30.9 us -> 35.9 us  [exchange(): return lax.all_to_all(x, axes, split_axis=0, concat_axis=0, tiled=True)]
    pallas_call x2, Pallas kernels: 8.54 us -> 4.15 us  [forces(): pl.pallas_call(functools.partial(force_kernel, pair), grid_spec=pltpu.Pre...]
    ppermute x4 -> x2, starting transfers between devices: 6.32 us -> 3.09 us  [shift(): return lax.ppermute(x, 'y', [(i, (i + by) % N_Y) for i in range(N_Y)])]
    ppermute x4 -> x2, waiting for transfers between devices: 2.29 us -> 0.01 us  [shift(): return lax.ppermute(x, 'y', [(i, (i + by) % N_Y) for i in range(N_Y)])]
    unnamed x16 -> x24, local copies, waits for them, and re-layouts: 3.42 us -> 5.45 us
    all_to_all x3, starting transfers between devices: 14.7 us -> 16.6 us  [exchange(): return lax.all_to_all(x, axes, split_axis=0, concat_axis=0, tiled=True)]
    pallas_call x4 -> x3, Pallas kernels: 15.9 us -> 14.5 us  [inner_products(): pl.pallas_call(functools.partial(inner_kernel, counts), grid_spec=pltpu.P...]
  transfers between devices with their start and end apart: 17 -> 11, of which waited for: 5 -> 4; matrix products, arithmetic and copies ran while one was open for 0% -> 0% of each run, Pallas kernels for 18% -> 16%
where the time goes in v4:
time: 113 us
  blocking collectives  35.9 us (32%)
  waiting for transfers between devices  26 us (23%)
  Pallas kernels  21.7 us (19%)
  starting transfers between devices  20.8 us (18%)
  local copies, waits for them, and re-layouts  7.35 us (7%)
    all_to_all x2, blocking collectives, exchange(): return lax.all_to_all(x, axes, split_axis=0, concat_axis=0, tiled=True)  35.9 us
    all_to_all x3, waiting for transfers between devices, exchange(): return lax.all_to_all(x, axes, split_axis=0, concat_axis=0, tiled=True)  25 us
    all_to_all x3, starting transfers between devices, exchange(): return lax.all_to_all(x, axes, split_axis=0, concat_axis=0, tiled=True)  16.6 us
    pallas_call x3, Pallas kernels, inner_products(): pl.pallas_call(functools.partial(inner_kernel, counts), grid_spec=pltpu.P...  14.5 us
    unnamed x24, local copies, waits for them, and re-layouts  5.45 us
    pallas_call x2, Pallas kernels, forces(): pl.pallas_call(functools.partial(force_kernel, pair), grid_spec=pltpu.Pre...  4.15 us
    ppermute x2, starting transfers between devices, shift(): return lax.ppermute(x, 'y', [(i, (i + by) % N_Y) for i in range(N_Y)])  3.09 us
  transfers between devices with their start and end apart: 11, of which 4 were waited for; matrix products, arithmetic and copies ran while one was open for 0% of the time, Pallas kernels for 16%

profile of v4, /device:TPU:2, one launch (start us, length us, event | category | flops | bytes accessed | tf_op | source)
XLA Modules:
  0.0 112.8 jit_solution(7699655189628166098)
XLA Ops:
  0.6 0.8 dynamic-slice_convert_fusion
  1.5 0.1 broadcast_in_dim.20
  1.6 24.2 %all_to_all.25 = bf16[16,16,1024]{2,1,0:T(8,128)(2,1)S(1)} all-to-all(bf16[16,16,1024]{2,1,0:T(8,128)(2,1)S(1)} %broadcast_in_dim.20), channel_id=1, replica_groups=mesh['xh'=2,'y'=4,'xl'=2,'z'=8,'c'=2] {'xl','z'}, dimensions={0} | all-to-all | bytes 1048576 | tf_op jit(solution)/shard_map/all_to_all | solution.py:209
  25.8 3.1 %collective-permute-start = (bf16[128,1024]{1,0:T(8,128)(2,1)S(1)}, bf16[128,1024]{1,0:T(8,128)(2,1)S(1)}, u32[]{:S(2)}, u32[]{:S(2)}) collective-permute-start(bf16[128,1024]{1,0:T(8,128)(2,1)S(1)} %bitcast.19), channel_id=1, source_target_pairs={{0,96},{32,0},{64,32},{96,64},{1,97},{33,1},{65,33},{97,65},{2,98}... | collective-permute-start | bytes 786440 | tf_op jit(solution)/shard_map/ppermute | solution.py:221
  28.9 3.4 %copy-done = bf16[128,32,1024]{2,1,0:T(8,128)(2,1)S(1)} copy-done((bf16[128,32,1024]{2,1,0:T(8,128)(2,1)S(1)}, bf16[128,32,1024]{2,1,0:T(8,128)(2,1)}, u32[]{:S(2)}) %copy-start) | copy-done | bytes 8388632
  32.3 6.5 %inner_products.3 = (bf16[128,32,256]{2,1,0:T(8,128)(2,1)}, bf16[128,32,256]{2,1,0:T(8,128)(2,1)}, f32[128,256]{1,0:T(8,128)S(1)}, bf16[128,256]{1,0:T(8,128)(2,1)S(1)}) custom-call(s32[1]{0:T(128)} %bitcast.4.row_ref, bf16[128,32,1024]{2,1,0:T(8,128)(2,1)S(1)} %copy-done, bf16[256,1024]{1,0:T(8,128)(2,1)S(1)} %bitcast.12, ...), custom_call_target="tpu_custom_call" | custom-call | flops 4294967296 | bytes 10485760 | tf_op jit(solution)/shard_map/inner_products/pallas_call | solution.py:61
  38.8 0.3 collective-permute-start.3
  39.2 0.3 collective-permute-start.4
  39.4 0.2 collective-permute-start.5
  39.7 4.0 %inner_products.4 = (bf16[128,32,256]{2,1,0:T(8,128)(2,1)}, f32[128,256]{1,0:T(8,128)S(1)}) custom-call(s32[1]{0:T(128)} %bitcast.4.row_ref, bf16[128,32,1024]{2,1,0:T(8,128)(2,1)S(1)} %copy-done, bf16[128,1024]{1,0:T(8,128)(2,1)S(1)} %collective-permute-done.refs_0_, bf16[128,1024]{1,0:T(8,128)(2,1)S(1)} %collective-permute-done.1.refs_1_), custom_call_target="tpu_custom_call" | custom-call | flops 2147483648 | bytes 10485760 | tf_op jit(solution)/shard_map/inner_products/pallas_call | solution.py:61
  43.7 4.0 %inner_products.5 = (bf16[128,32,256]{2,1,0:T(8,128)(2,1)}, bf16[128,256]{1,0:T(8,128)(2,1)S(1)}) custom-call(s32[1]{0:T(128)} %bitcast.4.row_ref, bf16[128,32,1024]{2,1,0:T(8,128)(2,1)S(1)} %copy-done, bf16[128,1024]{1,0:T(8,128)(2,1)S(1)} %collective-permute-done.3.refs_0_, bf16[128,1024]{1,0:T(8,128)(2,1)S(1)} %collective-permute-done.4.refs_1_), custom_call_target="tpu_custom_call" | custom-call | flops 2147483648 | bytes 10485760 | tf_op jit(solution)/shard_map/inner_products/pallas_call | solution.py:61
  47.7 0.3 collective-permute-start.6
  47.9 1.0 collective-permute-done.6.refs_3_
  48.9 0.7 combine.1
  49.6 5.8 %all-to-all-start.1 = ((bf16[16,8,512]{2,1,0:T(8,128)(2,1)}), bf16[16,8,512]{2,1,0:T(8,128)(2,1)S(1)}, u32[]{:S(2)}, u32[]{:S(2)}) async-start(bf16[16,8,512]{2,1,0:T(8,128)(2,1)} %bitcast.6), calls=%async_computation.1 | async-start | bytes 262144 | tf_op jit(solution)/shard_map/all_to_all | solution.py:209
  55.4 0.1 dynamic_slice.7
  55.5 7.8 %all-to-all-done.1 = bf16[16,8,512]{2,1,0:T(8,128)(2,1)S(1)} async-done(((bf16[16,8,512]{2,1,0:T(8,128)(2,1)}), bf16[16,8,512]{2,1,0:T(8,128)(2,1)S(1)}, u32[]{:S(2)}, u32[]{:S(2)}) %all-to-all-start.1) | async-done | bytes 131104 | tf_op jit(solution)/shard_map/all_to_all | solution.py:209
  63.3 0.1 divide_convert_fusion
  63.4 11.7 %all_to_all.26 = bf16[16,8,512]{2,1,0:T(8,128)(2,1)S(1)} all-to-all(bf16[16,8,512]{2,1,0:T(8,128)(2,1)S(1)} %broadcast_in_dim.21), channel_id=1, replica_groups=mesh['xh'=2,'y'=4,'xl'=2,'z'=8,'c'=2] {'xl','z'}, dimensions={0} | all-to-all | bytes 262144 | tf_op jit(solution)/shard_map/all_to_all | solution.py:209
  75.1 0.1 pad_add_fusion.place_ref
  75.2 1.6 %copy-done.3 = bf16[128,32,256]{2,1,0:T(8,128)(2,1)S(1)} copy-done((bf16[128,32,256]{2,1,0:T(8,128)(2,1)S(1)}, bf16[128,32,256]{2,1,0:T(8,128)(2,1)}, u32[]{:S(2)}) %copy-start.3) | copy-done | bytes 2097176
  76.8 1.8 %forces.2.refs_2_ = bf16[16,8,128]{2,1,0:T(8,128)(2,1)S(1)} custom-call(s32[2]{0:T(128)S(1)} %pad_add_fusion.place_ref, bf16[128,512]{1,0:T(8,128)(2,1)S(1)} %bitcast.14, bf16[128,32,256]{2,1,0:T(8,128)(2,1)S(1)} %copy-done.2, bf16[128,32,256]{2,1,0:T(8,128)(2,1)S(1)} %copy-done.3), custom_call_target="tpu_custom_call" | custom-call | flops 4194304 | bytes 4194304 | tf_op jit(solution)/shard_map/forces/pallas_call | solution.py:141
  78.6 0.4 copy-done.4
  79.0 2.4 %forces.3 = bf16[16,2,8,128]{3,2,1,0:T(8,128)(2,1)} custom-call(s32[2]{0:T(128)S(1)} %pad_add_fusion.place_ref, bf16[128,512]{1,0:T(8,128)(2,1)S(1)} %collective-permute-done.7.airy_ref.theirs_ref, bf16[128,32,256]{2,1,0:T(8,128)(2,1)S(1)} %copy-done.1, bf16[128,32,256]{2,1,0:T(8,128)(2,1)S(1)} %copy-done.4, bf16[16,8,128]{2,1,0:T(8,128)(2,1)S(1)} %forces.2.refs_2_), custom_call_target="tpu_custom_call" | custom-call | flops 4194304 | bytes 4194304 | tf_op jit(solution)/shard_map/forces/pallas_call | solution.py:141
  81.4 4.7 %all-to-all-start.3 = ((bf16[32,8,128]{2,1,0:T(8,128)(2,1)}), bf16[32,8,128]{2,1,0:T(8,128)(2,1)S(1)}, u32[]{:S(2)}, u32[]{:S(2)}) async-start(bf16[32,8,128]{2,1,0:T(8,128)(2,1)} %bitcast.8), calls=%async_computation.3 | async-start | bytes 131072 | tf_op jit(solution)/shard_map/all_to_all | solution.py:209
  86.2 7.7 %all-to-all-done.3 = bf16[32,8,128]{2,1,0:T(8,128)(2,1)S(1)} async-done(((bf16[32,8,128]{2,1,0:T(8,128)(2,1)}), bf16[32,8,128]{2,1,0:T(8,128)(2,1)S(1)}, u32[]{:S(2)}, u32[]{:S(2)}) %all-to-all-start.3) | async-done | bytes 65568 | tf_op jit(solution)/shard_map/all_to_all | solution.py:209
  93.9 0.9 broadcast_in_dim.26
  94.8 6.1 %all-to-all-start.4 = ((bf16[8,32,8,128]{3,2,1,0:T(8,128)(2,1)}), bf16[8,32,8,128]{3,2,1,0:T(8,128)(2,1)S(1)}, u32[]{:S(2)}, u32[]{:S(2)}) async-start(bf16[8,32,8,128]{3,2,1,0:T(8,128)(2,1)} %broadcast_in_dim.26), calls=%async_computation.4 | async-start | bytes 1048576 | tf_op jit(solution)/shard_map/all_to_all | solution.py:209
  100.9 0.1 select_add_fusion.base_ref
  101.0 1.5 %airy_output.1 = f32[16,2,2,16,128]{4,3,2,1,0:T(8,128)} custom-call(s32[2]{0:T(128)S(1)} %pad_add_fusion.place_ref, bf16[128,512]{1,0:T(8,128)(2,1)S(1)} %bitcast.15, bf16[128,512]{1,0:T(8,128)(2,1)S(1)} %collective-permute-done.7.airy_ref.theirs_ref), custom_call_target="tpu_custom_call" | custom-call | flops 1048576 | bytes 1048576 | tf_op jit(solution)/shard_map/airy_output/pallas_call | solution.py:172
  102.5 9.4 %all-to-all-done.4.parts_ref = bf16[8,32,8,128]{3,2,1,0:T(8,128)(2,1)S(1)} async-done(((bf16[8,32,8,128]{3,2,1,0:T(8,128)(2,1)}), bf16[8,32,8,128]{3,2,1,0:T(8,128)(2,1)S(1)}, u32[]{:S(2)}, u32[]{:S(2)}) %all-to-all-start.4) | async-done | bytes 524320 | tf_op jit(solution)/shard_map/all_to_all | solution.py:209
  112.0 0.9 final_step.1
  (36 shorter events, 0.2 us)
Async XLA Ops:
  25.8 3.1 %collective-permute-start.2 = (bf16[256,1024]{1,0:T(8,128)(2,1)S(1)}, bf16[256,1024]{1,0:T(8,128)(2,1)S(1)}, u32[]{:S(2)}, u32[]{:S(2)}) collective-permute-start(bf16[256,1024]{1,0:T(8,128)(2,1)S(1)} %bitcast.11), channel_id=1, source_target_pairs={{0,1},{1,0},{2,3},{3,2},{4,5},{5,4},{6,7},{7,6},{8,9},{9,8},{10,11... | collective-permute-start | bytes 1572872 | tf_op jit(solution)/shard_map/ppermute | solution.py:217
  25.8 13.0 %collective-permute-start = (bf16[128,1024]{1,0:T(8,128)(2,1)S(1)}, bf16[128,1024]{1,0:T(8,128)(2,1)S(1)}, u32[]{:S(2)}, u32[]{:S(2)}) collective-permute-start(bf16[128,1024]{1,0:T(8,128)(2,1)S(1)} %bitcast.19), channel_id=1, source_target_pairs={{0,96},{32,0},{64,32},{96,64},{1,97},{33,1},{65,33},{97,65},{2,98}... | collective-permute-start | bytes 786440 | tf_op jit(solution)/shard_map/ppermute | solution.py:221
  28.9 9.9 %collective-permute-start.1 = (bf16[128,1024]{1,0:T(8,128)(2,1)S(1)}, bf16[128,1024]{1,0:T(8,128)(2,1)S(1)}, u32[]{:S(2)}, u32[]{:S(2)}) collective-permute-start(bf16[128,1024]{1,0:T(8,128)(2,1)S(1)} %bitcast.18), channel_id=1, source_target_pairs={{0,32},{32,64},{64,96},{96,0},{1,33},{33,65},{65,97},{97,1},{2,34}... | collective-permute-start | bytes 786440 | tf_op jit(solution)/shard_map/ppermute | solution.py:221
  28.9 3.4 %copy-start = (bf16[128,32,1024]{2,1,0:T(8,128)(2,1)S(1)}, bf16[128,32,1024]{2,1,0:T(8,128)(2,1)}, u32[]{:S(2)}) copy-start(bf16[128,32,1024]{2,1,0:T(8,128)(2,1)} %tensor_ref.5) | copy-start | bytes 25165828
  38.8 4.8 %collective-permute-start.3 = (bf16[128,1024]{1,0:T(8,128)(2,1)S(1)}, bf16[128,1024]{1,0:T(8,128)(2,1)S(1)}, u32[]{:S(2)}, u32[]{:S(2)}) collective-permute-start(bf16[128,1024]{1,0:T(8,128)(2,1)S(1)} %collective-permute-done.refs_0_), channel_id=1, source_target_pairs={{0,1},{1,0},{2,3},{3,2},{4,5},{5,4},{6,7},{7,6},{8,9},{9,8},{10,11... | collective-permute-start | bytes 786440 | tf_op jit(solution)/shard_map/ppermute | solution.py:217
  39.2 4.5 %collective-permute-start.4 = (bf16[128,1024]{1,0:T(8,128)(2,1)S(1)}, bf16[128,1024]{1,0:T(8,128)(2,1)S(1)}, u32[]{:S(2)}, u32[]{:S(2)}) collective-permute-start(bf16[128,1024]{1,0:T(8,128)(2,1)S(1)} %collective-permute-done.1.refs_1_), channel_id=1, source_target_pairs={{0,1},{1,0},{2,3},{3,2},{4,5},{5,4},{6,7},{7,6},{8,9},{9,8},{10,11... | collective-permute-start | bytes 786440 | tf_op jit(solution)/shard_map/ppermute | solution.py:217
  39.4 8.5 %collective-permute-start.5 = (bf16[128,256]{1,0:T(8,128)(2,1)S(1)}, bf16[128,256]{1,0:T(8,128)(2,1)S(1)}, u32[]{:S(2)}, u32[]{:S(2)}) collective-permute-start(bf16[128,256]{1,0:T(8,128)(2,1)S(1)} %get-tuple-element.24), channel_id=1, source_target_pairs={{0,1},{1,0},{2,3},{3,2},{4,5},{5,4},{6,7},{7,6},{8,9},{9,8},{10,11... | collective-permute-start | bytes 196616 | tf_op jit(solution)/shard_map/ppermute | solution.py:217
  43.7 11.7 %copy-start.10 = (f32[128]{0:T(128)S(1)}, f32[128]{0:T(128)}, u32[]{:S(2)}) copy-start(f32[128]{0:T(128)} %param.12) | copy-start | bytes 1540
  43.7 31.5 %copy-start.2 = (bf16[128,32,256]{2,1,0:T(8,128)(2,1)S(1)}, bf16[128,32,256]{2,1,0:T(8,128)(2,1)}, u32[]{:S(2)}) copy-start(bf16[128,32,256]{2,1,0:T(8,128)(2,1)} %get-tuple-element.30.refs_0_) | copy-start | bytes 6291460
  47.7 1.3 %collective-permute-start.6 = (bf16[128,256]{1,0:T(8,128)(2,1)S(1)}, bf16[128,256]{1,0:T(8,128)(2,1)S(1)}, u32[]{:S(2)}, u32[]{:S(2)}) collective-permute-start(bf16[128,256]{1,0:T(8,128)(2,1)S(1)} %get-tuple-element.27), channel_id=1, source_target_pairs={{0,1},{1,0},{2,3},{3,2},{4,5},{5,4},{6,7},{7,6},{8,9},{9,8},{10,11... | collective-permute-start | bytes 196616 | tf_op jit(solution)/shard_map/ppermute | solution.py:217
  49.6 13.7 %all-to-all-start.1 = ((bf16[16,8,512]{2,1,0:T(8,128)(2,1)}), bf16[16,8,512]{2,1,0:T(8,128)(2,1)S(1)}, u32[]{:S(2)}, u32[]{:S(2)}) async-start(bf16[16,8,512]{2,1,0:T(8,128)(2,1)} %bitcast.6), calls=%async_computation.1 | async-start | bytes 262144 | tf_op jit(solution)/shard_map/all_to_all | solution.py:209
  75.1 3.4 %collective-permute-start.7 = (bf16[128,512]{1,0:T(8,128)(2,1)S(1)}, bf16[128,512]{1,0:T(8,128)(2,1)S(1)}, u32[]{:S(2)}, u32[]{:S(2)}) collective-permute-start(bf16[128,512]{1,0:T(8,128)(2,1)S(1)} %bitcast.13), channel_id=1, source_target_pairs={{0,1},{1,0},{2,3},{3,2},{4,5},{5,4},{6,7},{7,6},{8,9},{9,8},{10,11... | collective-permute-start | bytes 393224 | tf_op jit(solution)/shard_map/ppermute | solution.py:217
  75.2 1.6 %copy-start.3 = (bf16[128,32,256]{2,1,0:T(8,128)(2,1)S(1)}, bf16[128,32,256]{2,1,0:T(8,128)(2,1)}, u32[]{:S(2)}) copy-start(bf16[128,32,256]{2,1,0:T(8,128)(2,1)} %get-tuple-element.31.refs_1_) | copy-start | bytes 6291460
  76.8 1.8 %copy-start.1 = (bf16[128,32,256]{2,1,0:T(8,128)(2,1)S(1)}, bf16[128,32,256]{2,1,0:T(8,128)(2,1)}, u32[]{:S(2)}) copy-start(bf16[128,32,256]{2,1,0:T(8,128)(2,1)} %get-tuple-element.28.refs_0_) | copy-start | bytes 6291460
  76.8 2.2 %copy-start.4 = (bf16[128,32,256]{2,1,0:T(8,128)(2,1)S(1)}, bf16[128,32,256]{2,1,0:T(8,128)(2,1)}, u32[]{:S(2)}) copy-start(bf16[128,32,256]{2,1,0:T(8,128)(2,1)} %get-tuple-element.29.refs_1_) | copy-start | bytes 6291460
  79.0 7.2 %copy-start.11 = (s32[32]{0:T(128)S(1)}, s32[32]{0:T(128)}, u32[]{:S(2)}) copy-start(s32[32]{0:T(128)} %param.15) | copy-start | bytes 388
  79.0 21.9 %copy-start.5 = (f32[1024]{0:T(1024)S(1)}, f32[1024]{0:T(1024)}, u32[]{:S(2)}) copy-start(f32[1024]{0:T(1024)} %param.13) | copy-start | bytes 12292
  79.0 21.9 %copy-start.6 = (f32[32,1024]{1,0:T(8,128)S(1)}, f32[32,1024]{1,0:T(8,128)}, u32[]{:S(2)}) copy-start(f32[32,1024]{1,0:T(8,128)} %param.8) | copy-start | bytes 393220
  79.0 21.9 %copy-start.7 = (f32[32,1024]{1,0:T(8,128)S(1)}, f32[32,1024]{1,0:T(8,128)}, u32[]{:S(2)}) copy-start(f32[32,1024]{1,0:T(8,128)} %param.9) | copy-start | bytes 393220
  79.0 21.9 %copy-start.8 = (f32[1024]{0:T(1024)S(1)}, f32[1024]{0:T(1024)}, u32[]{:S(2)}) copy-start(f32[1024]{0:T(1024)} %param.11) | copy-start | bytes 12292
  79.0 21.9 %copy-start.9 = (s32[32]{0:T(128)S(1)}, s32[32]{0:T(128)}, u32[]{:S(2)}) copy-start(s32[32]{0:T(128)} %param.14) | copy-start | bytes 388
  81.4 12.5 %all-to-all-start.3 = ((bf16[32,8,128]{2,1,0:T(8,128)(2,1)}), bf16[32,8,128]{2,1,0:T(8,128)(2,1)S(1)}, u32[]{:S(2)}, u32[]{:S(2)}) async-start(bf16[32,8,128]{2,1,0:T(8,128)(2,1)} %bitcast.8), calls=%async_computation.3 | async-start | bytes 131072 | tf_op jit(solution)/shard_map/all_to_all | solution.py:209
  94.8 17.1 %all-to-all-start.4 = ((bf16[8,32,8,128]{3,2,1,0:T(8,128)(2,1)}), bf16[8,32,8,128]{3,2,1,0:T(8,128)(2,1)S(1)}, u32[]{:S(2)}, u32[]{:S(2)}) async-start(bf16[8,32,8,128]{3,2,1,0:T(8,128)(2,1)} %broadcast_in_dim.26), calls=%async_computation.4 | async-start | bytes 1048576 | tf_op jit(solution)/shard_map/all_to_all | solution.py:209

commit v5 on v4

--- a/solution.py
+++ b/solution.py
@@ -23,15 +23,23 @@
 F32 = jnp.float32
 
 
-def inner_kernel(counts, row_ref, tensor_ref, *refs):
+VMEM = pl.BlockSpec(memory_space=pltpu.VMEM)
+
+
+def in_vmem(x):
+    return pltpu.with_memory_space_constraint(x, pltpu.VMEM)
+
+
+def inner_kernel(counts, slabs, row_ref, tensor_ref, *refs):
     n_in, blocks = sum(counts), len(counts)
     case_refs = refs[:n_in]
     inner_refs = refs[n_in : n_in + blocks]
     part_refs = refs[n_in + blocks : n_in + 2 * blocks]
     turned = refs[-1]
-    slabs, rows, width = tensor_ref.shape
-
-    @pl.when(pl.program_id(0) == 0)
+    _, rows, width = tensor_ref.shape
+    step = pl.program_id(0)
+
+    @pl.when(step == 0)
     def _():
         at = 0
         for b, count in enumerate(counts):
@@ -42,8 +50,9 @@
 
     start = pl.multiple_of(row_ref[0] * rows, rows)
     columns = turned[pl.ds(start, rows), :].astype(F32)
+    tensor = tensor_ref[pl.ds(step * slabs, slabs)]
     inner = jnp.dot(
-        tensor_ref[...].reshape(slabs * rows, width), turned[...], preferred_element_type=F32
+        tensor.reshape(slabs * rows, width), turned[...], preferred_element_type=F32
     ).reshape(slabs, rows, blocks * WIDE)
     for b in range(blocks):
         span = slice(b * WIDE, (b + 1) * WIDE)
@@ -59,12 +68,11 @@
     cases = [c for g in groups for c in g]
     blocks = len(groups)
     out = pl.pallas_call(
-        functools.partial(inner_kernel, counts),
+        functools.partial(inner_kernel, counts, slabs),
         grid_spec=pltpu.PrefetchScalarGridSpec(
             num_scalar_prefetch=1,
             grid=(n_k // slabs,),
-            in_specs=[pl.BlockSpec((slabs, rows, width), lambda k, r: (k, 0, 0))]
-            + [pl.BlockSpec(c.shape, lambda k, r: (0, 0)) for c in cases],
+            in_specs=[VMEM] * (1 + len(cases)),
             out_specs=[pl.BlockSpec((slabs, rows, WIDE), lambda k, r: (k, 0, 0))] * blocks
             + [pl.BlockSpec((slabs, WIDE), lambda k, r: (k, 0))] * blocks,
             scratch_shapes=[pltpu.VMEM((width, blocks * WIDE), BF)],
@@ -74,9 +82,9 @@
         cost_estimate=pl.CostEstimate(
             flops=2 * n_k * rows * width * blocks * WIDE, bytes_accessed=10 << 20, transcendentals=0
         ),
-        compiler_params=pltpu.CompilerParams(vmem_limit_bytes=24 << 20),
+        compiler_params=pltpu.CompilerParams(vmem_limit_bytes=20 << 20),
         name="inner_products",
-    )(row, coupling, *cases)
+    )(row, in_vmem(coupling), *[in_vmem(c) for c in cases])
     return out[:blocks], out[blocks:]
 
 
@@ -103,59 +111,43 @@
         *inner_refs, mine_ref, out_ref, total = refs
     else:
         *inner_refs, out_ref, total = refs
-    step = pl.program_id(0)
-    slabs, rows, _ = inner_refs[0].shape
+    n_k, rows, _ = inner_refs[0].shape
     half, core = place_ref[0], place_ref[1]
 
     for d, inner_ref in enumerate(inner_refs):
         acc = jnp.zeros((rows, WIDE), F32)
-        for k in range(slabs):
+        for k in range(n_k):
             weight = airy_ref[k : k + 1, d * WIDE : (d + 1) * WIDE].astype(F32)
             acc = acc + weight * inner_ref[k].astype(F32)
         at = pl.ds(pl.multiple_of(((half + d) % PARTS) * rows, rows), rows)
-
-        @pl.when(step == 0)
-        def _():
-            total[at, :] = acc
-
-        @pl.when(step > 0)
-        def _():
-            total[at, :] += acc
-
-    @pl.when(step == pl.num_programs(0) - 1)
-    def _():
-        turned = total[...].T.reshape(N_SAME, FEW, PARTS * rows)
-        turned = jnp.concatenate([turned[:, :8], turned[:, 8:]], axis=2).astype(BF)
-        if pair:
-            out_ref[:, core] = mine_ref[...]
-            out_ref[:, 1 - core] = turned
-        else:
-            out_ref[...] = turned
-
-
-def forces(place, airy, inners, mine=None, slabs=32):
+        total[at, :] = acc
+
+    turned = total[...].T.reshape(N_SAME, FEW, PARTS * rows)
+    turned = jnp.concatenate([turned[:, :8], turned[:, 8:]], axis=2).astype(BF)
+    if pair:
+        out_ref[:, core] = mine_ref[...]
+        out_ref[:, 1 - core] = turned
+    else:
+        out_ref[...] = turned
+
+
+def forces(place, airy, inners, mine=None):
     n_k, rows, _ = inners[0].shape
     pair = mine is not None
     shape = (N_SAME, 2, 8, 128) if pair else (N_SAME, 8, 128)
-    extra = [mine] if pair else []
+    operands = [airy, *inners] + ([mine] if pair else [])
     return pl.pallas_call(
         functools.partial(force_kernel, pair),
-        grid_spec=pltpu.PrefetchScalarGridSpec(
-            num_scalar_prefetch=1,
-            grid=(n_k // slabs,),
-            in_specs=[pl.BlockSpec((slabs, airy.shape[1]), lambda k, s: (k, 0))]
-            + [pl.BlockSpec((slabs, rows, WIDE), lambda k, s: (k, 0, 0))] * len(inners)
-            + [pl.BlockSpec(m.shape, lambda k, s: (0, 0, 0)) for m in extra],
-            out_specs=pl.BlockSpec(shape, lambda k, s: (0,) * len(shape)),
-            scratch_shapes=[pltpu.VMEM((PARTS * rows, WIDE), F32)],
-        ),
+        in_specs=[pl.BlockSpec(memory_space=pltpu.SMEM)] + [VMEM] * len(operands),
+        out_specs=VMEM,
         out_shape=jax.ShapeDtypeStruct(shape, BF),
+        scratch_shapes=[pltpu.VMEM((PARTS * rows, WIDE), F32)],
         cost_estimate=pl.CostEstimate(
             flops=2 * n_k * rows * airy.shape[1], bytes_accessed=4 << 20, transcendentals=0
         ),
-        compiler_params=pltpu.CompilerParams(vmem_limit_bytes=12 << 20),
+        compiler_params=pltpu.CompilerParams(vmem_limit_bytes=8 << 20),
         name="forces",
-    )(place, airy, *inners, *extra)
+    )(place, *[in_vmem(x) for x in operands])
 
 
 def airy_kernel(place_ref, mine_ref, theirs_ref, out_ref):

time: 113 us -> 113 us (level)
  no operation moved by 1% of the time
where the time goes in v5:
time: 113 us
  blocking collectives  35.9 us (32%)
  waiting for transfers between devices  26 us (23%)
  Pallas kernels  21.6 us (19%)
  starting transfers between devices  20.8 us (18%)
  local copies, waits for them, and re-layouts  7.41 us (7%)
    all_to_all x2, blocking collectives, exchange(): return lax.all_to_all(x, axes, split_axis=0, concat_axis=0, tiled=True)  35.9 us
    all_to_all x3, waiting for transfers between devices, exchange(): return lax.all_to_all(x, axes, split_axis=0, concat_axis=0, tiled=True)  25 us
    all_to_all x3, starting transfers between devices, exchange(): return lax.all_to_all(x, axes, split_axis=0, concat_axis=0, tiled=True)  16.6 us
    pallas_call x3, Pallas kernels, inner_products(): pl.pallas_call(functools.partial(inner_kernel, counts, slabs), grid_spec=...  14.5 us
    unnamed x24, local copies, waits for them, and re-layouts  5.5 us
    pallas_call x2, Pallas kernels, forces(): pl.pallas_call(functools.partial(force_kernel, pair), in_specs=[pl.BlockS...  4.07 us
    ppermute x2, starting transfers between devices, shift(): return lax.ppermute(x, 'y', [(i, (i + by) % N_Y) for i in range(N_Y)])  3.09 us
  transfers between devices with their start and end apart: 11, of which 4 were waited for; matrix products, arithmetic and copies ran while one was open for 0% of the time, Pallas kernels for 16%

profile of v5, /device:TPU:2, one launch (start us, length us, event | category | flops | bytes accessed | tf_op | source)
XLA Modules:
  0.0 112.8 jit_solution(3934028550071490362)
XLA Ops:
  0.6 0.8 dynamic-slice_convert_fusion
  1.5 0.1 broadcast_in_dim.20
  1.6 24.2 %all_to_all.25 = bf16[16,16,1024]{2,1,0:T(8,128)(2,1)S(1)} all-to-all(bf16[16,16,1024]{2,1,0:T(8,128)(2,1)S(1)} %broadcast_in_dim.20), channel_id=1, replica_groups=mesh['xh'=2,'y'=4,'xl'=2,'z'=8,'c'=2] {'xl','z'}, dimensions={0} | all-to-all | bytes 1048576 | tf_op jit(solution)/shard_map/all_to_all | solution.py:201
  25.8 3.1 %collective-permute-start = (bf16[128,1024]{1,0:T(8,128)(2,1)S(1)}, bf16[128,1024]{1,0:T(8,128)(2,1)S(1)}, u32[]{:S(2)}, u32[]{:S(2)}) collective-permute-start(bf16[128,1024]{1,0:T(8,128)(2,1)S(1)} %bitcast.19), channel_id=1, source_target_pairs={{0,96},{32,0},{64,32},{96,64},{1,97},{33,1},{65,33},{97,65},{2,98}... | collective-permute-start | bytes 786440 | tf_op jit(solution)/shard_map/ppermute | solution.py:213
  28.9 3.4 %copy-done = bf16[128,32,1024]{2,1,0:T(8,128)(2,1)S(1)} copy-done((bf16[128,32,1024]{2,1,0:T(8,128)(2,1)S(1)}, bf16[128,32,1024]{2,1,0:T(8,128)(2,1)}, u32[]{:S(2)}) %copy-start) | copy-done | bytes 8388632
  32.3 6.5 %inner_products.3 = (bf16[128,32,256]{2,1,0:T(8,128)(2,1)}, bf16[128,32,256]{2,1,0:T(8,128)(2,1)}, f32[128,256]{1,0:T(8,128)S(1)}, bf16[128,256]{1,0:T(8,128)(2,1)S(1)}) custom-call(s32[1]{0:T(128)} %bitcast.4.row_ref, bf16[128,32,1024]{2,1,0:T(8,128)(2,1)S(1)} %copy-done, bf16[256,1024]{1,0:T(8,128)(2,1)S(1)} %bitcast.12, ...), custom_call_target="tpu_custom_call" | custom-call | flops 4294967296 | bytes 10485760 | tf_op jit(solution)/shard_map/inner_products/pallas_call | solution.py:70
  38.8 0.3 collective-permute-start.3
  39.1 0.3 collective-permute-start.4
  39.4 0.2 collective-permute-start.5
  39.6 4.0 %inner_products.4 = (bf16[128,32,256]{2,1,0:T(8,128)(2,1)}, f32[128,256]{1,0:T(8,128)S(1)}) custom-call(s32[1]{0:T(128)} %bitcast.4.row_ref, bf16[128,32,1024]{2,1,0:T(8,128)(2,1)S(1)} %copy-done, bf16[128,1024]{1,0:T(8,128)(2,1)S(1)} %collective-permute-done.refs_0_, bf16[128,1024]{1,0:T(8,128)(2,1)S(1)} %collective-permute-done.1.refs_1_), custom_call_target="tpu_custom_call" | custom-call | flops 2147483648 | bytes 10485760 | tf_op jit(solution)/shard_map/inner_products/pallas_call | solution.py:70
  43.7 4.0 %inner_products.5 = (bf16[128,32,256]{2,1,0:T(8,128)(2,1)}, bf16[128,256]{1,0:T(8,128)(2,1)S(1)}) custom-call(s32[1]{0:T(128)} %bitcast.4.row_ref, bf16[128,32,1024]{2,1,0:T(8,128)(2,1)S(1)} %copy-done, bf16[128,1024]{1,0:T(8,128)(2,1)S(1)} %collective-permute-done.3.refs_0_, bf16[128,1024]{1,0:T(8,128)(2,1)S(1)} %collective-permute-done.4.refs_1_), custom_call_target="tpu_custom_call" | custom-call | flops 2147483648 | bytes 10485760 | tf_op jit(solution)/shard_map/inner_products/pallas_call | solution.py:70
  47.6 0.3 collective-permute-start.6
  47.9 1.0 collective-permute-done.6.refs_3_
  48.9 0.7 combine.1
  49.6 5.8 %all-to-all-start.1 = ((bf16[16,8,512]{2,1,0:T(8,128)(2,1)}), bf16[16,8,512]{2,1,0:T(8,128)(2,1)S(1)}, u32[]{:S(2)}, u32[]{:S(2)}) async-start(bf16[16,8,512]{2,1,0:T(8,128)(2,1)} %bitcast.6), calls=%async_computation.1 | async-start | bytes 262144 | tf_op jit(solution)/shard_map/all_to_all | solution.py:201
  55.4 0.1 dynamic_slice.7
  55.4 7.9 %all-to-all-done.1 = bf16[16,8,512]{2,1,0:T(8,128)(2,1)S(1)} async-done(((bf16[16,8,512]{2,1,0:T(8,128)(2,1)}), bf16[16,8,512]{2,1,0:T(8,128)(2,1)S(1)}, u32[]{:S(2)}, u32[]{:S(2)}) %all-to-all-start.1) | async-done | bytes 131104 | tf_op jit(solution)/shard_map/all_to_all | solution.py:201
  63.3 0.1 divide_convert_fusion
  63.4 11.7 %all_to_all.26 = bf16[16,8,512]{2,1,0:T(8,128)(2,1)S(1)} all-to-all(bf16[16,8,512]{2,1,0:T(8,128)(2,1)S(1)} %broadcast_in_dim.21), channel_id=1, replica_groups=mesh['xh'=2,'y'=4,'xl'=2,'z'=8,'c'=2] {'xl','z'}, dimensions={0} | all-to-all | bytes 262144 | tf_op jit(solution)/shard_map/all_to_all | solution.py:201
  75.1 0.1 pad_add_fusion.place_ref
  75.2 1.6 %copy-done.3 = bf16[128,32,256]{2,1,0:T(8,128)(2,1)S(1)} copy-done((bf16[128,32,256]{2,1,0:T(8,128)(2,1)S(1)}, bf16[128,32,256]{2,1,0:T(8,128)(2,1)}, u32[]{:S(2)}) %copy-start.3) | copy-done | bytes 2097176
  76.8 1.7 %forces.2.refs_2_ = bf16[16,8,128]{2,1,0:T(8,128)(2,1)S(1)} custom-call(s32[2]{0:T(128)S(1)} %pad_add_fusion.place_ref, bf16[128,512]{1,0:T(8,128)(2,1)S(1)} %bitcast.14, bf16[128,32,256]{2,1,0:T(8,128)(2,1)S(1)} %copy-done.2, bf16[128,32,256]{2,1,0:T(8,128)(2,1)S(1)} %copy-done.3), custom_call_target="tpu_custom_call" | custom-call | flops 4194304 | bytes 4194304 | tf_op jit(solution)/shard_map/forces/pallas_call | solution.py:139
  78.5 0.5 copy-done.4
  79.0 2.4 %forces.3 = bf16[16,2,8,128]{3,2,1,0:T(8,128)(2,1)} custom-call(s32[2]{0:T(128)S(1)} %pad_add_fusion.place_ref, bf16[128,512]{1,0:T(8,128)(2,1)S(1)} %collective-permute-done.7.airy_ref.theirs_ref, bf16[128,32,256]{2,1,0:T(8,128)(2,1)S(1)} %copy-done.1, bf16[128,32,256]{2,1,0:T(8,128)(2,1)S(1)} %copy-done.4, bf16[16,8,128]{2,1,0:T(8,128)(2,1)S(1)} %forces.2.refs_2_), custom_call_target="tpu_custom_call" | custom-call | flops 4194304 | bytes 4194304 | tf_op jit(solution)/shard_map/forces/pallas_call | solution.py:139
  81.4 4.7 %all-to-all-start.3 = ((bf16[32,8,128]{2,1,0:T(8,128)(2,1)}), bf16[32,8,128]{2,1,0:T(8,128)(2,1)S(1)}, u32[]{:S(2)}, u32[]{:S(2)}) async-start(bf16[32,8,128]{2,1,0:T(8,128)(2,1)} %bitcast.8), calls=%async_computation.3 | async-start | bytes 131072 | tf_op jit(solution)/shard_map/all_to_all | solution.py:201
  86.2 7.7 %all-to-all-done.3 = bf16[32,8,128]{2,1,0:T(8,128)(2,1)S(1)} async-done(((bf16[32,8,128]{2,1,0:T(8,128)(2,1)}), bf16[32,8,128]{2,1,0:T(8,128)(2,1)S(1)}, u32[]{:S(2)}, u32[]{:S(2)}) %all-to-all-start.3) | async-done | bytes 65568 | tf_op jit(solution)/shard_map/all_to_all | solution.py:201
  93.9 0.9 broadcast_in_dim.26
  94.8 6.1 %all-to-all-start.4 = ((bf16[8,32,8,128]{3,2,1,0:T(8,128)(2,1)}), bf16[8,32,8,128]{3,2,1,0:T(8,128)(2,1)S(1)}, u32[]{:S(2)}, u32[]{:S(2)}) async-start(bf16[8,32,8,128]{3,2,1,0:T(8,128)(2,1)} %broadcast_in_dim.26), calls=%async_computation.4 | async-start | bytes 1048576 | tf_op jit(solution)/shard_map/all_to_all | solution.py:201
  100.9 0.1 select_add_fusion.base_ref
  101.0 1.5 %airy_output.1 = f32[16,2,2,16,128]{4,3,2,1,0:T(8,128)} custom-call(s32[2]{0:T(128)S(1)} %pad_add_fusion.place_ref, bf16[128,512]{1,0:T(8,128)(2,1)S(1)} %bitcast.15, bf16[128,512]{1,0:T(8,128)(2,1)S(1)} %collective-permute-done.7.airy_ref.theirs_ref), custom_call_target="tpu_custom_call" | custom-call | flops 1048576 | bytes 1048576 | tf_op jit(solution)/shard_map/airy_output/pallas_call | solution.py:164
  102.5 9.4 %all-to-all-done.4.parts_ref = bf16[8,32,8,128]{3,2,1,0:T(8,128)(2,1)S(1)} async-done(((bf16[8,32,8,128]{3,2,1,0:T(8,128)(2,1)}), bf16[8,32,8,128]{3,2,1,0:T(8,128)(2,1)S(1)}, u32[]{:S(2)}, u32[]{:S(2)}) %all-to-all-start.4) | async-done | bytes 524320 | tf_op jit(solution)/shard_map/all_to_all | solution.py:201
  111.9 0.9 final_step.1
  (36 shorter events, 0.2 us)
Async XLA Ops:
  25.8 3.1 %collective-permute-start.2 = (bf16[256,1024]{1,0:T(8,128)(2,1)S(1)}, bf16[256,1024]{1,0:T(8,128)(2,1)S(1)}, u32[]{:S(2)}, u32[]{:S(2)}) collective-permute-start(bf16[256,1024]{1,0:T(8,128)(2,1)S(1)} %bitcast.11), channel_id=1, source_target_pairs={{0,1},{1,0},{2,3},{3,2},{4,5},{5,4},{6,7},{7,6},{8,9},{9,8},{10,11... | collective-permute-start | bytes 1572872 | tf_op jit(solution)/shard_map/ppermute | solution.py:209
  25.8 13.0 %collective-permute-start = (bf16[128,1024]{1,0:T(8,128)(2,1)S(1)}, bf16[128,1024]{1,0:T(8,128)(2,1)S(1)}, u32[]{:S(2)}, u32[]{:S(2)}) collective-permute-start(bf16[128,1024]{1,0:T(8,128)(2,1)S(1)} %bitcast.19), channel_id=1, source_target_pairs={{0,96},{32,0},{64,32},{96,64},{1,97},{33,1},{65,33},{97,65},{2,98}... | collective-permute-start | bytes 786440 | tf_op jit(solution)/shard_map/ppermute | solution.py:213
  28.9 9.9 %collective-permute-start.1 = (bf16[128,1024]{1,0:T(8,128)(2,1)S(1)}, bf16[128,1024]{1,0:T(8,128)(2,1)S(1)}, u32[]{:S(2)}, u32[]{:S(2)}) collective-permute-start(bf16[128,1024]{1,0:T(8,128)(2,1)S(1)} %bitcast.18), channel_id=1, source_target_pairs={{0,32},{32,64},{64,96},{96,0},{1,33},{33,65},{65,97},{97,1},{2,34}... | collective-permute-start | bytes 786440 | tf_op jit(solution)/shard_map/ppermute | solution.py:213
  28.9 3.4 %copy-start = (bf16[128,32,1024]{2,1,0:T(8,128)(2,1)S(1)}, bf16[128,32,1024]{2,1,0:T(8,128)(2,1)}, u32[]{:S(2)}) copy-start(bf16[128,32,1024]{2,1,0:T(8,128)(2,1)} %tensor_ref.5) | copy-start | bytes 25165828
  38.8 4.8 %collective-permute-start.3 = (bf16[128,1024]{1,0:T(8,128)(2,1)S(1)}, bf16[128,1024]{1,0:T(8,128)(2,1)S(1)}, u32[]{:S(2)}, u32[]{:S(2)}) collective-permute-start(bf16[128,1024]{1,0:T(8,128)(2,1)S(1)} %collective-permute-done.refs_0_), channel_id=1, source_target_pairs={{0,1},{1,0},{2,3},{3,2},{4,5},{5,4},{6,7},{7,6},{8,9},{9,8},{10,11... | collective-permute-start | bytes 786440 | tf_op jit(solution)/shard_map/ppermute | solution.py:209
  39.1 4.5 %collective-permute-start.4 = (bf16[128,1024]{1,0:T(8,128)(2,1)S(1)}, bf16[128,1024]{1,0:T(8,128)(2,1)S(1)}, u32[]{:S(2)}, u32[]{:S(2)}) collective-permute-start(bf16[128,1024]{1,0:T(8,128)(2,1)S(1)} %collective-permute-done.1.refs_1_), channel_id=1, source_target_pairs={{0,1},{1,0},{2,3},{3,2},{4,5},{5,4},{6,7},{7,6},{8,9},{9,8},{10,11... | collective-permute-start | bytes 786440 | tf_op jit(solution)/shard_map/ppermute | solution.py:209
  39.4 8.5 %collective-permute-start.5 = (bf16[128,256]{1,0:T(8,128)(2,1)S(1)}, bf16[128,256]{1,0:T(8,128)(2,1)S(1)}, u32[]{:S(2)}, u32[]{:S(2)}) collective-permute-start(bf16[128,256]{1,0:T(8,128)(2,1)S(1)} %get-tuple-element.24), channel_id=1, source_target_pairs={{0,1},{1,0},{2,3},{3,2},{4,5},{5,4},{6,7},{7,6},{8,9},{9,8},{10,11... | collective-permute-start | bytes 196616 | tf_op jit(solution)/shard_map/ppermute | solution.py:209
  43.7 11.7 %copy-start.10 = (f32[128]{0:T(128)S(1)}, f32[128]{0:T(128)}, u32[]{:S(2)}) copy-start(f32[128]{0:T(128)} %param.12) | copy-start | bytes 1540
  43.7 31.5 %copy-start.2 = (bf16[128,32,256]{2,1,0:T(8,128)(2,1)S(1)}, bf16[128,32,256]{2,1,0:T(8,128)(2,1)}, u32[]{:S(2)}) copy-start(bf16[128,32,256]{2,1,0:T(8,128)(2,1)} %get-tuple-element.30.refs_0_) | copy-start | bytes 6291460
  47.6 1.3 %collective-permute-start.6 = (bf16[128,256]{1,0:T(8,128)(2,1)S(1)}, bf16[128,256]{1,0:T(8,128)(2,1)S(1)}, u32[]{:S(2)}, u32[]{:S(2)}) collective-permute-start(bf16[128,256]{1,0:T(8,128)(2,1)S(1)} %get-tuple-element.27), channel_id=1, source_target_pairs={{0,1},{1,0},{2,3},{3,2},{4,5},{5,4},{6,7},{7,6},{8,9},{9,8},{10,11... | collective-permute-start | bytes 196616 | tf_op jit(solution)/shard_map/ppermute | solution.py:209
  49.6 13.7 %all-to-all-start.1 = ((bf16[16,8,512]{2,1,0:T(8,128)(2,1)}), bf16[16,8,512]{2,1,0:T(8,128)(2,1)S(1)}, u32[]{:S(2)}, u32[]{:S(2)}) async-start(bf16[16,8,512]{2,1,0:T(8,128)(2,1)} %bitcast.6), calls=%async_computation.1 | async-start | bytes 262144 | tf_op jit(solution)/shard_map/all_to_all | solution.py:201
  75.1 3.4 %collective-permute-start.7 = (bf16[128,512]{1,0:T(8,128)(2,1)S(1)}, bf16[128,512]{1,0:T(8,128)(2,1)S(1)}, u32[]{:S(2)}, u32[]{:S(2)}) collective-permute-start(bf16[128,512]{1,0:T(8,128)(2,1)S(1)} %bitcast.13), channel_id=1, source_target_pairs={{0,1},{1,0},{2,3},{3,2},{4,5},{5,4},{6,7},{7,6},{8,9},{9,8},{10,11... | collective-permute-start | bytes 393224 | tf_op jit(solution)/shard_map/ppermute | solution.py:209
  75.2 1.6 %copy-start.3 = (bf16[128,32,256]{2,1,0:T(8,128)(2,1)S(1)}, bf16[128,32,256]{2,1,0:T(8,128)(2,1)}, u32[]{:S(2)}) copy-start(bf16[128,32,256]{2,1,0:T(8,128)(2,1)} %get-tuple-element.31.refs_1_) | copy-start | bytes 6291460
  76.8 1.7 %copy-start.1 = (bf16[128,32,256]{2,1,0:T(8,128)(2,1)S(1)}, bf16[128,32,256]{2,1,0:T(8,128)(2,1)}, u32[]{:S(2)}) copy-start(bf16[128,32,256]{2,1,0:T(8,128)(2,1)} %get-tuple-element.28.refs_0_) | copy-start | bytes 6291460
  76.8 2.2 %copy-start.4 = (bf16[128,32,256]{2,1,0:T(8,128)(2,1)S(1)}, bf16[128,32,256]{2,1,0:T(8,128)(2,1)}, u32[]{:S(2)}) copy-start(bf16[128,32,256]{2,1,0:T(8,128)(2,1)} %get-tuple-element.29.refs_1_) | copy-start | bytes 6291460
  79.0 7.2 %copy-start.11 = (s32[32]{0:T(128)S(1)}, s32[32]{0:T(128)}, u32[]{:S(2)}) copy-start(s32[32]{0:T(128)} %param.15) | copy-start | bytes 388
  79.0 21.9 %copy-start.5 = (f32[1024]{0:T(1024)S(1)}, f32[1024]{0:T(1024)}, u32[]{:S(2)}) copy-start(f32[1024]{0:T(1024)} %param.13) | copy-start | bytes 12292
  79.0 21.9 %copy-start.6 = (f32[32,1024]{1,0:T(8,128)S(1)}, f32[32,1024]{1,0:T(8,128)}, u32[]{:S(2)}) copy-start(f32[32,1024]{1,0:T(8,128)} %param.8) | copy-start | bytes 393220
  79.0 21.9 %copy-start.7 = (f32[32,1024]{1,0:T(8,128)S(1)}, f32[32,1024]{1,0:T(8,128)}, u32[]{:S(2)}) copy-start(f32[32,1024]{1,0:T(8,128)} %param.9) | copy-start | bytes 393220
  79.0 21.9 %copy-start.8 = (f32[1024]{0:T(1024)S(1)}, f32[1024]{0:T(1024)}, u32[]{:S(2)}) copy-start(f32[1024]{0:T(1024)} %param.11) | copy-start | bytes 12292
  79.0 21.9 %copy-start.9 = (s32[32]{0:T(128)S(1)}, s32[32]{0:T(128)}, u32[]{:S(2)}) copy-start(s32[32]{0:T(128)} %param.14) | copy-start | bytes 388
  81.4 12.5 %all-to-all-start.3 = ((bf16[32,8,128]{2,1,0:T(8,128)(2,1)}), bf16[32,8,128]{2,1,0:T(8,128)(2,1)S(1)}, u32[]{:S(2)}, u32[]{:S(2)}) async-start(bf16[32,8,128]{2,1,0:T(8,128)(2,1)} %bitcast.8), calls=%async_computation.3 | async-start | bytes 131072 | tf_op jit(solution)/shard_map/all_to_all | solution.py:201
  94.8 17.1 %all-to-all-start.4 = ((bf16[8,32,8,128]{3,2,1,0:T(8,128)(2,1)}), bf16[8,32,8,128]{3,2,1,0:T(8,128)(2,1)S(1)}, u32[]{:S(2)}, u32[]{:S(2)}) async-start(bf16[8,32,8,128]{3,2,1,0:T(8,128)(2,1)} %broadcast_in_dim.26), calls=%async_computation.4 | async-start | bytes 1048576 | tf_op jit(solution)/shard_map/all_to_all | solution.py:201

commit v6 on v5

--- a/solution.py
+++ b/solution.py
@@ -30,7 +30,7 @@
     return pltpu.with_memory_space_constraint(x, pltpu.VMEM)
 
 
-def inner_kernel(counts, slabs, row_ref, tensor_ref, *refs):
+def inner_kernel(counts, slabs, stream, row_ref, tensor_ref, *refs):
     n_in, blocks = sum(counts), len(counts)
     case_refs = refs[:n_in]
     inner_refs = refs[n_in : n_in + blocks]
@@ -50,7 +50,7 @@
 
     start = pl.multiple_of(row_ref[0] * rows, rows)
     columns = turned[pl.ds(start, rows), :].astype(F32)
-    tensor = tensor_ref[pl.ds(step * slabs, slabs)]
+    tensor = tensor_ref[...] if stream else tensor_ref[pl.ds(step * slabs, slabs)]
     inner = jnp.dot(
         tensor.reshape(slabs * rows, width), turned[...], preferred_element_type=F32
     ).reshape(slabs, rows, blocks * WIDE)
@@ -59,22 +59,25 @@
         piece = inner[:, :, span]
         inner_refs[b][...] = piece.astype(BF)
         part = jnp.sum(piece * columns[None, :, span], axis=1)
-        part_refs[b][...] = part.astype(part_refs[b].dtype)
-
-
-def inner_products(row, coupling, groups, part_types, slabs=32):
+        at = pl.ds(pl.multiple_of(step * slabs, slabs), slabs)
+        part_refs[b][at, :] = part.astype(part_refs[b].dtype)
+
+
+def inner_products(row, coupling, groups, part_types, slabs=32, stream=False):
     n_k, rows, width = coupling.shape
     counts = tuple(len(g) for g in groups)
     cases = [c for g in groups for c in g]
     blocks = len(groups)
+    placed = pltpu.with_memory_space_constraint(coupling, pltpu.HBM if stream else pltpu.VMEM)
     out = pl.pallas_call(
-        functools.partial(inner_kernel, counts, slabs),
+        functools.partial(inner_kernel, counts, slabs, stream),
         grid_spec=pltpu.PrefetchScalarGridSpec(
             num_scalar_prefetch=1,
             grid=(n_k // slabs,),
-            in_specs=[VMEM] * (1 + len(cases)),
+            in_specs=[pl.BlockSpec((slabs, rows, width), lambda k, r: (k, 0, 0)) if stream else VMEM]
+            + [VMEM] * len(cases),
             out_specs=[pl.BlockSpec((slabs, rows, WIDE), lambda k, r: (k, 0, 0))] * blocks
-            + [pl.BlockSpec((slabs, WIDE), lambda k, r: (k, 0))] * blocks,
+            + [VMEM] * blocks,
             scratch_shapes=[pltpu.VMEM((width, blocks * WIDE), BF)],
         ),
         out_shape=[pltpu.HBM((n_k, rows, WIDE), BF)] * blocks
@@ -84,7 +87,7 @@
         ),
         compiler_params=pltpu.CompilerParams(vmem_limit_bytes=20 << 20),
         name="inner_products",
-    )(row, in_vmem(coupling), *[in_vmem(c) for c in cases])
+    )(row, placed, *[in_vmem(c) for c in cases])
     return out[:blocks], out[blocks:]
 
 
@@ -232,28 +235,29 @@
     b0 = spread(piece, SAME, N_SAME).reshape(WIDE, width)
     b1 = [shift(b0[: WIDE // 2], -1), shift(b0[WIDE // 2 :], 1)]
     o0 = swap(b0)
-    (i0, j0), (p0, q0) = inner_products(row, coupling, [[b0], [o0]], [F32, BF])
-
-    b1, p0, q0 = after((b1, p0, q0))
+    (i0, j0), (p0, q0) = inner_products(row, coupling, [[b0], [o0]], [F32, BF], 16, True)
+
+    per = n_k // N_SAME
+    n_half = PARTS * WIDE
+    scale = lax.dynamic_slice_in_dim(airy_scale, same * per, per, 0)
+    b1, p0, q0, scale = after((b1, p0, q0, scale))
     o1 = [swap(b) for b in b1]
-    (i1,), (p1,) = inner_products(row, coupling, [b1], [F32])
+    (i1,), (p1,) = inner_products(row, coupling, [b1], [F32], 64)
 
     o1, p1 = after((o1, p1))
-    (j1,), (q1,) = inner_products(row, coupling, [o1], [BF])
+    (j1,), (q1,) = inner_products(row, coupling, [o1], [BF], 64)
 
     part = combine([p0, p1], [swap(q0), swap(q1)])
-    per = n_k // N_SAME
-    n_half = part.shape[1]
     shares = exchange(part.reshape(N_SAME, per, n_half), SAME)
-    scale = lax.dynamic_slice_in_dim(airy_scale, same * per, per, 0)
     summed = jnp.sum(shares.astype(F32), axis=0) / scale[:, None]
     airy_own = spread(summed.astype(BF), SAME, N_SAME).reshape(n_k, n_half)
     airy_other = swap(airy_own)
 
     force_own = forces(place, airy_own, [i0, i1])
     messages = forces(place, airy_other, [j0, j1], force_own)
+    messages, late = after((messages, (amplitudes, previous, damping, stiffness, strike_mode, strike_offset)))
+    amplitudes, previous, damping, stiffness, strike_mode, strike_offset = late
     arrived = exchange(messages.reshape(2 * N_SAME, 8, 128), ROW)
-    parts = spread(arrived, INPLANE, N_IN)
     airy = airy_output(place, airy_own, airy_other).reshape(2 * N_SAME * rows, n_k)
 
     offset = strike_offset.astype(F32)
@@ -263,6 +267,9 @@
     modes = jnp.arange(width, dtype=jnp.int32)
     excite = jnp.where(modes[None, :] == strike_mode[:, None], pulse[:, None], 0.0)
     base = 2.0 * amplitudes - (1.0 - damping) * previous - stiffness * amplitudes + excite
+
+    arrived, airy, base = after((arrived, airy, base))
+    parts = spread(arrived, INPLANE, N_IN)
     result = final_step(parts, base, damping[None, :])
     return (result, airy)
 

time: 113 us -> 112 us (level)
  blocking collectives: 35.9 us -> 66.8 us
  waiting for transfers between devices: 26 us -> 7.16 us
  starting transfers between devices: 20.8 us -> 8.95 us
  local copies, waits for them, and re-layouts: 7.41 us -> 2.18 us
  Pallas kernels: 21.6 us -> 24.9 us
    all_to_all x2 -> x4, blocking collectives: 35.9 us -> 66.8 us  [exchange(): return lax.all_to_all(x, axes, split_axis=0, concat_axis=0, tiled=True)]
    all_to_all x3 -> x1, waiting for transfers between devices: 25 us -> 6.18 us  [exchange(): return lax.all_to_all(x, axes, split_axis=0, concat_axis=0, tiled=True)]
    all_to_all x3 -> x1, starting transfers between devices: 16.6 us -> 4.74 us  [exchange(): return lax.all_to_all(x, axes, split_axis=0, concat_axis=0, tiled=True)]
    unnamed x24, local copies, waits for them, and re-layouts: 5.5 us -> 0.43 us
    pallas_call x3, Pallas kernels: 14.5 us -> 18.3 us  [inner_products(): pl.pallas_call(functools.partial(inner_kernel, counts, slabs, stream), gr...]
  transfers between devices with their start and end apart: 11 -> 9, of which waited for: 4 -> 2; matrix products, arithmetic and copies ran while one was open for 0% -> 1% of each run, Pallas kernels for 16% -> 19%
where the time goes in v6:
time: 112 us; the launch traced here: 111 us
  blocking collectives  66.8 us (60%)
  Pallas kernels  24.9 us (22%)
  starting transfers between devices  8.95 us (8%)
  waiting for transfers between devices  7.16 us (6%)
  local copies, waits for them, and re-layouts  2.18 us (2%)
    all_to_all x4, blocking collectives, exchange(): return lax.all_to_all(x, axes, split_axis=0, concat_axis=0, tiled=True)  66.8 us
    pallas_call x3, Pallas kernels, inner_products(): pl.pallas_call(functools.partial(inner_kernel, counts, slabs, stream), gr...  18.3 us
    all_to_all x1, waiting for transfers between devices, exchange(): return lax.all_to_all(x, axes, split_axis=0, concat_axis=0, tiled=True)  6.18 us
    all_to_all x1, starting transfers between devices, exchange(): return lax.all_to_all(x, axes, split_axis=0, concat_axis=0, tiled=True)  4.74 us
    pallas_call x2, Pallas kernels, forces(): pl.pallas_call(functools.partial(force_kernel, pair), in_specs=[pl.BlockS...  4.18 us
    ppermute x2, starting transfers between devices, shift(): return lax.ppermute(x, 'y', [(i, (i + by) % N_Y) for i in range(N_Y)])  3.09 us
  transfers between devices with their start and end apart: 9, of which 2 were waited for; matrix products, arithmetic and copies ran while one was open for 1% of the time, Pallas kernels for 19%

profile of v6, /device:TPU:2, one launch (start us, length us, event | category | flops | bytes accessed | tf_op | source)
XLA Modules:
  0.0 111.0 jit_solution(8686445987420147040)
XLA Ops:
  0.6 0.8 dynamic-slice_convert_fusion
  1.5 0.1 broadcast_in_dim.24
  1.6 24.2 %all_to_all.25 = bf16[16,16,1024]{2,1,0:T(8,128)(2,1)S(1)} all-to-all(bf16[16,16,1024]{2,1,0:T(8,128)(2,1)S(1)} %broadcast_in_dim.24), channel_id=1, replica_groups=mesh['xh'=2,'y'=4,'xl'=2,'z'=8,'c'=2] {'xl','z'}, dimensions={0} | all-to-all | bytes 1048576 | tf_op jit(solution)/shard_map/all_to_all | solution.py:204
  25.8 0.7 dynamic_slice.7
  26.5 3.1 %collective-permute-start = (bf16[128,1024]{1,0:T(8,128)(2,1)S(1)}, bf16[128,1024]{1,0:T(8,128)(2,1)S(1)}, u32[]{:S(2)}, u32[]{:S(2)}) collective-permute-start(bf16[128,1024]{1,0:T(8,128)(2,1)S(1)} %bitcast.22), channel_id=1, source_target_pairs={{0,96},{32,0},{64,32},{96,64},{1,97},{33,1},{65,33},{97,65},{2,98}... | collective-permute-start | bytes 786440 | tf_op jit(solution)/shard_map/ppermute | solution.py:216
  29.6 0.0 collective-permute-start.1
  29.6 10.6 %inner_products.3 = (bf16[128,32,256]{2,1,0:T(8,128)(2,1)}, bf16[128,32,256]{2,1,0:T(8,128)(2,1)}, f32[128,256]{1,0:T(8,128)S(1)}, bf16[128,256]{1,0:T(8,128)(2,1)S(1)}) custom-call(s32[1]{0:T(128)} %bitcast.4.row_ref, bf16[128,32,1024]{2,1,0:T(8,128)(2,1)} %tensor_ref.5, bf16[256,1024]{1,0:T(8,128)(2,1)S(1)} %bitcast.14, ...), custom_call_target="tpu_custom_call" | custom-call | flops 4294967296 | bytes 10485760 | tf_op jit(solution)/shard_map/inner_products/pallas_call | solution.py:72
  40.3 0.0 collective-permute-done.refs_0_
  40.3 0.0 collective-permute-done.1.refs_1_
  40.3 0.3 collective-permute-start.3
  40.6 0.3 collective-permute-start.4
  40.9 0.2 collective-permute-start.5
  41.1 3.9 %inner_products.4 = (bf16[128,32,256]{2,1,0:T(8,128)(2,1)}, f32[128,256]{1,0:T(8,128)S(1)}) custom-call(s32[1]{0:T(128)} %bitcast.4.row_ref, bf16[128,32,1024]{2,1,0:T(8,128)(2,1)S(1)} %bitcast.12, bf16[128,1024]{1,0:T(8,128)(2,1)S(1)} %collective-permute-done.refs_0_, bf16[128,1024]{1,0:T(8,128)(2,1)S(1)} %collective-permute-done.1.refs_1_), custom_call_target="tpu_custom_call" | custom-call | flops 2147483648 | bytes 10485760 | tf_op jit(solution)/shard_map/inner_products/pallas_call | solution.py:72
  45.0 3.8 %inner_products.5 = (bf16[128,32,256]{2,1,0:T(8,128)(2,1)}, bf16[128,256]{1,0:T(8,128)(2,1)S(1)}) custom-call(s32[1]{0:T(128)} %bitcast.4.row_ref, bf16[128,32,1024]{2,1,0:T(8,128)(2,1)S(1)} %bitcast.12, bf16[128,1024]{1,0:T(8,128)(2,1)S(1)} %collective-permute-done.3.refs_0_, bf16[128,1024]{1,0:T(8,128)(2,1)S(1)} %collective-permute-done.4.refs_1_), custom_call_target="tpu_custom_call" | custom-call | flops 2147483648 | bytes 10485760 | tf_op jit(solution)/shard_map/inner_products/pallas_call | solution.py:72
  48.8 0.3 collective-permute-start.6
  49.1 1.0 collective-permute-done.6.refs_3_
  50.1 13.5 %all_to_all.26 = bf16[16,8,512]{2,1,0:T(8,128)(2,1)S(1)} all-to-all(bf16[16,8,512]{2,1,0:T(8,128)(2,1)S(1)} %bitcast.18), channel_id=1, replica_groups=mesh['xh'=2,'y'=4,'xl'=2,'z'=8,'c'=2] {'xl','z'}, dimensions={0} | all-to-all | bytes 262144 | tf_op jit(solution)/shard_map/all_to_all | solution.py:204
  63.7 0.1 divide_convert_fusion
  63.8 11.7 %all_to_all.27 = bf16[16,8,512]{2,1,0:T(8,128)(2,1)S(1)} all-to-all(bf16[16,8,512]{2,1,0:T(8,128)(2,1)S(1)} %broadcast_in_dim.25), channel_id=1, replica_groups=mesh['xh'=2,'y'=4,'xl'=2,'z'=8,'c'=2] {'xl','z'}, dimensions={0} | all-to-all | bytes 262144 | tf_op jit(solution)/shard_map/all_to_all | solution.py:204
  75.4 0.1 pad_add_fusion.place_ref
  75.5 1.8 %forces.2.refs_2_ = bf16[16,8,128]{2,1,0:T(8,128)(2,1)S(1)} custom-call(s32[2]{0:T(128)S(1)} %pad_add_fusion.place_ref, bf16[128,512]{1,0:T(8,128)(2,1)S(1)} %bitcast.16, bf16[128,32,256]{2,1,0:T(8,128)(2,1)S(1)} %copy-done.1, bf16[128,32,256]{2,1,0:T(8,128)(2,1)S(1)} %copy-done.2), custom_call_target="tpu_custom_call" | custom-call | flops 4194304 | bytes 4194304 | tf_op jit(solution)/shard_map/forces/pallas_call | solution.py:142
  77.4 0.4 copy-done.3
  77.8 0.0 copy-start.7
  77.8 0.0 copy-start.8
  77.8 2.4 %forces.3 = bf16[16,2,8,128]{3,2,1,0:T(8,128)(2,1)} custom-call(s32[2]{0:T(128)S(1)} %pad_add_fusion.place_ref, bf16[128,512]{1,0:T(8,128)(2,1)S(1)} %collective-permute-done.7.airy_ref.theirs_ref, bf16[128,32,256]{2,1,0:T(8,128)(2,1)S(1)} %copy-done, bf16[128,32,256]{2,1,0:T(8,128)(2,1)S(1)} %copy-done.3, bf16[16,8,128]{2,1,0:T(8,128)(2,1)S(1)} %forces.2.refs_2_), custom_call_target="tpu_custom_call" | custom-call | flops 4194304 | bytes 4194304 | tf_op jit(solution)/shard_map/forces/pallas_call | solution.py:142
  80.2 4.7 %all-to-all-start.3 = ((bf16[32,8,128]{2,1,0:T(8,128)(2,1)}), bf16[32,8,128]{2,1,0:T(8,128)(2,1)S(1)}, u32[]{:S(2)}, u32[]{:S(2)}) async-start(bf16[32,8,128]{2,1,0:T(8,128)(2,1)} %bitcast.8), calls=%async_computation.3 | async-start | bytes 131072 | tf_op jit(solution)/shard_map/all_to_all | solution.py:204
  85.0 1.5 %airy_output.1 = f32[16,2,2,16,128]{4,3,2,1,0:T(8,128)} custom-call(s32[2]{0:T(128)S(1)} %pad_add_fusion.place_ref, bf16[128,512]{1,0:T(8,128)(2,1)S(1)} %bitcast.17, bf16[128,512]{1,0:T(8,128)(2,1)S(1)} %collective-permute-done.7.airy_ref.theirs_ref), custom_call_target="tpu_custom_call" | custom-call | flops 1048576 | bytes 1048576 | tf_op jit(solution)/shard_map/airy_output/pallas_call | solution.py:167
  86.5 0.1 select_add_fusion.base_ref
  86.6 6.2 %all-to-all-done.3 = bf16[32,8,128]{2,1,0:T(8,128)(2,1)S(1)} async-done(((bf16[32,8,128]{2,1,0:T(8,128)(2,1)}), bf16[32,8,128]{2,1,0:T(8,128)(2,1)S(1)}, u32[]{:S(2)}, u32[]{:S(2)}) %all-to-all-start.3) | async-done | bytes 65568 | tf_op jit(solution)/shard_map/all_to_all | solution.py:204
  92.7 0.1 broadcast_in_dim.48
  92.8 17.4 %all_to_all.28.parts_ref = bf16[8,32,8,128]{3,2,1,0:T(8,128)(2,1)S(1)} all-to-all(bf16[8,32,8,128]{3,2,1,0:T(8,128)(2,1)S(1)} %broadcast_in_dim.48), channel_id=1, replica_groups=mesh['xh'=2,'y'=4,'xl'=2,'z'=8,'c'=2] {'xh','y'}, dimensions={0} | all-to-all | bytes 1048576 | tf_op jit(solution)/shard_map/all_to_all | solution.py:204
  110.2 0.9 final_step.1
  (35 shorter events, 0.2 us)
Async XLA Ops:
  25.8 3.9 %collective-permute-start.2 = (bf16[256,1024]{1,0:T(8,128)(2,1)S(1)}, bf16[256,1024]{1,0:T(8,128)(2,1)S(1)}, u32[]{:S(2)}, u32[]{:S(2)}) collective-permute-start(bf16[256,1024]{1,0:T(8,128)(2,1)S(1)} %bitcast.13), channel_id=1, source_target_pairs={{0,1},{1,0},{2,3},{3,2},{4,5},{5,4},{6,7},{7,6},{8,9},{9,8},{10,11... | collective-permute-start | bytes 1572872 | tf_op jit(solution)/shard_map/ppermute | solution.py:212
  26.5 14.6 %slice-start = ((s8[8388608]{0:T(1024)(128)(4,1)}), s8[4194304]{0:T(1024)(128)(4,1)S(1)}, s32[]{:S(2)}) async-start(s8[8388608]{0:T(1024)(128)(4,1)} %bitcast.11), calls=%async_computation.5 | async-start | bytes 8388608
  26.5 13.7 %collective-permute-start = (bf16[128,1024]{1,0:T(8,128)(2,1)S(1)}, bf16[128,1024]{1,0:T(8,128)(2,1)S(1)}, u32[]{:S(2)}, u32[]{:S(2)}) collective-permute-start(bf16[128,1024]{1,0:T(8,128)(2,1)S(1)} %bitcast.22), channel_id=1, source_target_pairs={{0,96},{32,0},{64,32},{96,64},{1,97},{33,1},{65,33},{97,65},{2,98}... | collective-permute-start | bytes 786440 | tf_op jit(solution)/shard_map/ppermute | solution.py:216
  29.6 10.7 %collective-permute-start.1 = (bf16[128,1024]{1,0:T(8,128)(2,1)S(1)}, bf16[128,1024]{1,0:T(8,128)(2,1)S(1)}, u32[]{:S(2)}, u32[]{:S(2)}) collective-permute-start(bf16[128,1024]{1,0:T(8,128)(2,1)S(1)} %bitcast.21), channel_id=1, source_target_pairs={{0,32},{32,64},{64,96},{96,0},{1,33},{33,65},{65,97},{97,1},{2,34}... | collective-permute-start | bytes 786440 | tf_op jit(solution)/shard_map/ppermute | solution.py:216
  29.6 11.5 %slice-start.1 = ((s8[8388608]{0:T(1024)(128)(4,1)}), s8[4194304]{0:T(1024)(128)(4,1)S(1)}, s32[]{:S(2)}) async-start(s8[8388608]{0:T(1024)(128)(4,1)} %bitcast.11), calls=%async_computation.6 | async-start | bytes 8388608
  40.3 4.7 %collective-permute-start.3 = (bf16[128,1024]{1,0:T(8,128)(2,1)S(1)}, bf16[128,1024]{1,0:T(8,128)(2,1)S(1)}, u32[]{:S(2)}, u32[]{:S(2)}) collective-permute-start(bf16[128,1024]{1,0:T(8,128)(2,1)S(1)} %collective-permute-done.refs_0_), channel_id=1, source_target_pairs={{0,1},{1,0},{2,3},{3,2},{4,5},{5,4},{6,7},{7,6},{8,9},{9,8},{10,11... | collective-permute-start | bytes 786440 | tf_op jit(solution)/shard_map/ppermute | solution.py:212
  40.6 4.4 %collective-permute-start.4 = (bf16[128,1024]{1,0:T(8,128)(2,1)S(1)}, bf16[128,1024]{1,0:T(8,128)(2,1)S(1)}, u32[]{:S(2)}, u32[]{:S(2)}) collective-permute-start(bf16[128,1024]{1,0:T(8,128)(2,1)S(1)} %collective-permute-done.1.refs_1_), channel_id=1, source_target_pairs={{0,1},{1,0},{2,3},{3,2},{4,5},{5,4},{6,7},{7,6},{8,9},{9,8},{10,11... | collective-permute-start | bytes 786440 | tf_op jit(solution)/shard_map/ppermute | solution.py:212
  40.9 8.2 %collective-permute-start.5 = (bf16[128,256]{1,0:T(8,128)(2,1)S(1)}, bf16[128,256]{1,0:T(8,128)(2,1)S(1)}, u32[]{:S(2)}, u32[]{:S(2)}) collective-permute-start(bf16[128,256]{1,0:T(8,128)(2,1)S(1)} %get-tuple-element.35), channel_id=1, source_target_pairs={{0,1},{1,0},{2,3},{3,2},{4,5},{5,4},{6,7},{7,6},{8,9},{9,8},{10,11... | collective-permute-start | bytes 196616 | tf_op jit(solution)/shard_map/ppermute | solution.py:212
  45.0 30.5 %copy-start.1 = (bf16[128,32,256]{2,1,0:T(8,128)(2,1)S(1)}, bf16[128,32,256]{2,1,0:T(8,128)(2,1)}, u32[]{:S(2)}) copy-start(bf16[128,32,256]{2,1,0:T(8,128)(2,1)} %get-tuple-element.42.refs_0_) | copy-start | bytes 6291460
  45.0 30.5 %copy-start.2 = (bf16[128,32,256]{2,1,0:T(8,128)(2,1)S(1)}, bf16[128,32,256]{2,1,0:T(8,128)(2,1)}, u32[]{:S(2)}) copy-start(bf16[128,32,256]{2,1,0:T(8,128)(2,1)} %get-tuple-element.43.refs_1_) | copy-start | bytes 6291460
  48.8 1.3 %collective-permute-start.6 = (bf16[128,256]{1,0:T(8,128)(2,1)S(1)}, bf16[128,256]{1,0:T(8,128)(2,1)S(1)}, u32[]{:S(2)}, u32[]{:S(2)}) collective-permute-start(bf16[128,256]{1,0:T(8,128)(2,1)S(1)} %get-tuple-element.38), channel_id=1, source_target_pairs={{0,1},{1,0},{2,3},{3,2},{4,5},{5,4},{6,7},{7,6},{8,9},{9,8},{10,11... | collective-permute-start | bytes 196616 | tf_op jit(solution)/shard_map/ppermute | solution.py:212
  75.4 1.9 %collective-permute-start.7 = (bf16[128,512]{1,0:T(8,128)(2,1)S(1)}, bf16[128,512]{1,0:T(8,128)(2,1)S(1)}, u32[]{:S(2)}, u32[]{:S(2)}) collective-permute-start(bf16[128,512]{1,0:T(8,128)(2,1)S(1)} %bitcast.15), channel_id=1, source_target_pairs={{0,1},{1,0},{2,3},{3,2},{4,5},{5,4},{6,7},{7,6},{8,9},{9,8},{10,11... | collective-permute-start | bytes 393224 | tf_op jit(solution)/shard_map/ppermute | solution.py:212
  75.5 1.8 %copy-start = (bf16[128,32,256]{2,1,0:T(8,128)(2,1)S(1)}, bf16[128,32,256]{2,1,0:T(8,128)(2,1)}, u32[]{:S(2)}) copy-start(bf16[128,32,256]{2,1,0:T(8,128)(2,1)} %get-tuple-element.40.refs_0_) | copy-start | bytes 6291460
  75.5 2.2 %copy-start.3 = (bf16[128,32,256]{2,1,0:T(8,128)(2,1)S(1)}, bf16[128,32,256]{2,1,0:T(8,128)(2,1)}, u32[]{:S(2)}) copy-start(bf16[128,32,256]{2,1,0:T(8,128)(2,1)} %get-tuple-element.41.refs_1_) | copy-start | bytes 6291460
  77.8 2.4 %copy-start.9 = (s32[32]{0:T(128)S(1)}, s32[32]{0:T(128)}, u32[]{:S(2)}) copy-start(s32[32]{0:T(128)} %param.15) | copy-start | bytes 388
  77.8 2.5 %copy-start.4 = (f32[1024]{0:T(1024)S(1)}, f32[1024]{0:T(1024)}, u32[]{:S(2)}) copy-start(f32[1024]{0:T(1024)} %param.13) | copy-start | bytes 12292
  77.8 8.7 %copy-start.5 = (f32[32,1024]{1,0:T(8,128)S(1)}, f32[32,1024]{1,0:T(8,128)}, u32[]{:S(2)}) copy-start(f32[32,1024]{1,0:T(8,128)} %param.8) | copy-start | bytes 393220
  77.8 8.7 %copy-start.6 = (f32[32,1024]{1,0:T(8,128)S(1)}, f32[32,1024]{1,0:T(8,128)}, u32[]{:S(2)}) copy-start(f32[32,1024]{1,0:T(8,128)} %param.9) | copy-start | bytes 393220
  77.8 8.7 %copy-start.7 = (f32[1024]{0:T(1024)S(1)}, f32[1024]{0:T(1024)}, u32[]{:S(2)}) copy-start(f32[1024]{0:T(1024)} %param.11) | copy-start | bytes 12292
  77.8 8.7 %copy-start.8 = (s32[32]{0:T(128)S(1)}, s32[32]{0:T(128)}, u32[]{:S(2)}) copy-start(s32[32]{0:T(128)} %param.14) | copy-start | bytes 388
  80.2 12.5 %all-to-all-start.3 = ((bf16[32,8,128]{2,1,0:T(8,128)(2,1)}), bf16[32,8,128]{2,1,0:T(8,128)(2,1)S(1)}, u32[]{:S(2)}, u32[]{:S(2)}) async-start(bf16[32,8,128]{2,1,0:T(8,128)(2,1)} %bitcast.8), calls=%async_computation.3 | async-start | bytes 131072 | tf_op jit(solution)/shard_map/all_to_all | solution.py:204

commit v7 on v6

--- a/solution.py
+++ b/solution.py
@@ -80,7 +80,7 @@
             + [VMEM] * blocks,
             scratch_shapes=[pltpu.VMEM((width, blocks * WIDE), BF)],
         ),
-        out_shape=[pltpu.HBM((n_k, rows, WIDE), BF)] * blocks
+        out_shape=[jax.ShapeDtypeStruct((n_k, rows, WIDE), BF)] * blocks
         + [jax.ShapeDtypeStruct((n_k, WIDE), t) for t in part_types],
         cost_estimate=pl.CostEstimate(
             flops=2 * n_k * rows * width * blocks * WIDE, bytes_accessed=10 << 20, transcendentals=0
@@ -231,16 +231,17 @@
     half = y % PARTS
     place = jnp.stack([half, core])
 
+    per = n_k // N_SAME
+    n_half = PARTS * WIDE
     piece = lax.dynamic_slice_in_dim(amplitudes, half * FEW, FEW, 0).astype(BF)
+    scale = lax.dynamic_slice_in_dim(airy_scale, same * per, per, 0)
+    piece, scale, row, place = after((piece, scale, row, place))
     b0 = spread(piece, SAME, N_SAME).reshape(WIDE, width)
     b1 = [shift(b0[: WIDE // 2], -1), shift(b0[WIDE // 2 :], 1)]
     o0 = swap(b0)
-    (i0, j0), (p0, q0) = inner_products(row, coupling, [[b0], [o0]], [F32, BF], 16, True)
-
-    per = n_k // N_SAME
-    n_half = PARTS * WIDE
-    scale = lax.dynamic_slice_in_dim(airy_scale, same * per, per, 0)
-    b1, p0, q0, scale = after((b1, p0, q0, scale))
+    (i0, j0), (p0, q0) = inner_products(row, coupling, [[b0], [o0]], [F32, BF])
+
+    b1, p0, q0 = after((b1, p0, q0))
     o1 = [swap(b) for b in b1]
     (i1,), (p1,) = inner_products(row, coupling, [b1], [F32], 64)
 

time: 112 us -> 108 us (0.964)
  Pallas kernels: 24.9 us -> 17.8 us
  local copies, waits for them, and re-layouts: 2.18 us -> 5.16 us
    pallas_call x3, Pallas kernels: 18.3 us -> 11.2 us  [inner_products(): pl.pallas_call(functools.partial(inner_kernel, counts, slabs, stream), gr...]
    unnamed x24 -> x14, local copies, waits for them, and re-layouts: 0.43 us -> 3.42 us
  transfers between devices with their start and end apart: 9 -> 9, of which waited for: 2 -> 3; matrix products, arithmetic and copies ran while one was open for 1% -> 0% of each run, Pallas kernels for 19% -> 14%
where the time goes in v7:
time: 108 us; the launch traced here: 107 us
  blocking collectives  66.3 us (61%)
  Pallas kernels  17.8 us (16%)
  starting transfers between devices  8.95 us (8%)
  waiting for transfers between devices  7.76 us (7%)
  local copies, waits for them, and re-layouts  5.16 us (5%)
    all_to_all x4, blocking collectives, exchange(): return lax.all_to_all(x, axes, split_axis=0, concat_axis=0, tiled=True)  66.3 us
    pallas_call x3, Pallas kernels, inner_products(): pl.pallas_call(functools.partial(inner_kernel, counts, slabs, stream), gr...  11.2 us
    all_to_all x1, waiting for transfers between devices, exchange(): return lax.all_to_all(x, axes, split_axis=0, concat_axis=0, tiled=True)  6.18 us
    all_to_all x1, starting transfers between devices, exchange(): return lax.all_to_all(x, axes, split_axis=0, concat_axis=0, tiled=True)  4.74 us
    pallas_call x2, Pallas kernels, forces(): pl.pallas_call(functools.partial(force_kernel, pair), in_specs=[pl.BlockS...  4.24 us
    unnamed x14, local copies, waits for them, and re-layouts  3.42 us
    ppermute x2, starting transfers between devices, shift(): return lax.ppermute(x, 'y', [(i, (i + by) % N_Y) for i in range(N_Y)])  3.09 us
  transfers between devices with their start and end apart: 9, of which 3 were waited for; matrix products, arithmetic and copies ran while one was open for 0% of the time, Pallas kernels for 14%

profile of v7, /device:TPU:2, one launch (start us, length us, event | category | flops | bytes accessed | tf_op | source)
XLA Modules:
  0.0 107.1 jit_solution(8858277257536510363)
XLA Ops:
  0.7 0.1 pad_add_fusion.place_ref
  0.7 0.7 dynamic_slice.7
  1.5 0.8 dynamic-slice_convert_fusion
  2.3 0.1 broadcast_in_dim.24
  2.4 24.2 %all_to_all.25 = bf16[16,16,1024]{2,1,0:T(8,128)(2,1)S(1)} all-to-all(bf16[16,16,1024]{2,1,0:T(8,128)(2,1)S(1)} %broadcast_in_dim.24), channel_id=1, replica_groups=mesh['xh'=2,'y'=4,'xl'=2,'z'=8,'c'=2] {'xl','z'}, dimensions={0} | all-to-all | bytes 1048576 | tf_op jit(solution)/shard_map/all_to_all | solution.py:204
  26.6 3.1 %collective-permute-start = (bf16[128,1024]{1,0:T(8,128)(2,1)S(1)}, bf16[128,1024]{1,0:T(8,128)(2,1)S(1)}, u32[]{:S(2)}, u32[]{:S(2)}) collective-permute-start(bf16[128,1024]{1,0:T(8,128)(2,1)S(1)} %bitcast.20), channel_id=1, source_target_pairs={{0,96},{32,0},{64,32},{96,64},{1,97},{33,1},{65,33},{97,65},{2,98}... | collective-permute-start | bytes 786440 | tf_op jit(solution)/shard_map/ppermute | solution.py:216
  29.7 3.4 %copy-done = bf16[128,32,1024]{2,1,0:T(8,128)(2,1)S(1)} copy-done((bf16[128,32,1024]{2,1,0:T(8,128)(2,1)S(1)}, bf16[128,32,1024]{2,1,0:T(8,128)(2,1)}, u32[]{:S(2)}) %copy-start) | copy-done | bytes 8388632
  33.1 5.6 %inner_products.3 = (bf16[128,32,256]{2,1,0:T(8,128)(2,1)S(1)}, bf16[128,32,256]{2,1,0:T(8,128)(2,1)S(1)}, f32[128,256]{1,0:T(8,128)S(1)}, bf16[128,256]{1,0:T(8,128)(2,1)S(1)}) custom-call(s32[1]{0:T(128)} %bitcast.row_ref, bf16[128,32,1024]{2,1,0:T(8,128)(2,1)S(1)} %copy-done, bf16[256,1024]{1,0:T(8,128)(2,1)S(1)} %bitcast.12, ...), custom_call_target="tpu_custom_call" | custom-call | flops 4294967296 | bytes 10485760 | tf_op jit(solution)/shard_map/inner_products/pallas_call | solution.py:72
  38.7 0.7 collective-permute-done.1.refs_1_
  39.4 0.5 collective-permute-start.4
  39.9 2.8 %inner_products.4 = (bf16[128,32,256]{2,1,0:T(8,128)(2,1)S(1)}, f32[128,256]{1,0:T(8,128)S(1)}) custom-call(s32[1]{0:T(128)} %bitcast.row_ref, bf16[128,32,1024]{2,1,0:T(8,128)(2,1)S(1)} %copy-done, bf16[128,1024]{1,0:T(8,128)(2,1)S(1)} %collective-permute-done.refs_0_, bf16[128,1024]{1,0:T(8,128)(2,1)S(1)} %collective-permute-done.1.refs_1_), custom_call_target="tpu_custom_call" | custom-call | flops 2147483648 | bytes 10485760 | tf_op jit(solution)/shard_map/inner_products/pallas_call | solution.py:72
  42.7 2.9 %inner_products.5 = (bf16[128,32,256]{2,1,0:T(8,128)(2,1)S(1)}, bf16[128,256]{1,0:T(8,128)(2,1)S(1)}) custom-call(s32[1]{0:T(128)} %bitcast.row_ref, bf16[128,32,1024]{2,1,0:T(8,128)(2,1)S(1)} %copy-done, bf16[128,1024]{1,0:T(8,128)(2,1)S(1)} %collective-permute-done.3.refs_0_, bf16[128,1024]{1,0:T(8,128)(2,1)S(1)} %collective-permute-done.4.refs_1_), custom_call_target="tpu_custom_call" | custom-call | flops 2147483648 | bytes 10485760 | tf_op jit(solution)/shard_map/inner_products/pallas_call | solution.py:72
  45.6 0.6 collective-permute-start.6
  46.2 0.9 collective-permute-done.6.refs_3_
  47.1 13.6 %all_to_all.26 = bf16[16,8,512]{2,1,0:T(8,128)(2,1)S(1)} all-to-all(bf16[16,8,512]{2,1,0:T(8,128)(2,1)S(1)} %bitcast.16), channel_id=1, replica_groups=mesh['xh'=2,'y'=4,'xl'=2,'z'=8,'c'=2] {'xl','z'}, dimensions={0} | all-to-all | bytes 262144 | tf_op jit(solution)/shard_map/all_to_all | solution.py:204
  60.7 0.1 divide_convert_fusion
  60.8 11.7 %all_to_all.27 = bf16[16,8,512]{2,1,0:T(8,128)(2,1)S(1)} all-to-all(bf16[16,8,512]{2,1,0:T(8,128)(2,1)S(1)} %broadcast_in_dim.25), channel_id=1, replica_groups=mesh['xh'=2,'y'=4,'xl'=2,'z'=8,'c'=2] {'xl','z'}, dimensions={0} | all-to-all | bytes 262144 | tf_op jit(solution)/shard_map/all_to_all | solution.py:204
  72.5 1.8 %forces.2.refs_2_ = bf16[16,8,128]{2,1,0:T(8,128)(2,1)S(1)} custom-call(s32[2]{0:T(128)S(1)} %pad_add_fusion.place_ref, bf16[128,512]{1,0:T(8,128)(2,1)S(1)} %bitcast.14, bf16[128,32,256]{2,1,0:T(8,128)(2,1)S(1)} %get-tuple-element.48.refs_0_, bf16[128,32,256]{2,1,0:T(8,128)(2,1)S(1)} %get-tuple-element.49.refs_1_), custom_call_target="tpu_custom_call" | custom-call | flops 4194304 | bytes 4194304 | tf_op jit(solution)/shard_map/forces/pallas_call | solution.py:142
  74.3 0.0 copy-start.6
  74.3 0.0 copy-start.1
  74.3 0.0 copy-start.2
  74.3 0.0 copy-start.3
  74.4 0.0 copy-start.4
  74.4 0.0 copy-start.5
  74.4 2.4 %forces.3 = bf16[16,2,8,128]{3,2,1,0:T(8,128)(2,1)} custom-call(s32[2]{0:T(128)S(1)} %pad_add_fusion.place_ref, bf16[128,512]{1,0:T(8,128)(2,1)S(1)} %collective-permute-done.7.airy_ref.theirs_ref, bf16[128,32,256]{2,1,0:T(8,128)(2,1)S(1)} %get-tuple-element.46.refs_0_, bf16[128,32,256]{2,1,0:T(8,128)(2,1)S(1)} %get-tuple-element.47.refs_1_, ...), custom_call_target="tpu_custom_call" | custom-call | flops 4194304 | bytes 4194304 | tf_op jit(solution)/shard_map/forces/pallas_call | solution.py:142
  76.9 4.7 %all-to-all-start.3 = ((bf16[32,8,128]{2,1,0:T(8,128)(2,1)}), bf16[32,8,128]{2,1,0:T(8,128)(2,1)S(1)}, u32[]{:S(2)}, u32[]{:S(2)}) async-start(bf16[32,8,128]{2,1,0:T(8,128)(2,1)} %bitcast.8), calls=%async_computation.3 | async-start | bytes 131072 | tf_op jit(solution)/shard_map/all_to_all | solution.py:204
  81.6 1.5 %airy_output.1 = f32[16,2,2,16,128]{4,3,2,1,0:T(8,128)} custom-call(s32[2]{0:T(128)S(1)} %pad_add_fusion.place_ref, bf16[128,512]{1,0:T(8,128)(2,1)S(1)} %bitcast.15, bf16[128,512]{1,0:T(8,128)(2,1)S(1)} %collective-permute-done.7.airy_ref.theirs_ref), custom_call_target="tpu_custom_call" | custom-call | flops 1048576 | bytes 1048576 | tf_op jit(solution)/shard_map/airy_output/pallas_call | solution.py:167
  83.1 0.1 select_add_fusion.base_ref
  83.2 6.2 %all-to-all-done.3 = bf16[32,8,128]{2,1,0:T(8,128)(2,1)S(1)} async-done(((bf16[32,8,128]{2,1,0:T(8,128)(2,1)}), bf16[32,8,128]{2,1,0:T(8,128)(2,1)S(1)}, u32[]{:S(2)}, u32[]{:S(2)}) %all-to-all-start.3) | async-done | bytes 65568 | tf_op jit(solution)/shard_map/all_to_all | solution.py:204
  89.4 0.1 broadcast_in_dim.48
  89.5 16.8 %all_to_all.28.parts_ref = bf16[8,32,8,128]{3,2,1,0:T(8,128)(2,1)S(1)} all-to-all(bf16[8,32,8,128]{3,2,1,0:T(8,128)(2,1)S(1)} %broadcast_in_dim.48), channel_id=1, replica_groups=mesh['xh'=2,'y'=4,'xl'=2,'z'=8,'c'=2] {'xh','y'}, dimensions={0} | all-to-all | bytes 1048576 | tf_op jit(solution)/shard_map/all_to_all | solution.py:204
  106.3 0.9 final_step.1
  (24 shorter events, 0.2 us)
Async XLA Ops:
  26.6 3.1 %collective-permute-start.2 = (bf16[256,1024]{1,0:T(8,128)(2,1)S(1)}, bf16[256,1024]{1,0:T(8,128)(2,1)S(1)}, u32[]{:S(2)}, u32[]{:S(2)}) collective-permute-start(bf16[256,1024]{1,0:T(8,128)(2,1)S(1)} %bitcast.11), channel_id=1, source_target_pairs={{0,1},{1,0},{2,3},{3,2},{4,5},{5,4},{6,7},{7,6},{8,9},{9,8},{10,11... | collective-permute-start | bytes 1572872 | tf_op jit(solution)/shard_map/ppermute | solution.py:212
  26.6 12.1 %collective-permute-start = (bf16[128,1024]{1,0:T(8,128)(2,1)S(1)}, bf16[128,1024]{1,0:T(8,128)(2,1)S(1)}, u32[]{:S(2)}, u32[]{:S(2)}) collective-permute-start(bf16[128,1024]{1,0:T(8,128)(2,1)S(1)} %bitcast.20), channel_id=1, source_target_pairs={{0,96},{32,0},{64,32},{96,64},{1,97},{33,1},{65,33},{97,65},{2,98}... | collective-permute-start | bytes 786440 | tf_op jit(solution)/shard_map/ppermute | solution.py:216
  29.7 9.6 %collective-permute-start.1 = (bf16[128,1024]{1,0:T(8,128)(2,1)S(1)}, bf16[128,1024]{1,0:T(8,128)(2,1)S(1)}, u32[]{:S(2)}, u32[]{:S(2)}) collective-permute-start(bf16[128,1024]{1,0:T(8,128)(2,1)S(1)} %bitcast.19), channel_id=1, source_target_pairs={{0,32},{32,64},{64,96},{96,0},{1,33},{33,65},{65,97},{97,1},{2,34}... | collective-permute-start | bytes 786440 | tf_op jit(solution)/shard_map/ppermute | solution.py:216
  29.7 3.4 %copy-start = (bf16[128,32,1024]{2,1,0:T(8,128)(2,1)S(1)}, bf16[128,32,1024]{2,1,0:T(8,128)(2,1)}, u32[]{:S(2)}) copy-start(bf16[128,32,1024]{2,1,0:T(8,128)(2,1)} %tensor_ref.5) | copy-start | bytes 25165828
  39.4 3.3 %collective-permute-start.3 = (bf16[128,1024]{1,0:T(8,128)(2,1)S(1)}, bf16[128,1024]{1,0:T(8,128)(2,1)S(1)}, u32[]{:S(2)}, u32[]{:S(2)}) collective-permute-start(bf16[128,1024]{1,0:T(8,128)(2,1)S(1)} %collective-permute-done.refs_0_), channel_id=1, source_target_pairs={{0,1},{1,0},{2,3},{3,2},{4,5},{5,4},{6,7},{7,6},{8,9},{9,8},{10,11... | collective-permute-start | bytes 786440 | tf_op jit(solution)/shard_map/ppermute | solution.py:212
  39.4 3.3 %collective-permute-start.4 = (bf16[128,1024]{1,0:T(8,128)(2,1)S(1)}, bf16[128,1024]{1,0:T(8,128)(2,1)S(1)}, u32[]{:S(2)}, u32[]{:S(2)}) collective-permute-start(bf16[128,1024]{1,0:T(8,128)(2,1)S(1)} %collective-permute-done.1.refs_1_), channel_id=1, source_target_pairs={{0,1},{1,0},{2,3},{3,2},{4,5},{5,4},{6,7},{7,6},{8,9},{9,8},{10,11... | collective-permute-start | bytes 786440 | tf_op jit(solution)/shard_map/ppermute | solution.py:212
  39.9 6.3 %collective-permute-start.5 = (bf16[128,256]{1,0:T(8,128)(2,1)S(1)}, bf16[128,256]{1,0:T(8,128)(2,1)S(1)}, u32[]{:S(2)}, u32[]{:S(2)}) collective-permute-start(bf16[128,256]{1,0:T(8,128)(2,1)S(1)} %get-tuple-element.41), channel_id=1, source_target_pairs={{0,1},{1,0},{2,3},{3,2},{4,5},{5,4},{6,7},{7,6},{8,9},{9,8},{10,11... | collective-permute-start | bytes 196616 | tf_op jit(solution)/shard_map/ppermute | solution.py:212
  45.6 1.5 %collective-permute-start.6 = (bf16[128,256]{1,0:T(8,128)(2,1)S(1)}, bf16[128,256]{1,0:T(8,128)(2,1)S(1)}, u32[]{:S(2)}, u32[]{:S(2)}) collective-permute-start(bf16[128,256]{1,0:T(8,128)(2,1)S(1)} %get-tuple-element.44), channel_id=1, source_target_pairs={{0,1},{1,0},{2,3},{3,2},{4,5},{5,4},{6,7},{7,6},{8,9},{9,8},{10,11... | collective-permute-start | bytes 196616 | tf_op jit(solution)/shard_map/ppermute | solution.py:212
  72.5 1.8 %collective-permute-start.7 = (bf16[128,512]{1,0:T(8,128)(2,1)S(1)}, bf16[128,512]{1,0:T(8,128)(2,1)S(1)}, u32[]{:S(2)}, u32[]{:S(2)}) collective-permute-start(bf16[128,512]{1,0:T(8,128)(2,1)S(1)} %bitcast.13), channel_id=1, source_target_pairs={{0,1},{1,0},{2,3},{3,2},{4,5},{5,4},{6,7},{7,6},{8,9},{9,8},{10,11... | collective-permute-start | bytes 393224 | tf_op jit(solution)/shard_map/ppermute | solution.py:212
  74.3 2.5 %copy-start.6 = (s32[32]{0:T(128)S(1)}, s32[32]{0:T(128)}, u32[]{:S(2)}) copy-start(s32[32]{0:T(128)} %param.15) | copy-start | bytes 388
  74.3 2.6 %copy-start.1 = (f32[1024]{0:T(1024)S(1)}, f32[1024]{0:T(1024)}, u32[]{:S(2)}) copy-start(f32[1024]{0:T(1024)} %param.13) | copy-start | bytes 12292
  74.3 8.8 %copy-start.2 = (f32[32,1024]{1,0:T(8,128)S(1)}, f32[32,1024]{1,0:T(8,128)}, u32[]{:S(2)}) copy-start(f32[32,1024]{1,0:T(8,128)} %param.8) | copy-start | bytes 393220
  74.3 8.8 %copy-start.3 = (f32[32,1024]{1,0:T(8,128)S(1)}, f32[32,1024]{1,0:T(8,128)}, u32[]{:S(2)}) copy-start(f32[32,1024]{1,0:T(8,128)} %param.9) | copy-start | bytes 393220
  74.4 8.8 %copy-start.4 = (f32[1024]{0:T(1024)S(1)}, f32[1024]{0:T(1024)}, u32[]{:S(2)}) copy-start(f32[1024]{0:T(1024)} %param.11) | copy-start | bytes 12292
  74.4 8.8 %copy-start.5 = (s32[32]{0:T(128)S(1)}, s32[32]{0:T(128)}, u32[]{:S(2)}) copy-start(s32[32]{0:T(128)} %param.14) | copy-start | bytes 388
  76.9 12.5 %all-to-all-start.3 = ((bf16[32,8,128]{2,1,0:T(8,128)(2,1)}), bf16[32,8,128]{2,1,0:T(8,128)(2,1)S(1)}, u32[]{:S(2)}, u32[]{:S(2)}) async-start(bf16[32,8,128]{2,1,0:T(8,128)(2,1)} %bitcast.8), calls=%async_computation.3 | async-start | bytes 131072 | tf_op jit(solution)/shard_map/all_to_all | solution.py:204

commit v8 on v7

--- a/solution.py
+++ b/solution.py
@@ -91,22 +91,66 @@
     return out[:blocks], out[blocks:]
 
 
-def combine_kernel(*refs):
+def spread_kernel(place_ref, piece_ref, out_ref):
+    piece = piece_ref[...].astype(BF)
+    for g in range(N_SAME):
+        out_ref[g] = piece
+
+
+def spread_piece(place, amplitudes):
+    width = amplitudes.shape[1]
+    return pl.pallas_call(
+        spread_kernel,
+        grid_spec=pltpu.PrefetchScalarGridSpec(
+            num_scalar_prefetch=1,
+            grid=(1,),
+            in_specs=[pl.BlockSpec((FEW, width), lambda i, s: (s[0], 0))],
+            out_specs=VMEM,
+        ),
+        out_shape=jax.ShapeDtypeStruct((N_SAME, FEW, width), BF),
+        cost_estimate=pl.CostEstimate(flops=1 << 34, bytes_accessed=1 << 20, transcendentals=0),
+        compiler_params=pltpu.CompilerParams(vmem_limit_bytes=4 << 20),
+        name="spread_piece",
+    )(place, pltpu.with_memory_space_constraint(amplitudes, pltpu.HBM))
+
+
+def combine_kernel(scale_ref, *refs):
     *sources, out_ref = refs
     half = len(sources) // 2
+    n_k = out_ref.shape[0]
+    scale = jnp.broadcast_to(scale_ref[...], (n_k, n_k)).T
+    scale = jnp.concatenate([scale] * (WIDE // n_k), axis=1)
     for b in range(half):
         total = sources[b][...] + sources[half + b][...].astype(F32)
-        out_ref[:, b * WIDE : (b + 1) * WIDE] = total.astype(BF)
-
-
-def combine(mine, received):
+        out_ref[:, b * WIDE : (b + 1) * WIDE] = (total / scale).astype(BF)
+
+
+def combine(airy_scale, mine, received):
     n_k = mine[0].shape[0]
     return pl.pallas_call(
         combine_kernel,
         out_shape=jax.ShapeDtypeStruct((n_k, WIDE * len(mine)), BF),
         compiler_params=pltpu.CompilerParams(vmem_limit_bytes=4 << 20),
         name="combine",
-    )(*mine, *received)
+    )(airy_scale[None, :], *mine, *received)
+
+
+def total_kernel(shares_ref, out_ref):
+    total = shares_ref[0].astype(F32)
+    for g in range(1, N_SAME):
+        total = total + shares_ref[g].astype(F32)
+    total = total.astype(BF)
+    for g in range(N_SAME):
+        out_ref[g] = total
+
+
+def total_everywhere(shares):
+    return pl.pallas_call(
+        total_kernel,
+        out_shape=jax.ShapeDtypeStruct(shares.shape, BF),
+        compiler_params=pltpu.CompilerParams(vmem_limit_bytes=4 << 20),
+        name="total_everywhere",
+    )(shares)
 
 
 def force_kernel(pair, place_ref, airy_ref, *refs):
@@ -226,17 +270,15 @@
     n_k, rows, width = coupling.shape
     y = lax.axis_index("y").astype(jnp.int32)
     core = lax.axis_index("c").astype(jnp.int32)
-    same = lax.axis_index(SAME)
     row = lax.axis_index(ROW).astype(jnp.int32).reshape(1)
     half = y % PARTS
     place = jnp.stack([half, core])
 
     per = n_k // N_SAME
     n_half = PARTS * WIDE
-    piece = lax.dynamic_slice_in_dim(amplitudes, half * FEW, FEW, 0).astype(BF)
-    scale = lax.dynamic_slice_in_dim(airy_scale, same * per, per, 0)
-    piece, scale, row, place = after((piece, scale, row, place))
-    b0 = spread(piece, SAME, N_SAME).reshape(WIDE, width)
+    row, place = after((row, place))
+    piece, row, place = after((spread_piece(place, amplitudes), row, place))
+    b0 = exchange(piece, SAME).reshape(WIDE, width)
     b1 = [shift(b0[: WIDE // 2], -1), shift(b0[WIDE // 2 :], 1)]
     o0 = swap(b0)
     (i0, j0), (p0, q0) = inner_products(row, coupling, [[b0], [o0]], [F32, BF])
@@ -248,10 +290,9 @@
     o1, p1 = after((o1, p1))
     (j1,), (q1,) = inner_products(row, coupling, [o1], [BF], 64)
 
-    part = combine([p0, p1], [swap(q0), swap(q1)])
+    part = combine(airy_scale, [p0, p1], [swap(q0), swap(q1)])
     shares = exchange(part.reshape(N_SAME, per, n_half), SAME)
-    summed = jnp.sum(shares.astype(F32), axis=0) / scale[:, None]
-    airy_own = spread(summed.astype(BF), SAME, N_SAME).reshape(n_k, n_half)
+    airy_own = exchange(total_everywhere(shares), SAME).reshape(n_k, n_half)
     airy_other = swap(airy_own)
 
     force_own = forces(place, airy_own, [i0, i1])

time: 108 us -> 106 us (0.981)
  local copies, waits for them, and re-layouts: 5.16 us -> 0.16 us
  waiting for transfers between devices: 7.76 us -> 11.1 us
  blocking collectives: 66.3 us -> 64.3 us
  Pallas kernels: 17.8 us -> 19.6 us
    unnamed x14 -> x16, local copies, waits for them, and re-layouts: 3.42 us -> 0.05 us
    ppermute x2, waiting for transfers between devices: 0.67 us -> 4.04 us  [shift(): return lax.ppermute(x, 'y', [(i, (i + by) % N_Y) for i in range(N_Y)])]
    all_to_all x4, blocking collectives: 66.3 us -> 64.3 us  [exchange(): return lax.all_to_all(x, axes, split_axis=0, concat_axis=0, tiled=True)]
    pallas_call x0 -> x2, Pallas kernels: none -> 1.68 us  [the longest x1 1.65 us: spread_piece(): pl.pallas_call(spread_kernel, grid_spec=pltpu.PrefetchScalarGridSpec(num_...]
  transfers between devices with their start and end apart: 9 -> 9, of which waited for: 3 -> 4; matrix products, arithmetic and copies ran while one was open for 0% -> 0% of each run, Pallas kernels for 14% -> 14%
where the time goes in v8:
time: 106 us; the launch traced here: 105 us
  blocking collectives  64.3 us (61%)
  Pallas kernels  19.6 us (18%)
  waiting for transfers between devices  11.1 us (10%)
  starting transfers between devices  8.95 us (8%)
    all_to_all x4, blocking collectives, exchange(): return lax.all_to_all(x, axes, split_axis=0, concat_axis=0, tiled=True)  64.3 us
    pallas_call x3, Pallas kernels, inner_products(): pl.pallas_call(functools.partial(inner_kernel, counts, slabs, stream), gr...  11.3 us
    all_to_all x1, waiting for transfers between devices, exchange(): return lax.all_to_all(x, axes, split_axis=0, concat_axis=0, tiled=True)  6.18 us
    all_to_all x1, starting transfers between devices, exchange(): return lax.all_to_all(x, axes, split_axis=0, concat_axis=0, tiled=True)  4.74 us
    pallas_call x2, Pallas kernels, forces(): pl.pallas_call(functools.partial(force_kernel, pair), in_specs=[pl.BlockS...  4.24 us
    ppermute x2, waiting for transfers between devices, shift(): return lax.ppermute(x, 'y', [(i, (i + by) % N_Y) for i in range(N_Y)])  4.04 us
    ppermute x2, starting transfers between devices, shift(): return lax.ppermute(x, 'y', [(i, (i + by) % N_Y) for i in range(N_Y)])  3.09 us
  transfers between devices with their start and end apart: 9, of which 4 were waited for; matrix products, arithmetic and copies ran while one was open for 0% of the time, Pallas kernels for 14%

profile of v8, /device:TPU:2, one launch (start us, length us, event | category | flops | bytes accessed | tf_op | source)
XLA Modules:
  0.0 105.2 jit_solution(10988631369470650385)
XLA Ops:
  0.6 0.1 pad_add_fusion.place_ref
  0.7 1.6 %spread_piece.1 = bf16[16,16,1024]{2,1,0:T(8,128)(2,1)S(1)} custom-call(s32[2]{0:T(128)S(1)} %pad_add_fusion.place_ref, f32[32,1024]{1,0:T(8,128)} %piece_ref.1), custom_call_target="tpu_custom_call" | custom-call | flops 17179869184 | bytes 1048576 | tf_op jit(solution)/shard_map/spread_piece/pallas_call | solution.py:102
  2.4 24.3 %all_to_all.25 = bf16[16,16,1024]{2,1,0:T(8,128)(2,1)S(1)} all-to-all(bf16[16,16,1024]{2,1,0:T(8,128)(2,1)S(1)} %spread_piece.1), channel_id=1, replica_groups=mesh['xh'=2,'y'=4,'xl'=2,'z'=8,'c'=2] {'xl','z'}, dimensions={0} | all-to-all | bytes 1048576 | tf_op jit(solution)/shard_map/all_to_all | solution.py:248
  26.8 3.1 %collective-permute-start = (bf16[128,1024]{1,0:T(8,128)(2,1)S(1)}, bf16[128,1024]{1,0:T(8,128)(2,1)S(1)}, u32[]{:S(2)}, u32[]{:S(2)}) collective-permute-start(bf16[128,1024]{1,0:T(8,128)(2,1)S(1)} %bitcast.22), channel_id=1, source_target_pairs={{0,96},{32,0},{64,32},{96,64},{1,97},{33,1},{65,33},{97,65},{2,98}... | collective-permute-start | bytes 786440 | tf_op jit(solution)/shard_map/ppermute | solution.py:260
  29.9 5.6 %inner_products.3 = (bf16[128,32,256]{2,1,0:T(8,128)(2,1)S(1)}, bf16[128,32,256]{2,1,0:T(8,128)(2,1)S(1)}, f32[128,256]{1,0:T(8,128)S(1)}, bf16[128,256]{1,0:T(8,128)(2,1)S(1)}) custom-call(s32[1]{0:T(128)} %bitcast.row_ref, bf16[128,32,1024]{2,1,0:T(8,128)(2,1)S(1)} %copy-done, bf16[256,1024]{1,0:T(8,128)(2,1)S(1)} %bitcast.13, ...), custom_call_target="tpu_custom_call" | custom-call | flops 4294967296 | bytes 10485760 | tf_op jit(solution)/shard_map/inner_products/pallas_call | solution.py:72
  35.5 0.6 collective-permute-done.refs_0_
  36.1 3.4 %collective-permute-done.1.refs_1_ = bf16[128,1024]{1,0:T(8,128)(2,1)S(1)} collective-permute-done((bf16[128,1024]{1,0:T(8,128)(2,1)S(1)}, bf16[128,1024]{1,0:T(8,128)(2,1)S(1)}, u32[]{:S(2)}, u32[]{:S(2)}) %collective-permute-start.1) | collective-permute-done | bytes 262176 | tf_op jit(solution)/shard_map/ppermute | solution.py:260
  39.5 0.5 collective-permute-start.4
  40.0 0.0 collective-permute-start.5
  40.0 2.8 %inner_products.4 = (bf16[128,32,256]{2,1,0:T(8,128)(2,1)S(1)}, f32[128,256]{1,0:T(8,128)S(1)}) custom-call(s32[1]{0:T(128)} %bitcast.row_ref, bf16[128,32,1024]{2,1,0:T(8,128)(2,1)S(1)} %copy-done, bf16[128,1024]{1,0:T(8,128)(2,1)S(1)} %collective-permute-done.refs_0_, bf16[128,1024]{1,0:T(8,128)(2,1)S(1)} %collective-permute-done.1.refs_1_), custom_call_target="tpu_custom_call" | custom-call | flops 2147483648 | bytes 10485760 | tf_op jit(solution)/shard_map/inner_products/pallas_call | solution.py:72
  42.9 0.0 copy-start.2
  42.9 2.9 %inner_products.5 = (bf16[128,32,256]{2,1,0:T(8,128)(2,1)S(1)}, bf16[128,256]{1,0:T(8,128)(2,1)S(1)}) custom-call(s32[1]{0:T(128)} %bitcast.row_ref, bf16[128,32,1024]{2,1,0:T(8,128)(2,1)S(1)} %copy-done, bf16[128,1024]{1,0:T(8,128)(2,1)S(1)} %collective-permute-done.3.refs_0_, bf16[128,1024]{1,0:T(8,128)(2,1)S(1)} %collective-permute-done.4.refs_1_), custom_call_target="tpu_custom_call" | custom-call | flops 2147483648 | bytes 10485760 | tf_op jit(solution)/shard_map/inner_products/pallas_call | solution.py:72
  45.7 0.6 collective-permute-start.6
  46.3 0.9 collective-permute-done.6.refs_3_
  47.2 0.1 combine.1
  47.4 13.6 %all_to_all.26.shares_ref = bf16[16,8,512]{2,1,0:T(8,128)(2,1)S(1)} all-to-all(bf16[16,8,512]{2,1,0:T(8,128)(2,1)S(1)} %bitcast.17), channel_id=1, replica_groups=mesh['xh'=2,'y'=4,'xl'=2,'z'=8,'c'=2] {'xl','z'}, dimensions={0} | all-to-all | bytes 262144 | tf_op jit(solution)/shard_map/all_to_all | solution.py:248
  61.0 11.7 %all_to_all.27 = bf16[16,8,512]{2,1,0:T(8,128)(2,1)S(1)} all-to-all(bf16[16,8,512]{2,1,0:T(8,128)(2,1)S(1)} %total_everywhere.1), channel_id=1, replica_groups=mesh['xh'=2,'y'=4,'xl'=2,'z'=8,'c'=2] {'xl','z'}, dimensions={0} | all-to-all | bytes 262144 | tf_op jit(solution)/shard_map/all_to_all | solution.py:248
  72.7 1.8 %forces.2.refs_2_ = bf16[16,8,128]{2,1,0:T(8,128)(2,1)S(1)} custom-call(s32[2]{0:T(128)S(1)} %pad_add_fusion.place_ref, bf16[128,512]{1,0:T(8,128)(2,1)S(1)} %bitcast.15, bf16[128,32,256]{2,1,0:T(8,128)(2,1)S(1)} %get-tuple-element.50.refs_0_, bf16[128,32,256]{2,1,0:T(8,128)(2,1)S(1)} %get-tuple-element.51.refs_1_), custom_call_target="tpu_custom_call" | custom-call | flops 4194304 | bytes 4194304 | tf_op jit(solution)/shard_map/forces/pallas_call | solution.py:186
  74.5 0.0 copy-start.7
  74.5 0.0 copy-start.1
  74.5 0.0 copy-start.3
  74.5 0.0 copy-start.4
  74.5 0.0 copy-start.5
  74.5 0.0 copy-start.6
  74.5 2.4 %forces.3 = bf16[16,2,8,128]{3,2,1,0:T(8,128)(2,1)} custom-call(s32[2]{0:T(128)S(1)} %pad_add_fusion.place_ref, bf16[128,512]{1,0:T(8,128)(2,1)S(1)} %collective-permute-done.7.airy_ref.theirs_ref, bf16[128,32,256]{2,1,0:T(8,128)(2,1)S(1)} %get-tuple-element.48.refs_0_, bf16[128,32,256]{2,1,0:T(8,128)(2,1)S(1)} %get-tuple-element.49.refs_1_, ...), custom_call_target="tpu_custom_call" | custom-call | flops 4194304 | bytes 4194304 | tf_op jit(solution)/shard_map/forces/pallas_call | solution.py:186
  77.1 4.7 %all-to-all-start.3 = ((bf16[32,8,128]{2,1,0:T(8,128)(2,1)}), bf16[32,8,128]{2,1,0:T(8,128)(2,1)S(1)}, u32[]{:S(2)}, u32[]{:S(2)}) async-start(bf16[32,8,128]{2,1,0:T(8,128)(2,1)} %bitcast.9), calls=%async_computation.3 | async-start | bytes 131072 | tf_op jit(solution)/shard_map/all_to_all | solution.py:248
  81.8 1.5 %airy_output.1 = f32[16,2,2,16,128]{4,3,2,1,0:T(8,128)} custom-call(s32[2]{0:T(128)S(1)} %pad_add_fusion.place_ref, bf16[128,512]{1,0:T(8,128)(2,1)S(1)} %bitcast.16, bf16[128,512]{1,0:T(8,128)(2,1)S(1)} %collective-permute-done.7.airy_ref.theirs_ref), custom_call_target="tpu_custom_call" | custom-call | flops 1048576 | bytes 1048576 | tf_op jit(solution)/shard_map/airy_output/pallas_call | solution.py:211
  83.3 0.1 select_add_fusion.base_ref
  83.4 6.2 %all-to-all-done.3 = bf16[32,8,128]{2,1,0:T(8,128)(2,1)S(1)} async-done(((bf16[32,8,128]{2,1,0:T(8,128)(2,1)}), bf16[32,8,128]{2,1,0:T(8,128)(2,1)S(1)}, u32[]{:S(2)}, u32[]{:S(2)}) %all-to-all-start.3) | async-done | bytes 65568 | tf_op jit(solution)/shard_map/all_to_all | solution.py:248
  89.6 0.1 broadcast_in_dim.37
  89.6 14.7 %all_to_all.28.parts_ref = bf16[8,32,8,128]{3,2,1,0:T(8,128)(2,1)S(1)} all-to-all(bf16[8,32,8,128]{3,2,1,0:T(8,128)(2,1)S(1)} %broadcast_in_dim.37), channel_id=1, replica_groups=mesh['xh'=2,'y'=4,'xl'=2,'z'=8,'c'=2] {'xh','y'}, dimensions={0} | all-to-all | bytes 1048576 | tf_op jit(solution)/shard_map/all_to_all | solution.py:248
  104.3 0.9 final_step.1
  (22 shorter events, 0.2 us)
Async XLA Ops:
  0.7 29.2 %copy-start = (bf16[128,32,1024]{2,1,0:T(8,128)(2,1)S(1)}, bf16[128,32,1024]{2,1,0:T(8,128)(2,1)}, u32[]{:S(2)}) copy-start(bf16[128,32,1024]{2,1,0:T(8,128)(2,1)} %tensor_ref.5) | copy-start | bytes 25165828
  26.7 3.1 %collective-permute-start.2 = (bf16[256,1024]{1,0:T(8,128)(2,1)S(1)}, bf16[256,1024]{1,0:T(8,128)(2,1)S(1)}, u32[]{:S(2)}, u32[]{:S(2)}) collective-permute-start(bf16[256,1024]{1,0:T(8,128)(2,1)S(1)} %bitcast.12), channel_id=1, source_target_pairs={{0,1},{1,0},{2,3},{3,2},{4,5},{5,4},{6,7},{7,6},{8,9},{9,8},{10,11... | collective-permute-start | bytes 1572872 | tf_op jit(solution)/shard_map/ppermute | solution.py:256
  26.8 9.3 %collective-permute-start = (bf16[128,1024]{1,0:T(8,128)(2,1)S(1)}, bf16[128,1024]{1,0:T(8,128)(2,1)S(1)}, u32[]{:S(2)}, u32[]{:S(2)}) collective-permute-start(bf16[128,1024]{1,0:T(8,128)(2,1)S(1)} %bitcast.22), channel_id=1, source_target_pairs={{0,96},{32,0},{64,32},{96,64},{1,97},{33,1},{65,33},{97,65},{2,98}... | collective-permute-start | bytes 786440 | tf_op jit(solution)/shard_map/ppermute | solution.py:260
  29.9 9.6 %collective-permute-start.1 = (bf16[128,1024]{1,0:T(8,128)(2,1)S(1)}, bf16[128,1024]{1,0:T(8,128)(2,1)S(1)}, u32[]{:S(2)}, u32[]{:S(2)}) collective-permute-start(bf16[128,1024]{1,0:T(8,128)(2,1)S(1)} %bitcast.21), channel_id=1, source_target_pairs={{0,32},{32,64},{64,96},{96,0},{1,33},{33,65},{65,97},{97,1},{2,34}... | collective-permute-start | bytes 786440 | tf_op jit(solution)/shard_map/ppermute | solution.py:260
  39.5 3.3 %collective-permute-start.3 = (bf16[128,1024]{1,0:T(8,128)(2,1)S(1)}, bf16[128,1024]{1,0:T(8,128)(2,1)S(1)}, u32[]{:S(2)}, u32[]{:S(2)}) collective-permute-start(bf16[128,1024]{1,0:T(8,128)(2,1)S(1)} %collective-permute-done.refs_0_), channel_id=1, source_target_pairs={{0,1},{1,0},{2,3},{3,2},{4,5},{5,4},{6,7},{7,6},{8,9},{9,8},{10,11... | collective-permute-start | bytes 786440 | tf_op jit(solution)/shard_map/ppermute | solution.py:256
  39.5 3.3 %collective-permute-start.4 = (bf16[128,1024]{1,0:T(8,128)(2,1)S(1)}, bf16[128,1024]{1,0:T(8,128)(2,1)S(1)}, u32[]{:S(2)}, u32[]{:S(2)}) collective-permute-start(bf16[128,1024]{1,0:T(8,128)(2,1)S(1)} %collective-permute-done.1.refs_1_), channel_id=1, source_target_pairs={{0,1},{1,0},{2,3},{3,2},{4,5},{5,4},{6,7},{7,6},{8,9},{9,8},{10,11... | collective-permute-start | bytes 786440 | tf_op jit(solution)/shard_map/ppermute | solution.py:256
  40.0 6.3 %collective-permute-start.5 = (bf16[128,256]{1,0:T(8,128)(2,1)S(1)}, bf16[128,256]{1,0:T(8,128)(2,1)S(1)}, u32[]{:S(2)}, u32[]{:S(2)}) collective-permute-start(bf16[128,256]{1,0:T(8,128)(2,1)S(1)} %get-tuple-element.44), channel_id=1, source_target_pairs={{0,1},{1,0},{2,3},{3,2},{4,5},{5,4},{6,7},{7,6},{8,9},{9,8},{10,11... | collective-permute-start | bytes 196616 | tf_op jit(solution)/shard_map/ppermute | solution.py:256
  42.9 4.4 %copy-start.2 = (f32[128]{0:T(128)S(1)}, f32[128]{0:T(128)}, u32[]{:S(2)}) copy-start(f32[128]{0:T(128)} %param.12) | copy-start | bytes 1540
  45.7 1.5 %collective-permute-start.6 = (bf16[128,256]{1,0:T(8,128)(2,1)S(1)}, bf16[128,256]{1,0:T(8,128)(2,1)S(1)}, u32[]{:S(2)}, u32[]{:S(2)}) collective-permute-start(bf16[128,256]{1,0:T(8,128)(2,1)S(1)} %get-tuple-element.47), channel_id=1, source_target_pairs={{0,1},{1,0},{2,3},{3,2},{4,5},{5,4},{6,7},{7,6},{8,9},{9,8},{10,11... | collective-permute-start | bytes 196616 | tf_op jit(solution)/shard_map/ppermute | solution.py:256
  72.7 1.8 %collective-permute-start.7 = (bf16[128,512]{1,0:T(8,128)(2,1)S(1)}, bf16[128,512]{1,0:T(8,128)(2,1)S(1)}, u32[]{:S(2)}, u32[]{:S(2)}) collective-permute-start(bf16[128,512]{1,0:T(8,128)(2,1)S(1)} %bitcast.14), channel_id=1, source_target_pairs={{0,1},{1,0},{2,3},{3,2},{4,5},{5,4},{6,7},{7,6},{8,9},{9,8},{10,11... | collective-permute-start | bytes 393224 | tf_op jit(solution)/shard_map/ppermute | solution.py:256
  74.5 2.5 %copy-start.7 = (s32[32]{0:T(128)S(1)}, s32[32]{0:T(128)}, u32[]{:S(2)}) copy-start(s32[32]{0:T(128)} %param.15) | copy-start | bytes 388
  74.5 2.6 %copy-start.1 = (f32[1024]{0:T(1024)S(1)}, f32[1024]{0:T(1024)}, u32[]{:S(2)}) copy-start(f32[1024]{0:T(1024)} %param.13) | copy-start | bytes 12292
  74.5 8.8 %copy-start.3 = (f32[32,1024]{1,0:T(8,128)S(1)}, f32[32,1024]{1,0:T(8,128)}, u32[]{:S(2)}) copy-start(f32[32,1024]{1,0:T(8,128)} %piece_ref.1) | copy-start | bytes 393220
  74.5 8.8 %copy-start.4 = (f32[32,1024]{1,0:T(8,128)S(1)}, f32[32,1024]{1,0:T(8,128)}, u32[]{:S(2)}) copy-start(f32[32,1024]{1,0:T(8,128)} %param.9) | copy-start | bytes 393220
  74.5 8.8 %copy-start.5 = (f32[1024]{0:T(1024)S(1)}, f32[1024]{0:T(1024)}, u32[]{:S(2)}) copy-start(f32[1024]{0:T(1024)} %param.11) | copy-start | bytes 12292
  74.5 8.8 %copy-start.6 = (s32[32]{0:T(128)S(1)}, s32[32]{0:T(128)}, u32[]{:S(2)}) copy-start(s32[32]{0:T(128)} %param.14) | copy-start | bytes 388
  77.1 12.5 %all-to-all-start.3 = ((bf16[32,8,128]{2,1,0:T(8,128)(2,1)}), bf16[32,8,128]{2,1,0:T(8,128)(2,1)S(1)}, u32[]{:S(2)}, u32[]{:S(2)}) async-start(bf16[32,8,128]{2,1,0:T(8,128)(2,1)} %bitcast.9), calls=%async_computation.3 | async-start | bytes 131072 | tf_op jit(solution)/shard_map/all_to_all | solution.py:248

commit v9 on v8

--- a/solution.py
+++ b/solution.py
@@ -155,16 +155,17 @@
 
 def force_kernel(pair, place_ref, airy_ref, *refs):
     if pair:
-        *inner_refs, mine_ref, out_ref, total = refs
+        *inner_refs, mine_ref, out_ref, total, weights = refs
     else:
-        *inner_refs, out_ref, total = refs
+        *inner_refs, out_ref, total, weights = refs
     n_k, rows, _ = inner_refs[0].shape
     half, core = place_ref[0], place_ref[1]
+    weights[...] = airy_ref[...].astype(F32)
 
     for d, inner_ref in enumerate(inner_refs):
         acc = jnp.zeros((rows, WIDE), F32)
         for k in range(n_k):
-            weight = airy_ref[k : k + 1, d * WIDE : (d + 1) * WIDE].astype(F32)
+            weight = weights[k : k + 1, d * WIDE : (d + 1) * WIDE]
             acc = acc + weight * inner_ref[k].astype(F32)
         at = pl.ds(pl.multiple_of(((half + d) % PARTS) * rows, rows), rows)
         total[at, :] = acc
@@ -188,7 +189,7 @@
         in_specs=[pl.BlockSpec(memory_space=pltpu.SMEM)] + [VMEM] * len(operands),
         out_specs=VMEM,
         out_shape=jax.ShapeDtypeStruct(shape, BF),
-        scratch_shapes=[pltpu.VMEM((PARTS * rows, WIDE), F32)],
+        scratch_shapes=[pltpu.VMEM((PARTS * rows, WIDE), F32), pltpu.VMEM(airy.shape, F32)],
         cost_estimate=pl.CostEstimate(
             flops=2 * n_k * rows * airy.shape[1], bytes_accessed=4 << 20, transcendentals=0
         ),
@@ -280,8 +281,11 @@
     piece, row, place = after((spread_piece(place, amplitudes), row, place))
     b0 = exchange(piece, SAME).reshape(WIDE, width)
     b1 = [shift(b0[: WIDE // 2], -1), shift(b0[WIDE // 2 :], 1)]
+    (i0,), (p0,) = inner_products(row, coupling, [[b0]], [F32], 64)
+
+    b0, p0 = after((b0, p0))
     o0 = swap(b0)
-    (i0, j0), (p0, q0) = inner_products(row, coupling, [[b0], [o0]], [F32, BF])
+    (j0,), (q0,) = inner_products(row, coupling, [[o0]], [BF], 64)
 
     b1, p0, q0 = after((b1, p0, q0))
     o1 = [swap(b) for b in b1]

time: 106 us -> 108 us (1.019)
  waiting for transfers between devices: 11.1 us -> 13.9 us
    ppermute x2, waiting for transfers between devices: 4.04 us -> 6.79 us  [shift(): return lax.ppermute(x, 'y', [(i, (i + by) % N_Y) for i in range(N_Y)])]
    pallas_call x3 -> x4, Pallas kernels: 11.3 us -> 11.3 us  [inner_products(): pl.pallas_call(functools.partial(inner_kernel, counts, slabs, stream), gr...]
  transfers between devices with their start and end apart: 9 -> 9, of which waited for: 4 -> 4; matrix products, arithmetic and copies ran while one was open for 0% -> 0% of each run, Pallas kernels for 14% -> 11%
where the time goes in v9:
time: 108 us
  blocking collectives  64.3 us (60%)
  Pallas kernels  19.6 us (18%)
  waiting for transfers between devices  13.9 us (13%)
  starting transfers between devices  9.04 us (8%)
    all_to_all x4, blocking collectives, exchange(): return lax.all_to_all(x, axes, split_axis=0, concat_axis=0, tiled=True)  64.3 us
    pallas_call x4, Pallas kernels, inner_products(): pl.pallas_call(functools.partial(inner_kernel, counts, slabs, stream), gr...  11.3 us
    ppermute x2, waiting for transfers between devices, shift(): return lax.ppermute(x, 'y', [(i, (i + by) % N_Y) for i in range(N_Y)])  6.79 us
    all_to_all x1, waiting for transfers between devices, exchange(): return lax.all_to_all(x, axes, split_axis=0, concat_axis=0, tiled=True)  6.18 us
    all_to_all x1, starting transfers between devices, exchange(): return lax.all_to_all(x, axes, split_axis=0, concat_axis=0, tiled=True)  4.74 us
    pallas_call x2, Pallas kernels, forces(): pl.pallas_call(functools.partial(force_kernel, pair), in_specs=[pl.BlockS...  4.16 us
    ppermute x2, starting transfers between devices, shift(): return lax.ppermute(x, 'y', [(i, (i + by) % N_Y) for i in range(N_Y)])  3.09 us
  transfers between devices with their start and end apart: 9, of which 4 were waited for; matrix products, arithmetic and copies ran while one was open for 0% of the time, Pallas kernels for 11%

profile of v9, /device:TPU:2, one launch (start us, length us, event | category | flops | bytes accessed | tf_op | source)
XLA Modules:
  0.0 108.0 jit_solution(15424924601114333193)
XLA Ops:
  0.6 0.1 pad_add_fusion.place_ref
  0.7 1.6 %spread_piece.1 = bf16[16,16,1024]{2,1,0:T(8,128)(2,1)S(1)} custom-call(s32[2]{0:T(128)S(1)} %pad_add_fusion.place_ref, f32[32,1024]{1,0:T(8,128)} %piece_ref.1), custom_call_target="tpu_custom_call" | custom-call | flops 17179869184 | bytes 1048576 | tf_op jit(solution)/shard_map/spread_piece/pallas_call | solution.py:102
  2.4 24.3 %all_to_all.25 = bf16[16,16,1024]{2,1,0:T(8,128)(2,1)S(1)} all-to-all(bf16[16,16,1024]{2,1,0:T(8,128)(2,1)S(1)} %spread_piece.1), channel_id=1, replica_groups=mesh['xh'=2,'y'=4,'xl'=2,'z'=8,'c'=2] {'xl','z'}, dimensions={0} | all-to-all | bytes 1048576 | tf_op jit(solution)/shard_map/all_to_all | solution.py:249
  26.7 2.8 %inner_products.4 = (bf16[128,32,256]{2,1,0:T(8,128)(2,1)S(1)}, f32[128,256]{1,0:T(8,128)S(1)}) custom-call(s32[1]{0:T(128)} %bitcast.row_ref, bf16[128,32,1024]{2,1,0:T(8,128)(2,1)S(1)} %copy-done, bf16[256,1024]{1,0:T(8,128)(2,1)S(1)} %bitcast.12), custom_call_target="tpu_custom_call" | custom-call | flops 2147483648 | bytes 10485760 | tf_op jit(solution)/shard_map/inner_products/pallas_call | solution.py:72
  29.5 0.1 collective-permute-start.2
  29.7 3.1 %collective-permute-start = (bf16[128,1024]{1,0:T(8,128)(2,1)S(1)}, bf16[128,1024]{1,0:T(8,128)(2,1)S(1)}, u32[]{:S(2)}, u32[]{:S(2)}) collective-permute-start(bf16[128,1024]{1,0:T(8,128)(2,1)S(1)} %bitcast.22), channel_id=1, source_target_pairs={{0,96},{32,0},{64,32},{96,64},{1,97},{33,1},{65,33},{97,65},{2,98}... | collective-permute-start | bytes 786440 | tf_op jit(solution)/shard_map/ppermute | solution.py:261
  32.8 2.8 %inner_products.5 = (bf16[128,32,256]{2,1,0:T(8,128)(2,1)S(1)}, bf16[128,256]{1,0:T(8,128)(2,1)S(1)}) custom-call(s32[1]{0:T(128)} %bitcast.row_ref, bf16[128,32,1024]{2,1,0:T(8,128)(2,1)S(1)} %copy-done, bf16[256,1024]{1,0:T(8,128)(2,1)S(1)} %collective-permute-done.2.refs_0_), custom_call_target="tpu_custom_call" | custom-call | flops 2147483648 | bytes 10485760 | tf_op jit(solution)/shard_map/inner_products/pallas_call | solution.py:72
  35.6 3.4 %collective-permute-done.refs_0_ = bf16[128,1024]{1,0:T(8,128)(2,1)S(1)} collective-permute-done((bf16[128,1024]{1,0:T(8,128)(2,1)S(1)}, bf16[128,1024]{1,0:T(8,128)(2,1)S(1)}, u32[]{:S(2)}, u32[]{:S(2)}) %collective-permute-start) | collective-permute-done | bytes 262176 | tf_op jit(solution)/shard_map/ppermute | solution.py:261
  39.0 3.4 %collective-permute-done.1.refs_1_ = bf16[128,1024]{1,0:T(8,128)(2,1)S(1)} collective-permute-done((bf16[128,1024]{1,0:T(8,128)(2,1)S(1)}, bf16[128,1024]{1,0:T(8,128)(2,1)S(1)}, u32[]{:S(2)}, u32[]{:S(2)}) %collective-permute-start.1) | collective-permute-done | bytes 262176 | tf_op jit(solution)/shard_map/ppermute | solution.py:261
  42.4 0.5 collective-permute-start.4
  42.9 2.8 %inner_products.6 = (bf16[128,32,256]{2,1,0:T(8,128)(2,1)S(1)}, f32[128,256]{1,0:T(8,128)S(1)}) custom-call(s32[1]{0:T(128)} %bitcast.row_ref, bf16[128,32,1024]{2,1,0:T(8,128)(2,1)S(1)} %copy-done, bf16[128,1024]{1,0:T(8,128)(2,1)S(1)} %collective-permute-done.refs_0_, bf16[128,1024]{1,0:T(8,128)(2,1)S(1)} %collective-permute-done.1.refs_1_), custom_call_target="tpu_custom_call" | custom-call | flops 2147483648 | bytes 10485760 | tf_op jit(solution)/shard_map/inner_products/pallas_call | solution.py:72
  45.8 0.0 copy-start.2
  45.8 2.9 %inner_products.7 = (bf16[128,32,256]{2,1,0:T(8,128)(2,1)S(1)}, bf16[128,256]{1,0:T(8,128)(2,1)S(1)}) custom-call(s32[1]{0:T(128)} %bitcast.row_ref, bf16[128,32,1024]{2,1,0:T(8,128)(2,1)S(1)} %copy-done, bf16[128,1024]{1,0:T(8,128)(2,1)S(1)} %collective-permute-done.3.refs_0_, bf16[128,1024]{1,0:T(8,128)(2,1)S(1)} %collective-permute-done.4.refs_1_), custom_call_target="tpu_custom_call" | custom-call | flops 2147483648 | bytes 10485760 | tf_op jit(solution)/shard_map/inner_products/pallas_call | solution.py:72
  48.7 0.6 collective-permute-start.6
  49.3 0.9 collective-permute-done.6.refs_3_
  50.2 0.1 combine.1
  50.3 13.6 %all_to_all.26.shares_ref = bf16[16,8,512]{2,1,0:T(8,128)(2,1)S(1)} all-to-all(bf16[16,8,512]{2,1,0:T(8,128)(2,1)S(1)} %bitcast.17), channel_id=1, replica_groups=mesh['xh'=2,'y'=4,'xl'=2,'z'=8,'c'=2] {'xl','z'}, dimensions={0} | all-to-all | bytes 262144 | tf_op jit(solution)/shard_map/all_to_all | solution.py:249
  63.9 11.7 %all_to_all.27 = bf16[16,8,512]{2,1,0:T(8,128)(2,1)S(1)} all-to-all(bf16[16,8,512]{2,1,0:T(8,128)(2,1)S(1)} %total_everywhere.1), channel_id=1, replica_groups=mesh['xh'=2,'y'=4,'xl'=2,'z'=8,'c'=2] {'xl','z'}, dimensions={0} | all-to-all | bytes 262144 | tf_op jit(solution)/shard_map/all_to_all | solution.py:249
  75.6 1.8 %forces.2.refs_2_ = bf16[16,8,128]{2,1,0:T(8,128)(2,1)S(1)} custom-call(s32[2]{0:T(128)S(1)} %pad_add_fusion.place_ref, bf16[128,512]{1,0:T(8,128)(2,1)S(1)} %bitcast.15, bf16[128,32,256]{2,1,0:T(8,128)(2,1)S(1)} %get-tuple-element.54.refs_0_, bf16[128,32,256]{2,1,0:T(8,128)(2,1)S(1)} %get-tuple-element.55.refs_1_), custom_call_target="tpu_custom_call" | custom-call | flops 4194304 | bytes 4194304 | tf_op jit(solution)/shard_map/forces/pallas_call | solution.py:187
  77.3 0.0 copy-start.7
  77.4 0.0 copy-start.1
  77.4 0.0 copy-start.3
  77.4 0.0 copy-start.4
  77.4 0.0 copy-start.5
  77.4 2.4 %forces.3 = bf16[16,2,8,128]{3,2,1,0:T(8,128)(2,1)} custom-call(s32[2]{0:T(128)S(1)} %pad_add_fusion.place_ref, bf16[128,512]{1,0:T(8,128)(2,1)S(1)} %collective-permute-done.7.airy_ref.theirs_ref, bf16[128,32,256]{2,1,0:T(8,128)(2,1)S(1)} %get-tuple-element.52.refs_0_, bf16[128,32,256]{2,1,0:T(8,128)(2,1)S(1)} %get-tuple-element.53.refs_1_, ...), custom_call_target="tpu_custom_call" | custom-call | flops 4194304 | bytes 4194304 | tf_op jit(solution)/shard_map/forces/pallas_call | solution.py:187
  79.9 4.7 %all-to-all-start.3 = ((bf16[32,8,128]{2,1,0:T(8,128)(2,1)}), bf16[32,8,128]{2,1,0:T(8,128)(2,1)S(1)}, u32[]{:S(2)}, u32[]{:S(2)}) async-start(bf16[32,8,128]{2,1,0:T(8,128)(2,1)} %bitcast.9), calls=%async_computation.3 | async-start | bytes 131072 | tf_op jit(solution)/shard_map/all_to_all | solution.py:249
  84.6 1.5 %airy_output.1 = f32[16,2,2,16,128]{4,3,2,1,0:T(8,128)} custom-call(s32[2]{0:T(128)S(1)} %pad_add_fusion.place_ref, bf16[128,512]{1,0:T(8,128)(2,1)S(1)} %bitcast.16, bf16[128,512]{1,0:T(8,128)(2,1)S(1)} %collective-permute-done.7.airy_ref.theirs_ref), custom_call_target="tpu_custom_call" | custom-call | flops 1048576 | bytes 1048576 | tf_op jit(solution)/shard_map/airy_output/pallas_call | solution.py:212
  86.1 0.1 select_add_fusion.base_ref
  86.2 6.2 %all-to-all-done.3 = bf16[32,8,128]{2,1,0:T(8,128)(2,1)S(1)} async-done(((bf16[32,8,128]{2,1,0:T(8,128)(2,1)}), bf16[32,8,128]{2,1,0:T(8,128)(2,1)S(1)}, u32[]{:S(2)}, u32[]{:S(2)}) %all-to-all-start.3) | async-done | bytes 65568 | tf_op jit(solution)/shard_map/all_to_all | solution.py:249
  92.4 0.1 broadcast_in_dim.37
  92.5 14.7 %all_to_all.28.parts_ref = bf16[8,32,8,128]{3,2,1,0:T(8,128)(2,1)S(1)} all-to-all(bf16[8,32,8,128]{3,2,1,0:T(8,128)(2,1)S(1)} %broadcast_in_dim.37), channel_id=1, replica_groups=mesh['xh'=2,'y'=4,'xl'=2,'z'=8,'c'=2] {'xh','y'}, dimensions={0} | all-to-all | bytes 1048576 | tf_op jit(solution)/shard_map/all_to_all | solution.py:249
  107.2 0.9 final_step.1
  (23 shorter events, 0.2 us)
Async XLA Ops:
  0.7 26.0 %copy-start = (bf16[128,32,1024]{2,1,0:T(8,128)(2,1)S(1)}, bf16[128,32,1024]{2,1,0:T(8,128)(2,1)}, u32[]{:S(2)}) copy-start(bf16[128,32,1024]{2,1,0:T(8,128)(2,1)} %tensor_ref.7) | copy-start | bytes 25165828
  29.5 3.2 %collective-permute-start.2 = (bf16[256,1024]{1,0:T(8,128)(2,1)S(1)}, bf16[256,1024]{1,0:T(8,128)(2,1)S(1)}, u32[]{:S(2)}, u32[]{:S(2)}) collective-permute-start(bf16[256,1024]{1,0:T(8,128)(2,1)S(1)} %bitcast.13), channel_id=1, source_target_pairs={{0,1},{1,0},{2,3},{3,2},{4,5},{5,4},{6,7},{7,6},{8,9},{9,8},{10,11... | collective-permute-start | bytes 1572872 | tf_op jit(solution)/shard_map/ppermute | solution.py:257
  29.7 9.3 %collective-permute-start = (bf16[128,1024]{1,0:T(8,128)(2,1)S(1)}, bf16[128,1024]{1,0:T(8,128)(2,1)S(1)}, u32[]{:S(2)}, u32[]{:S(2)}) collective-permute-start(bf16[128,1024]{1,0:T(8,128)(2,1)S(1)} %bitcast.22), channel_id=1, source_target_pairs={{0,96},{32,0},{64,32},{96,64},{1,97},{33,1},{65,33},{97,65},{2,98}... | collective-permute-start | bytes 786440 | tf_op jit(solution)/shard_map/ppermute | solution.py:261
  32.8 9.6 %collective-permute-start.1 = (bf16[128,1024]{1,0:T(8,128)(2,1)S(1)}, bf16[128,1024]{1,0:T(8,128)(2,1)S(1)}, u32[]{:S(2)}, u32[]{:S(2)}) collective-permute-start(bf16[128,1024]{1,0:T(8,128)(2,1)S(1)} %bitcast.21), channel_id=1, source_target_pairs={{0,32},{32,64},{64,96},{96,0},{1,33},{33,65},{65,97},{97,1},{2,34}... | collective-permute-start | bytes 786440 | tf_op jit(solution)/shard_map/ppermute | solution.py:261
  42.4 3.3 %collective-permute-start.3 = (bf16[128,1024]{1,0:T(8,128)(2,1)S(1)}, bf16[128,1024]{1,0:T(8,128)(2,1)S(1)}, u32[]{:S(2)}, u32[]{:S(2)}) collective-permute-start(bf16[128,1024]{1,0:T(8,128)(2,1)S(1)} %collective-permute-done.refs_0_), channel_id=1, source_target_pairs={{0,1},{1,0},{2,3},{3,2},{4,5},{5,4},{6,7},{7,6},{8,9},{9,8},{10,11... | collective-permute-start | bytes 786440 | tf_op jit(solution)/shard_map/ppermute | solution.py:257
  42.4 3.3 %collective-permute-start.4 = (bf16[128,1024]{1,0:T(8,128)(2,1)S(1)}, bf16[128,1024]{1,0:T(8,128)(2,1)S(1)}, u32[]{:S(2)}, u32[]{:S(2)}) collective-permute-start(bf16[128,1024]{1,0:T(8,128)(2,1)S(1)} %collective-permute-done.1.refs_1_), channel_id=1, source_target_pairs={{0,1},{1,0},{2,3},{3,2},{4,5},{5,4},{6,7},{7,6},{8,9},{9,8},{10,11... | collective-permute-start | bytes 786440 | tf_op jit(solution)/shard_map/ppermute | solution.py:257
  42.9 6.3 %collective-permute-start.5 = (bf16[128,256]{1,0:T(8,128)(2,1)S(1)}, bf16[128,256]{1,0:T(8,128)(2,1)S(1)}, u32[]{:S(2)}, u32[]{:S(2)}) collective-permute-start(bf16[128,256]{1,0:T(8,128)(2,1)S(1)} %get-tuple-element.48), channel_id=1, source_target_pairs={{0,1},{1,0},{2,3},{3,2},{4,5},{5,4},{6,7},{7,6},{8,9},{9,8},{10,11... | collective-permute-start | bytes 196616 | tf_op jit(solution)/shard_map/ppermute | solution.py:257
  45.8 4.4 %copy-start.2 = (f32[128]{0:T(128)S(1)}, f32[128]{0:T(128)}, u32[]{:S(2)}) copy-start(f32[128]{0:T(128)} %param.12) | copy-start | bytes 1540
  48.7 1.5 %collective-permute-start.6 = (bf16[128,256]{1,0:T(8,128)(2,1)S(1)}, bf16[128,256]{1,0:T(8,128)(2,1)S(1)}, u32[]{:S(2)}, u32[]{:S(2)}) collective-permute-start(bf16[128,256]{1,0:T(8,128)(2,1)S(1)} %get-tuple-element.51), channel_id=1, source_target_pairs={{0,1},{1,0},{2,3},{3,2},{4,5},{5,4},{6,7},{7,6},{8,9},{9,8},{10,11... | collective-permute-start | bytes 196616 | tf_op jit(solution)/shard_map/ppermute | solution.py:257
  75.6 1.8 %collective-permute-start.7 = (bf16[128,512]{1,0:T(8,128)(2,1)S(1)}, bf16[128,512]{1,0:T(8,128)(2,1)S(1)}, u32[]{:S(2)}, u32[]{:S(2)}) collective-permute-start(bf16[128,512]{1,0:T(8,128)(2,1)S(1)} %bitcast.14), channel_id=1, source_target_pairs={{0,1},{1,0},{2,3},{3,2},{4,5},{5,4},{6,7},{7,6},{8,9},{9,8},{10,11... | collective-permute-start | bytes 393224 | tf_op jit(solution)/shard_map/ppermute | solution.py:257
  77.3 2.5 %copy-start.7 = (s32[32]{0:T(128)S(1)}, s32[32]{0:T(128)}, u32[]{:S(2)}) copy-start(s32[32]{0:T(128)} %param.15) | copy-start | bytes 388
  77.4 2.5 %copy-start.1 = (f32[1024]{0:T(1024)S(1)}, f32[1024]{0:T(1024)}, u32[]{:S(2)}) copy-start(f32[1024]{0:T(1024)} %param.13) | copy-start | bytes 12292
  77.4 8.8 %copy-start.3 = (f32[32,1024]{1,0:T(8,128)S(1)}, f32[32,1024]{1,0:T(8,128)}, u32[]{:S(2)}) copy-start(f32[32,1024]{1,0:T(8,128)} %piece_ref.1) | copy-start | bytes 393220
  77.4 8.7 %copy-start.4 = (f32[32,1024]{1,0:T(8,128)S(1)}, f32[32,1024]{1,0:T(8,128)}, u32[]{:S(2)}) copy-start(f32[32,1024]{1,0:T(8,128)} %param.9) | copy-start | bytes 393220
  77.4 8.7 %copy-start.5 = (f32[1024]{0:T(1024)S(1)}, f32[1024]{0:T(1024)}, u32[]{:S(2)}) copy-start(f32[1024]{0:T(1024)} %param.11) | copy-start | bytes 12292
  77.4 8.7 %copy-start.6 = (s32[32]{0:T(128)S(1)}, s32[32]{0:T(128)}, u32[]{:S(2)}) copy-start(s32[32]{0:T(128)} %param.14) | copy-start | bytes 388
  79.9 12.5 %all-to-all-start.3 = ((bf16[32,8,128]{2,1,0:T(8,128)(2,1)}), bf16[32,8,128]{2,1,0:T(8,128)(2,1)S(1)}, u32[]{:S(2)}, u32[]{:S(2)}) async-start(bf16[32,8,128]{2,1,0:T(8,128)(2,1)} %bitcast.9), calls=%async_computation.3 | async-start | bytes 131072 | tf_op jit(solution)/shard_map/all_to_all | solution.py:249

commit v10 on v9

--- a/solution.py
+++ b/solution.py
@@ -91,27 +91,22 @@
     return out[:blocks], out[blocks:]
 
 
-def spread_kernel(place_ref, piece_ref, out_ref):
-    piece = piece_ref[...].astype(BF)
-    for g in range(N_SAME):
-        out_ref[g] = piece
-
-
-def spread_piece(place, amplitudes):
-    width = amplitudes.shape[1]
-    return pl.pallas_call(
-        spread_kernel,
-        grid_spec=pltpu.PrefetchScalarGridSpec(
-            num_scalar_prefetch=1,
-            grid=(1,),
-            in_specs=[pl.BlockSpec((FEW, width), lambda i, s: (s[0], 0))],
-            out_specs=VMEM,
-        ),
-        out_shape=jax.ShapeDtypeStruct((N_SAME, FEW, width), BF),
+def split_kernel(whole_ref, *out_refs):
+    for i, out_ref in enumerate(out_refs):
+        out_ref[...] = whole_ref[i * WIDE // 2 : (i + 1) * WIDE // 2, :]
+
+
+def split(whole):
+    half = jax.ShapeDtypeStruct((WIDE // 2, whole.shape[1]), BF)
+    return pl.pallas_call(
+        split_kernel,
+        in_specs=[VMEM],
+        out_specs=[VMEM] * 2,
+        out_shape=[half] * 2,
         cost_estimate=pl.CostEstimate(flops=1 << 34, bytes_accessed=1 << 20, transcendentals=0),
         compiler_params=pltpu.CompilerParams(vmem_limit_bytes=4 << 20),
-        name="spread_piece",
-    )(place, pltpu.with_memory_space_constraint(amplitudes, pltpu.HBM))
+        name="split",
+    )(whole)
 
 
 def combine_kernel(scale_ref, *refs):
@@ -278,14 +273,13 @@
     per = n_k // N_SAME
     n_half = PARTS * WIDE
     row, place = after((row, place))
-    piece, row, place = after((spread_piece(place, amplitudes), row, place))
-    b0 = exchange(piece, SAME).reshape(WIDE, width)
-    b1 = [shift(b0[: WIDE // 2], -1), shift(b0[WIDE // 2 :], 1)]
-    (i0,), (p0,) = inner_products(row, coupling, [[b0]], [F32], 64)
-
-    b0, p0 = after((b0, p0))
-    o0 = swap(b0)
-    (j0,), (q0,) = inner_products(row, coupling, [[o0]], [BF], 64)
+    piece = lax.dynamic_slice_in_dim(amplitudes, half * FEW, FEW, 0).astype(BF)
+    piece, row, place = after((piece, row, place))
+    b0 = spread(piece, SAME, N_SAME).reshape(WIDE, width)
+    b0 = split(b0)
+    b1 = [shift(b0[0], -1), shift(b0[1], 1)]
+    o0 = [swap(b) for b in b0]
+    (i0, j0), (p0, q0) = inner_products(row, coupling, [b0, o0], [F32, BF])
 
     b1, p0, q0 = after((b1, p0, q0))
     o1 = [swap(b) for b in b1]

time: 108 us -> 105 us (0.972)
  waiting for transfers between devices: 13.9 us -> 10.7 us
  Pallas kernels: 19.6 us -> 17.9 us
    ppermute x2, waiting for transfers between devices: 6.79 us -> 3.6 us  [shift(): return lax.ppermute(x, 'y', [(i, (i + by) % N_Y) for i in range(N_Y)])]
    pallas_call x1, Pallas kernels: 1.65 us -> 0.03 us  [split(): pl.pallas_call(split_kernel, in_specs=[VMEM], out_specs=[VMEM] * 2, out_s...]
    pallas_call x4 -> x3, Pallas kernels: 11.3 us -> 11.3 us  [inner_products(): pl.pallas_call(functools.partial(inner_kernel, counts, slabs, stream), gr...]
  transfers between devices with their start and end apart: 9 -> 10, of which waited for: 4 -> 4; matrix products, arithmetic and copies ran while one was open for 0% -> 0% of each run, Pallas kernels for 11% -> 14%
where the time goes in v10:
time: 105 us
  blocking collectives  64.4 us (61%)
  Pallas kernels  17.9 us (17%)
  waiting for transfers between devices  10.7 us (10%)
  starting transfers between devices  9.46 us (9%)
    all_to_all x4, blocking collectives, exchange(): return lax.all_to_all(x, axes, split_axis=0, concat_axis=0, tiled=True)  64.4 us
    pallas_call x3, Pallas kernels, inner_products(): pl.pallas_call(functools.partial(inner_kernel, counts, slabs, stream), gr...  11.3 us
    all_to_all x1, waiting for transfers between devices, exchange(): return lax.all_to_all(x, axes, split_axis=0, concat_axis=0, tiled=True)  6.18 us
    all_to_all x1, starting transfers between devices, exchange(): return lax.all_to_all(x, axes, split_axis=0, concat_axis=0, tiled=True)  4.74 us
    pallas_call x2, Pallas kernels, forces(): pl.pallas_call(functools.partial(force_kernel, pair), in_specs=[pl.BlockS...  4.16 us
    ppermute x2, waiting for transfers between devices, shift(): return lax.ppermute(x, 'y', [(i, (i + by) % N_Y) for i in range(N_Y)])  3.6 us
    ppermute x2, starting transfers between devices, shift(): return lax.ppermute(x, 'y', [(i, (i + by) % N_Y) for i in range(N_Y)])  3.02 us
  transfers between devices with their start and end apart: 10, of which 4 were waited for; matrix products, arithmetic and copies ran while one was open for 0% of the time, Pallas kernels for 14%

profile of v10, /device:TPU:2, one launch (start us, length us, event | category | flops | bytes accessed | tf_op | source)
XLA Modules:
  0.0 104.6 jit_solution(18397160648433767583)
XLA Ops:
  0.6 0.1 pad_add_fusion.place_ref
  0.7 0.8 dynamic-slice_convert_fusion
  1.6 0.1 broadcast_in_dim.40
  1.6 0.0 slice-start
  1.6 24.5 %all_to_all.25 = bf16[16,16,1024]{2,1,0:T(8,128)(2,1)S(1)} all-to-all(bf16[16,16,1024]{2,1,0:T(8,128)(2,1)S(1)} %broadcast_in_dim.40), channel_id=1, replica_groups=mesh['xh'=2,'y'=4,'xl'=2,'z'=8,'c'=2] {'xl','z'}, dimensions={0} | all-to-all | bytes 1048576 | tf_op jit(solution)/shard_map/all_to_all | solution.py:244
  26.2 0.1 collective-permute-start.2
  26.3 0.5 collective-permute-start.3
  26.8 3.0 %collective-permute-start = (bf16[128,1024]{1,0:T(8,128)(2,1)S(1)}, bf16[128,1024]{1,0:T(8,128)(2,1)S(1)}, u32[]{:S(2)}, u32[]{:S(2)}) collective-permute-start(bf16[128,1024]{1,0:T(8,128)(2,1)S(1)} %get-tuple-element.38.refs_0_), channel_id=1, source_target_pairs={{0,96},{32,0},{64,32},{96,64},{1,97},{33,1},{65,33},{97,65},{2,98}... | collective-permute-start | bytes 786440 | tf_op jit(solution)/shard_map/ppermute | solution.py:256
  29.8 5.6 %inner_products.3 = (bf16[128,32,256]{2,1,0:T(8,128)(2,1)S(1)}, bf16[128,32,256]{2,1,0:T(8,128)(2,1)S(1)}, f32[128,256]{1,0:T(8,128)S(1)}, bf16[128,256]{1,0:T(8,128)(2,1)S(1)}) custom-call(s32[1]{0:T(128)} %bitcast.row_ref, bf16[128,32,1024]{2,1,0:T(8,128)(2,1)S(1)} %bitcast.11, bf16[128,1024]{1,0:T(8,128)(2,1)S(1)} %get-tuple-element.38.refs_0_, ...), custom_call_target="tpu_custom_call" | custom-call | flops 4294967296 | bytes 10485760 | tf_op jit(solution)/shard_map/inner_products/pallas_call | solution.py:72
  35.4 0.2 collective-permute-done.refs_0_
  35.6 3.4 %collective-permute-done.1.refs_1_ = bf16[128,1024]{1,0:T(8,128)(2,1)S(1)} collective-permute-done((bf16[128,1024]{1,0:T(8,128)(2,1)S(1)}, bf16[128,1024]{1,0:T(8,128)(2,1)S(1)}, u32[]{:S(2)}, u32[]{:S(2)}) %collective-permute-start.1) | collective-permute-done | bytes 262176 | tf_op jit(solution)/shard_map/ppermute | solution.py:256
  39.0 0.5 collective-permute-start.5
  39.5 2.8 %inner_products.4 = (bf16[128,32,256]{2,1,0:T(8,128)(2,1)S(1)}, f32[128,256]{1,0:T(8,128)S(1)}) custom-call(s32[1]{0:T(128)} %bitcast.row_ref, bf16[128,32,1024]{2,1,0:T(8,128)(2,1)S(1)} %bitcast.11, bf16[128,1024]{1,0:T(8,128)(2,1)S(1)} %collective-permute-done.refs_0_, bf16[128,1024]{1,0:T(8,128)(2,1)S(1)} %collective-permute-done.1.refs_1_), custom_call_target="tpu_custom_call" | custom-call | flops 2147483648 | bytes 10485760 | tf_op jit(solution)/shard_map/inner_products/pallas_call | solution.py:72
  42.4 0.0 copy-start.1
  42.4 2.9 %inner_products.5 = (bf16[128,32,256]{2,1,0:T(8,128)(2,1)S(1)}, bf16[128,256]{1,0:T(8,128)(2,1)S(1)}) custom-call(s32[1]{0:T(128)} %bitcast.row_ref, bf16[128,32,1024]{2,1,0:T(8,128)(2,1)S(1)} %bitcast.11, bf16[128,1024]{1,0:T(8,128)(2,1)S(1)} %collective-permute-done.4.refs_0_, bf16[128,1024]{1,0:T(8,128)(2,1)S(1)} %collective-permute-done.5.refs_1_), custom_call_target="tpu_custom_call" | custom-call | flops 2147483648 | bytes 10485760 | tf_op jit(solution)/shard_map/inner_products/pallas_call | solution.py:72
  45.2 0.6 collective-permute-start.7
  45.8 0.9 collective-permute-done.7.refs_3_
  46.7 0.1 combine.1
  46.9 13.6 %all_to_all.26.shares_ref = bf16[16,8,512]{2,1,0:T(8,128)(2,1)S(1)} all-to-all(bf16[16,8,512]{2,1,0:T(8,128)(2,1)S(1)} %bitcast.15), channel_id=1, replica_groups=mesh['xh'=2,'y'=4,'xl'=2,'z'=8,'c'=2] {'xl','z'}, dimensions={0} | all-to-all | bytes 262144 | tf_op jit(solution)/shard_map/all_to_all | solution.py:244
  60.5 11.7 %all_to_all.27 = bf16[16,8,512]{2,1,0:T(8,128)(2,1)S(1)} all-to-all(bf16[16,8,512]{2,1,0:T(8,128)(2,1)S(1)} %total_everywhere.1), channel_id=1, replica_groups=mesh['xh'=2,'y'=4,'xl'=2,'z'=8,'c'=2] {'xl','z'}, dimensions={0} | all-to-all | bytes 262144 | tf_op jit(solution)/shard_map/all_to_all | solution.py:244
  72.2 1.8 %forces.2.refs_2_ = bf16[16,8,128]{2,1,0:T(8,128)(2,1)S(1)} custom-call(s32[2]{0:T(128)S(1)} %pad_add_fusion.place_ref, bf16[128,512]{1,0:T(8,128)(2,1)S(1)} %bitcast.13, bf16[128,32,256]{2,1,0:T(8,128)(2,1)S(1)} %get-tuple-element.54.refs_0_, bf16[128,32,256]{2,1,0:T(8,128)(2,1)S(1)} %get-tuple-element.55.refs_1_), custom_call_target="tpu_custom_call" | custom-call | flops 4194304 | bytes 4194304 | tf_op jit(solution)/shard_map/forces/pallas_call | solution.py:182
  73.9 0.0 copy-start.6
  74.0 0.0 copy-start.2
  74.0 0.0 copy-start.3
  74.0 2.4 %forces.3 = bf16[16,2,8,128]{3,2,1,0:T(8,128)(2,1)} custom-call(s32[2]{0:T(128)S(1)} %pad_add_fusion.place_ref, bf16[128,512]{1,0:T(8,128)(2,1)S(1)} %collective-permute-done.8.airy_ref.theirs_ref, bf16[128,32,256]{2,1,0:T(8,128)(2,1)S(1)} %get-tuple-element.52.refs_0_, bf16[128,32,256]{2,1,0:T(8,128)(2,1)S(1)} %get-tuple-element.53.refs_1_, ...), custom_call_target="tpu_custom_call" | custom-call | flops 4194304 | bytes 4194304 | tf_op jit(solution)/shard_map/forces/pallas_call | solution.py:182
  76.5 4.7 %all-to-all-start.3 = ((bf16[32,8,128]{2,1,0:T(8,128)(2,1)}), bf16[32,8,128]{2,1,0:T(8,128)(2,1)S(1)}, u32[]{:S(2)}, u32[]{:S(2)}) async-start(bf16[32,8,128]{2,1,0:T(8,128)(2,1)} %bitcast.7), calls=%async_computation.3 | async-start | bytes 131072 | tf_op jit(solution)/shard_map/all_to_all | solution.py:244
  81.2 1.5 %airy_output.1 = f32[16,2,2,16,128]{4,3,2,1,0:T(8,128)} custom-call(s32[2]{0:T(128)S(1)} %pad_add_fusion.place_ref, bf16[128,512]{1,0:T(8,128)(2,1)S(1)} %bitcast.14, bf16[128,512]{1,0:T(8,128)(2,1)S(1)} %collective-permute-done.8.airy_ref.theirs_ref), custom_call_target="tpu_custom_call" | custom-call | flops 1048576 | bytes 1048576 | tf_op jit(solution)/shard_map/airy_output/pallas_call | solution.py:207
  82.7 0.1 select_add_fusion.base_ref
  82.8 6.2 %all-to-all-done.3 = bf16[32,8,128]{2,1,0:T(8,128)(2,1)S(1)} async-done(((bf16[32,8,128]{2,1,0:T(8,128)(2,1)}), bf16[32,8,128]{2,1,0:T(8,128)(2,1)S(1)}, u32[]{:S(2)}, u32[]{:S(2)}) %all-to-all-start.3) | async-done | bytes 65568 | tf_op jit(solution)/shard_map/all_to_all | solution.py:244
  89.0 0.1 broadcast_in_dim.44
  89.1 14.7 %all_to_all.28.parts_ref = bf16[8,32,8,128]{3,2,1,0:T(8,128)(2,1)S(1)} all-to-all(bf16[8,32,8,128]{3,2,1,0:T(8,128)(2,1)S(1)} %broadcast_in_dim.44), channel_id=1, replica_groups=mesh['xh'=2,'y'=4,'xl'=2,'z'=8,'c'=2] {'xh','y'}, dimensions={0} | all-to-all | bytes 1048576 | tf_op jit(solution)/shard_map/all_to_all | solution.py:244
  103.7 0.9 final_step.1
  (28 shorter events, 0.2 us)
Async XLA Ops:
  1.6 28.2 %slice-start = ((s8[8388608]{0:T(1024)(128)(4,1)}), s8[4194304]{0:T(1024)(128)(4,1)S(1)}, s32[]{:S(2)}) async-start(s8[8388608]{0:T(1024)(128)(4,1)} %bitcast.10), calls=%async_computation.5 | async-start | bytes 8388608
  26.1 3.7 %slice-start.1 = ((s8[8388608]{0:T(1024)(128)(4,1)}), s8[4194304]{0:T(1024)(128)(4,1)S(1)}, s32[]{:S(2)}) async-start(s8[8388608]{0:T(1024)(128)(4,1)} %bitcast.10), calls=%async_computation.6 | async-start | bytes 8388608
  26.2 3.6 %collective-permute-start.2 = (bf16[128,1024]{1,0:T(8,128)(2,1)S(1)}, bf16[128,1024]{1,0:T(8,128)(2,1)S(1)}, u32[]{:S(2)}, u32[]{:S(2)}) collective-permute-start(bf16[128,1024]{1,0:T(8,128)(2,1)S(1)} %get-tuple-element.38.refs_0_), channel_id=1, source_target_pairs={{0,1},{1,0},{2,3},{3,2},{4,5},{5,4},{6,7},{7,6},{8,9},{9,8},{10,11... | collective-permute-start | bytes 786440 | tf_op jit(solution)/shard_map/ppermute | solution.py:252
  26.3 3.5 %collective-permute-start.3 = (bf16[128,1024]{1,0:T(8,128)(2,1)S(1)}, bf16[128,1024]{1,0:T(8,128)(2,1)S(1)}, u32[]{:S(2)}, u32[]{:S(2)}) collective-permute-start(bf16[128,1024]{1,0:T(8,128)(2,1)S(1)} %get-tuple-element.39.refs_1_), channel_id=1, source_target_pairs={{0,1},{1,0},{2,3},{3,2},{4,5},{5,4},{6,7},{7,6},{8,9},{9,8},{10,11... | collective-permute-start | bytes 786440 | tf_op jit(solution)/shard_map/ppermute | solution.py:252
  26.8 8.8 %collective-permute-start = (bf16[128,1024]{1,0:T(8,128)(2,1)S(1)}, bf16[128,1024]{1,0:T(8,128)(2,1)S(1)}, u32[]{:S(2)}, u32[]{:S(2)}) collective-permute-start(bf16[128,1024]{1,0:T(8,128)(2,1)S(1)} %get-tuple-element.38.refs_0_), channel_id=1, source_target_pairs={{0,96},{32,0},{64,32},{96,64},{1,97},{33,1},{65,33},{97,65},{2,98}... | collective-permute-start | bytes 786440 | tf_op jit(solution)/shard_map/ppermute | solution.py:256
  29.8 9.2 %collective-permute-start.1 = (bf16[128,1024]{1,0:T(8,128)(2,1)S(1)}, bf16[128,1024]{1,0:T(8,128)(2,1)S(1)}, u32[]{:S(2)}, u32[]{:S(2)}) collective-permute-start(bf16[128,1024]{1,0:T(8,128)(2,1)S(1)} %get-tuple-element.39.refs_1_), channel_id=1, source_target_pairs={{0,32},{32,64},{64,96},{96,0},{1,33},{33,65},{65,97},{97,1},{2,34}... | collective-permute-start | bytes 786440 | tf_op jit(solution)/shard_map/ppermute | solution.py:256
  39.0 3.3 %collective-permute-start.4 = (bf16[128,1024]{1,0:T(8,128)(2,1)S(1)}, bf16[128,1024]{1,0:T(8,128)(2,1)S(1)}, u32[]{:S(2)}, u32[]{:S(2)}) collective-permute-start(bf16[128,1024]{1,0:T(8,128)(2,1)S(1)} %collective-permute-done.refs_0_), channel_id=1, source_target_pairs={{0,1},{1,0},{2,3},{3,2},{4,5},{5,4},{6,7},{7,6},{8,9},{9,8},{10,11... | collective-permute-start | bytes 786440 | tf_op jit(solution)/shard_map/ppermute | solution.py:252
  39.0 3.3 %collective-permute-start.5 = (bf16[128,1024]{1,0:T(8,128)(2,1)S(1)}, bf16[128,1024]{1,0:T(8,128)(2,1)S(1)}, u32[]{:S(2)}, u32[]{:S(2)}) collective-permute-start(bf16[128,1024]{1,0:T(8,128)(2,1)S(1)} %collective-permute-done.1.refs_1_), channel_id=1, source_target_pairs={{0,1},{1,0},{2,3},{3,2},{4,5},{5,4},{6,7},{7,6},{8,9},{9,8},{10,11... | collective-permute-start | bytes 786440 | tf_op jit(solution)/shard_map/ppermute | solution.py:252
  39.5 6.3 %collective-permute-start.6 = (bf16[128,256]{1,0:T(8,128)(2,1)S(1)}, bf16[128,256]{1,0:T(8,128)(2,1)S(1)}, u32[]{:S(2)}, u32[]{:S(2)}) collective-permute-start(bf16[128,256]{1,0:T(8,128)(2,1)S(1)} %get-tuple-element.48), channel_id=1, source_target_pairs={{0,1},{1,0},{2,3},{3,2},{4,5},{5,4},{6,7},{7,6},{8,9},{9,8},{10,11... | collective-permute-start | bytes 196616 | tf_op jit(solution)/shard_map/ppermute | solution.py:252
  42.4 4.4 %copy-start.1 = (f32[128]{0:T(128)S(1)}, f32[128]{0:T(128)}, u32[]{:S(2)}) copy-start(f32[128]{0:T(128)} %param.12) | copy-start | bytes 1540
  45.2 1.5 %collective-permute-start.7 = (bf16[128,256]{1,0:T(8,128)(2,1)S(1)}, bf16[128,256]{1,0:T(8,128)(2,1)S(1)}, u32[]{:S(2)}, u32[]{:S(2)}) collective-permute-start(bf16[128,256]{1,0:T(8,128)(2,1)S(1)} %get-tuple-element.51), channel_id=1, source_target_pairs={{0,1},{1,0},{2,3},{3,2},{4,5},{5,4},{6,7},{7,6},{8,9},{9,8},{10,11... | collective-permute-start | bytes 196616 | tf_op jit(solution)/shard_map/ppermute | solution.py:252
  72.2 1.8 %collective-permute-start.8 = (bf16[128,512]{1,0:T(8,128)(2,1)S(1)}, bf16[128,512]{1,0:T(8,128)(2,1)S(1)}, u32[]{:S(2)}, u32[]{:S(2)}) collective-permute-start(bf16[128,512]{1,0:T(8,128)(2,1)S(1)} %bitcast.12), channel_id=1, source_target_pairs={{0,1},{1,0},{2,3},{3,2},{4,5},{5,4},{6,7},{7,6},{8,9},{9,8},{10,11... | collective-permute-start | bytes 393224 | tf_op jit(solution)/shard_map/ppermute | solution.py:252
  73.9 2.5 %copy-start.6 = (s32[32]{0:T(128)S(1)}, s32[32]{0:T(128)}, u32[]{:S(2)}) copy-start(s32[32]{0:T(128)} %param.15) | copy-start | bytes 388
  73.9 2.5 %copy-start = (f32[1024]{0:T(1024)S(1)}, f32[1024]{0:T(1024)}, u32[]{:S(2)}) copy-start(f32[1024]{0:T(1024)} %param.13) | copy-start | bytes 12292
  74.0 8.8 %copy-start.2 = (f32[32,1024]{1,0:T(8,128)S(1)}, f32[32,1024]{1,0:T(8,128)}, u32[]{:S(2)}) copy-start(f32[32,1024]{1,0:T(8,128)} %param.8) | copy-start | bytes 393220
  74.0 8.7 %copy-start.3 = (f32[32,1024]{1,0:T(8,128)S(1)}, f32[32,1024]{1,0:T(8,128)}, u32[]{:S(2)}) copy-start(f32[32,1024]{1,0:T(8,128)} %param.9) | copy-start | bytes 393220
  74.0 8.7 %copy-start.4 = (f32[1024]{0:T(1024)S(1)}, f32[1024]{0:T(1024)}, u32[]{:S(2)}) copy-start(f32[1024]{0:T(1024)} %param.11) | copy-start | bytes 12292
  74.0 8.7 %copy-start.5 = (s32[32]{0:T(128)S(1)}, s32[32]{0:T(128)}, u32[]{:S(2)}) copy-start(s32[32]{0:T(128)} %param.14) | copy-start | bytes 388
  76.5 12.5 %all-to-all-start.3 = ((bf16[32,8,128]{2,1,0:T(8,128)(2,1)}), bf16[32,8,128]{2,1,0:T(8,128)(2,1)S(1)}, u32[]{:S(2)}, u32[]{:S(2)}) async-start(bf16[32,8,128]{2,1,0:T(8,128)(2,1)} %bitcast.7), calls=%async_computation.3 | async-start | bytes 131072 | tf_op jit(solution)/shard_map/all_to_all | solution.py:244

commit v11 on v10

--- a/solution.py
+++ b/solution.py
@@ -276,10 +276,9 @@
     piece = lax.dynamic_slice_in_dim(amplitudes, half * FEW, FEW, 0).astype(BF)
     piece, row, place = after((piece, row, place))
     b0 = spread(piece, SAME, N_SAME).reshape(WIDE, width)
-    b0 = split(b0)
-    b1 = [shift(b0[0], -1), shift(b0[1], 1)]
-    o0 = [swap(b) for b in b0]
-    (i0, j0), (p0, q0) = inner_products(row, coupling, [b0, o0], [F32, BF])
+    o0 = swap(b0)
+    b1 = [shift(b, by) for b, by in zip(split(b0), (-1, 1))]
+    (i0, j0), (p0, q0) = inner_products(row, coupling, [[b0], [o0]], [F32, BF])
 
     b1, p0, q0 = after((b1, p0, q0))
     o1 = [swap(b) for b in b1]

time: 105 us -> 105 us (level)
  transfers between devices with their start and end apart: 10 -> 9, of which waited for: 4 -> 4; matrix products, arithmetic and copies ran while one was open for 0% -> 0% of each run, Pallas kernels for 14% -> 14%
where the time goes in v11:
time: 105 us; the launch traced here: 104 us
  blocking collectives  64.2 us (61%)
  Pallas kernels  17.9 us (17%)
  waiting for transfers between devices  10.8 us (10%)
  starting transfers between devices  8.95 us (9%)
  local copies, waits for them, and re-layouts  1.33 us (1%)
    all_to_all x4, blocking collectives, exchange(): return lax.all_to_all(x, axes, split_axis=0, concat_axis=0, tiled=True)  64.2 us
    pallas_call x3, Pallas kernels, inner_products(): pl.pallas_call(functools.partial(inner_kernel, counts, slabs, stream), gr...  11.2 us
    all_to_all x1, waiting for transfers between devices, exchange(): return lax.all_to_all(x, axes, split_axis=0, concat_axis=0, tiled=True)  6.18 us
    all_to_all x1, starting transfers between devices, exchange(): return lax.all_to_all(x, axes, split_axis=0, concat_axis=0, tiled=True)  4.74 us
    pallas_call x2, Pallas kernels, forces(): pl.pallas_call(functools.partial(force_kernel, pair), in_specs=[pl.BlockS...  4.16 us
    ppermute x2, waiting for transfers between devices, shift(): return lax.ppermute(x, 'y', [(i, (i + by) % N_Y) for i in range(N_Y)])  3.74 us
    ppermute x2, starting transfers between devices, shift(): return lax.ppermute(x, 'y', [(i, (i + by) % N_Y) for i in range(N_Y)])  3.09 us
  transfers between devices with their start and end apart: 9, of which 4 were waited for; matrix products, arithmetic and copies ran while one was open for 0% of the time, Pallas kernels for 14%

profile of v11, /device:TPU:2, one launch (start us, length us, event | category | flops | bytes accessed | tf_op | source)
XLA Modules:
  0.0 104.2 jit_solution(9388715841383407942)
XLA Ops:
  0.6 0.1 pad_add_fusion.place_ref
  0.7 0.8 dynamic-slice_convert_fusion
  1.6 0.1 broadcast_in_dim.40
  1.6 24.2 %all_to_all.25 = bf16[16,16,1024]{2,1,0:T(8,128)(2,1)S(1)} all-to-all(bf16[16,16,1024]{2,1,0:T(8,128)(2,1)S(1)} %broadcast_in_dim.40), channel_id=1, replica_groups=mesh['xh'=2,'y'=4,'xl'=2,'z'=8,'c'=2] {'xl','z'}, dimensions={0} | all-to-all | bytes 1048576 | tf_op jit(solution)/shard_map/all_to_all | solution.py:244
  25.9 3.1 %collective-permute-start = (bf16[128,1024]{1,0:T(8,128)(2,1)S(1)}, bf16[128,1024]{1,0:T(8,128)(2,1)S(1)}, u32[]{:S(2)}, u32[]{:S(2)}) collective-permute-start(bf16[128,1024]{1,0:T(8,128)(2,1)S(1)} %get-tuple-element.38), channel_id=1, source_target_pairs={{0,96},{32,0},{64,32},{96,64},{1,97},{33,1},{65,33},{97,65},{2,98}... | collective-permute-start | bytes 786440 | tf_op jit(solution)/shard_map/ppermute | solution.py:256
  29.0 0.3 slice-done.1
  29.3 5.6 %inner_products.3 = (bf16[128,32,256]{2,1,0:T(8,128)(2,1)S(1)}, bf16[128,32,256]{2,1,0:T(8,128)(2,1)S(1)}, f32[128,256]{1,0:T(8,128)S(1)}, bf16[128,256]{1,0:T(8,128)(2,1)S(1)}) custom-call(s32[1]{0:T(128)} %bitcast.row_ref, bf16[128,32,1024]{2,1,0:T(8,128)(2,1)S(1)} %bitcast.11, bf16[256,1024]{1,0:T(8,128)(2,1)S(1)} %bitcast.18, ...), custom_call_target="tpu_custom_call" | custom-call | flops 4294967296 | bytes 10485760 | tf_op jit(solution)/shard_map/inner_products/pallas_call | solution.py:72
  34.9 0.3 collective-permute-done.refs_0_
  35.2 3.4 %collective-permute-done.1.refs_1_ = bf16[128,1024]{1,0:T(8,128)(2,1)S(1)} collective-permute-done((bf16[128,1024]{1,0:T(8,128)(2,1)S(1)}, bf16[128,1024]{1,0:T(8,128)(2,1)S(1)}, u32[]{:S(2)}, u32[]{:S(2)}) %collective-permute-start.1) | collective-permute-done | bytes 262176 | tf_op jit(solution)/shard_map/ppermute | solution.py:256
  38.6 0.5 collective-permute-start.4
  39.1 2.8 %inner_products.4 = (bf16[128,32,256]{2,1,0:T(8,128)(2,1)S(1)}, f32[128,256]{1,0:T(8,128)S(1)}) custom-call(s32[1]{0:T(128)} %bitcast.row_ref, bf16[128,32,1024]{2,1,0:T(8,128)(2,1)S(1)} %bitcast.11, bf16[128,1024]{1,0:T(8,128)(2,1)S(1)} %collective-permute-done.refs_0_, bf16[128,1024]{1,0:T(8,128)(2,1)S(1)} %collective-permute-done.1.refs_1_), custom_call_target="tpu_custom_call" | custom-call | flops 2147483648 | bytes 10485760 | tf_op jit(solution)/shard_map/inner_products/pallas_call | solution.py:72
  42.0 0.0 copy-start.1
  42.0 2.9 %inner_products.5 = (bf16[128,32,256]{2,1,0:T(8,128)(2,1)S(1)}, bf16[128,256]{1,0:T(8,128)(2,1)S(1)}) custom-call(s32[1]{0:T(128)} %bitcast.row_ref, bf16[128,32,1024]{2,1,0:T(8,128)(2,1)S(1)} %bitcast.11, bf16[128,1024]{1,0:T(8,128)(2,1)S(1)} %collective-permute-done.3.refs_0_, bf16[128,1024]{1,0:T(8,128)(2,1)S(1)} %collective-permute-done.4.refs_1_), custom_call_target="tpu_custom_call" | custom-call | flops 2147483648 | bytes 10485760 | tf_op jit(solution)/shard_map/inner_products/pallas_call | solution.py:72
  44.9 0.6 collective-permute-start.6
  45.5 0.9 collective-permute-done.6.refs_3_
  46.4 0.1 combine.1
  46.5 13.6 %all_to_all.26.shares_ref = bf16[16,8,512]{2,1,0:T(8,128)(2,1)S(1)} all-to-all(bf16[16,8,512]{2,1,0:T(8,128)(2,1)S(1)} %bitcast.15), channel_id=1, replica_groups=mesh['xh'=2,'y'=4,'xl'=2,'z'=8,'c'=2] {'xl','z'}, dimensions={0} | all-to-all | bytes 262144 | tf_op jit(solution)/shard_map/all_to_all | solution.py:244
  60.1 11.7 %all_to_all.27 = bf16[16,8,512]{2,1,0:T(8,128)(2,1)S(1)} all-to-all(bf16[16,8,512]{2,1,0:T(8,128)(2,1)S(1)} %total_everywhere.1), channel_id=1, replica_groups=mesh['xh'=2,'y'=4,'xl'=2,'z'=8,'c'=2] {'xl','z'}, dimensions={0} | all-to-all | bytes 262144 | tf_op jit(solution)/shard_map/all_to_all | solution.py:244
  71.8 1.8 %forces.2.refs_2_ = bf16[16,8,128]{2,1,0:T(8,128)(2,1)S(1)} custom-call(s32[2]{0:T(128)S(1)} %pad_add_fusion.place_ref, bf16[128,512]{1,0:T(8,128)(2,1)S(1)} %bitcast.13, bf16[128,32,256]{2,1,0:T(8,128)(2,1)S(1)} %get-tuple-element.54.refs_0_, bf16[128,32,256]{2,1,0:T(8,128)(2,1)S(1)} %get-tuple-element.55.refs_1_), custom_call_target="tpu_custom_call" | custom-call | flops 4194304 | bytes 4194304 | tf_op jit(solution)/shard_map/forces/pallas_call | solution.py:182
  73.5 0.0 copy-start.6
  73.6 0.0 copy-start
  73.6 0.0 copy-start.2
  73.6 0.0 copy-start.4
  73.6 0.0 copy-start.5
  73.6 2.4 %forces.3 = bf16[16,2,8,128]{3,2,1,0:T(8,128)(2,1)} custom-call(s32[2]{0:T(128)S(1)} %pad_add_fusion.place_ref, bf16[128,512]{1,0:T(8,128)(2,1)S(1)} %collective-permute-done.7.airy_ref.theirs_ref, bf16[128,32,256]{2,1,0:T(8,128)(2,1)S(1)} %get-tuple-element.52.refs_0_, bf16[128,32,256]{2,1,0:T(8,128)(2,1)S(1)} %get-tuple-element.53.refs_1_, ...), custom_call_target="tpu_custom_call" | custom-call | flops 4194304 | bytes 4194304 | tf_op jit(solution)/shard_map/forces/pallas_call | solution.py:182
  76.1 4.7 %all-to-all-start.3 = ((bf16[32,8,128]{2,1,0:T(8,128)(2,1)}), bf16[32,8,128]{2,1,0:T(8,128)(2,1)S(1)}, u32[]{:S(2)}, u32[]{:S(2)}) async-start(bf16[32,8,128]{2,1,0:T(8,128)(2,1)} %bitcast.7), calls=%async_computation.3 | async-start | bytes 131072 | tf_op jit(solution)/shard_map/all_to_all | solution.py:244
  80.8 1.5 %airy_output.1 = f32[16,2,2,16,128]{4,3,2,1,0:T(8,128)} custom-call(s32[2]{0:T(128)S(1)} %pad_add_fusion.place_ref, bf16[128,512]{1,0:T(8,128)(2,1)S(1)} %bitcast.14, bf16[128,512]{1,0:T(8,128)(2,1)S(1)} %collective-permute-done.7.airy_ref.theirs_ref), custom_call_target="tpu_custom_call" | custom-call | flops 1048576 | bytes 1048576 | tf_op jit(solution)/shard_map/airy_output/pallas_call | solution.py:207
  82.3 0.1 select_add_fusion.base_ref
  82.4 6.2 %all-to-all-done.3 = bf16[32,8,128]{2,1,0:T(8,128)(2,1)S(1)} async-done(((bf16[32,8,128]{2,1,0:T(8,128)(2,1)}), bf16[32,8,128]{2,1,0:T(8,128)(2,1)S(1)}, u32[]{:S(2)}, u32[]{:S(2)}) %all-to-all-start.3) | async-done | bytes 65568 | tf_op jit(solution)/shard_map/all_to_all | solution.py:244
  88.6 0.1 broadcast_in_dim.44
  88.7 14.7 %all_to_all.28.parts_ref = bf16[8,32,8,128]{3,2,1,0:T(8,128)(2,1)S(1)} all-to-all(bf16[8,32,8,128]{3,2,1,0:T(8,128)(2,1)S(1)} %broadcast_in_dim.44), channel_id=1, replica_groups=mesh['xh'=2,'y'=4,'xl'=2,'z'=8,'c'=2] {'xh','y'}, dimensions={0} | all-to-all | bytes 1048576 | tf_op jit(solution)/shard_map/all_to_all | solution.py:244
  103.4 0.9 final_step.1
  (26 shorter events, 0.2 us)
Async XLA Ops:
  25.8 3.1 %slice-start = ((s8[8388608]{0:T(1024)(128)(4,1)}), s8[4194304]{0:T(1024)(128)(4,1)S(1)}, s32[]{:S(2)}) async-start(s8[8388608]{0:T(1024)(128)(4,1)} %bitcast.10), calls=%async_computation.5 | async-start | bytes 8388608
  25.8 3.5 %slice-start.1 = ((s8[8388608]{0:T(1024)(128)(4,1)}), s8[4194304]{0:T(1024)(128)(4,1)S(1)}, s32[]{:S(2)}) async-start(s8[8388608]{0:T(1024)(128)(4,1)} %bitcast.10), calls=%async_computation.6 | async-start | bytes 8388608
  25.8 3.1 %collective-permute-start.2 = (bf16[256,1024]{1,0:T(8,128)(2,1)S(1)}, bf16[256,1024]{1,0:T(8,128)(2,1)S(1)}, u32[]{:S(2)}, u32[]{:S(2)}) collective-permute-start(bf16[256,1024]{1,0:T(8,128)(2,1)S(1)} %bitcast.16), channel_id=1, source_target_pairs={{0,1},{1,0},{2,3},{3,2},{4,5},{5,4},{6,7},{7,6},{8,9},{9,8},{10,11... | collective-permute-start | bytes 1572872 | tf_op jit(solution)/shard_map/ppermute | solution.py:252
  25.9 9.3 %collective-permute-start = (bf16[128,1024]{1,0:T(8,128)(2,1)S(1)}, bf16[128,1024]{1,0:T(8,128)(2,1)S(1)}, u32[]{:S(2)}, u32[]{:S(2)}) collective-permute-start(bf16[128,1024]{1,0:T(8,128)(2,1)S(1)} %get-tuple-element.38), channel_id=1, source_target_pairs={{0,96},{32,0},{64,32},{96,64},{1,97},{33,1},{65,33},{97,65},{2,98}... | collective-permute-start | bytes 786440 | tf_op jit(solution)/shard_map/ppermute | solution.py:256
  29.0 9.6 %collective-permute-start.1 = (bf16[128,1024]{1,0:T(8,128)(2,1)S(1)}, bf16[128,1024]{1,0:T(8,128)(2,1)S(1)}, u32[]{:S(2)}, u32[]{:S(2)}) collective-permute-start(bf16[128,1024]{1,0:T(8,128)(2,1)S(1)} %get-tuple-element.39), channel_id=1, source_target_pairs={{0,32},{32,64},{64,96},{96,0},{1,33},{33,65},{65,97},{97,1},{2,34}... | collective-permute-start | bytes 786440 | tf_op jit(solution)/shard_map/ppermute | solution.py:256
  38.6 3.3 %collective-permute-start.3 = (bf16[128,1024]{1,0:T(8,128)(2,1)S(1)}, bf16[128,1024]{1,0:T(8,128)(2,1)S(1)}, u32[]{:S(2)}, u32[]{:S(2)}) collective-permute-start(bf16[128,1024]{1,0:T(8,128)(2,1)S(1)} %collective-permute-done.refs_0_), channel_id=1, source_target_pairs={{0,1},{1,0},{2,3},{3,2},{4,5},{5,4},{6,7},{7,6},{8,9},{9,8},{10,11... | collective-permute-start | bytes 786440 | tf_op jit(solution)/shard_map/ppermute | solution.py:252
  38.6 3.3 %collective-permute-start.4 = (bf16[128,1024]{1,0:T(8,128)(2,1)S(1)}, bf16[128,1024]{1,0:T(8,128)(2,1)S(1)}, u32[]{:S(2)}, u32[]{:S(2)}) collective-permute-start(bf16[128,1024]{1,0:T(8,128)(2,1)S(1)} %collective-permute-done.1.refs_1_), channel_id=1, source_target_pairs={{0,1},{1,0},{2,3},{3,2},{4,5},{5,4},{6,7},{7,6},{8,9},{9,8},{10,11... | collective-permute-start | bytes 786440 | tf_op jit(solution)/shard_map/ppermute | solution.py:252
  39.1 6.3 %collective-permute-start.5 = (bf16[128,256]{1,0:T(8,128)(2,1)S(1)}, bf16[128,256]{1,0:T(8,128)(2,1)S(1)}, u32[]{:S(2)}, u32[]{:S(2)}) collective-permute-start(bf16[128,256]{1,0:T(8,128)(2,1)S(1)} %get-tuple-element.48), channel_id=1, source_target_pairs={{0,1},{1,0},{2,3},{3,2},{4,5},{5,4},{6,7},{7,6},{8,9},{9,8},{10,11... | collective-permute-start | bytes 196616 | tf_op jit(solution)/shard_map/ppermute | solution.py:252
  42.0 4.4 %copy-start.1 = (f32[128]{0:T(128)S(1)}, f32[128]{0:T(128)}, u32[]{:S(2)}) copy-start(f32[128]{0:T(128)} %param.12) | copy-start | bytes 1540
  44.9 1.5 %collective-permute-start.6 = (bf16[128,256]{1,0:T(8,128)(2,1)S(1)}, bf16[128,256]{1,0:T(8,128)(2,1)S(1)}, u32[]{:S(2)}, u32[]{:S(2)}) collective-permute-start(bf16[128,256]{1,0:T(8,128)(2,1)S(1)} %get-tuple-element.51), channel_id=1, source_target_pairs={{0,1},{1,0},{2,3},{3,2},{4,5},{5,4},{6,7},{7,6},{8,9},{9,8},{10,11... | collective-permute-start | bytes 196616 | tf_op jit(solution)/shard_map/ppermute | solution.py:252
  71.8 1.8 %collective-permute-start.7 = (bf16[128,512]{1,0:T(8,128)(2,1)S(1)}, bf16[128,512]{1,0:T(8,128)(2,1)S(1)}, u32[]{:S(2)}, u32[]{:S(2)}) collective-permute-start(bf16[128,512]{1,0:T(8,128)(2,1)S(1)} %bitcast.12), channel_id=1, source_target_pairs={{0,1},{1,0},{2,3},{3,2},{4,5},{5,4},{6,7},{7,6},{8,9},{9,8},{10,11... | collective-permute-start | bytes 393224 | tf_op jit(solution)/shard_map/ppermute | solution.py:252
  73.5 2.5 %copy-start.6 = (s32[32]{0:T(128)S(1)}, s32[32]{0:T(128)}, u32[]{:S(2)}) copy-start(s32[32]{0:T(128)} %param.15) | copy-start | bytes 388
  73.6 2.5 %copy-start = (f32[1024]{0:T(1024)S(1)}, f32[1024]{0:T(1024)}, u32[]{:S(2)}) copy-start(f32[1024]{0:T(1024)} %param.13) | copy-start | bytes 12292
  73.6 8.7 %copy-start.2 = (f32[32,1024]{1,0:T(8,128)S(1)}, f32[32,1024]{1,0:T(8,128)}, u32[]{:S(2)}) copy-start(f32[32,1024]{1,0:T(8,128)} %param.8) | copy-start | bytes 393220
  73.6 8.7 %copy-start.3 = (f32[32,1024]{1,0:T(8,128)S(1)}, f32[32,1024]{1,0:T(8,128)}, u32[]{:S(2)}) copy-start(f32[32,1024]{1,0:T(8,128)} %param.9) | copy-start | bytes 393220
  73.6 8.7 %copy-start.4 = (f32[1024]{0:T(1024)S(1)}, f32[1024]{0:T(1024)}, u32[]{:S(2)}) copy-start(f32[1024]{0:T(1024)} %param.11) | copy-start | bytes 12292
  73.6 8.7 %copy-start.5 = (s32[32]{0:T(128)S(1)}, s32[32]{0:T(128)}, u32[]{:S(2)}) copy-start(s32[32]{0:T(128)} %param.14) | copy-start | bytes 388
  76.1 12.5 %all-to-all-start.3 = ((bf16[32,8,128]{2,1,0:T(8,128)(2,1)}), bf16[32,8,128]{2,1,0:T(8,128)(2,1)S(1)}, u32[]{:S(2)}, u32[]{:S(2)}) async-start(bf16[32,8,128]{2,1,0:T(8,128)(2,1)} %bitcast.7), calls=%async_computation.3 | async-start | bytes 131072 | tf_op jit(solution)/shard_map/all_to_all | solution.py:244

commit v12 on v11

--- a/solution.py
+++ b/solution.py
@@ -278,7 +278,7 @@
     b0 = spread(piece, SAME, N_SAME).reshape(WIDE, width)
     o0 = swap(b0)
     b1 = [shift(b, by) for b, by in zip(split(b0), (-1, 1))]
-    (i0, j0), (p0, q0) = inner_products(row, coupling, [[b0], [o0]], [F32, BF])
+    (i0, j0), (p0, q0) = inner_products(row, coupling, [[b0], [o0]], [F32, BF], 64)
 
     b1, p0, q0 = after((b1, p0, q0))
     o1 = [swap(b) for b in b1]

time: 105 us -> 105 us (level)
  no operation moved by 1% of the time
where the time goes in v12:
time: 105 us; the launch traced here: 104 us
  blocking collectives  64.2 us (61%)
  Pallas kernels  18 us (17%)
  waiting for transfers between devices  10.8 us (10%)
  starting transfers between devices  8.94 us (9%)
  local copies, waits for them, and re-layouts  1.33 us (1%)
    all_to_all x4, blocking collectives, exchange(): return lax.all_to_all(x, axes, split_axis=0, concat_axis=0, tiled=True)  64.2 us
    pallas_call x3, Pallas kernels, inner_products(): pl.pallas_call(functools.partial(inner_kernel, counts, slabs, stream), gr...  11.3 us
    all_to_all x1, waiting for transfers between devices, exchange(): return lax.all_to_all(x, axes, split_axis=0, concat_axis=0, tiled=True)  6.18 us
    all_to_all x1, starting transfers between devices, exchange(): return lax.all_to_all(x, axes, split_axis=0, concat_axis=0, tiled=True)  4.74 us
    pallas_call x2, Pallas kernels, forces(): pl.pallas_call(functools.partial(force_kernel, pair), in_specs=[pl.BlockS...  4.16 us
    ppermute x2, waiting for transfers between devices, shift(): return lax.ppermute(x, 'y', [(i, (i + by) % N_Y) for i in range(N_Y)])  3.69 us
    ppermute x2, starting transfers between devices, shift(): return lax.ppermute(x, 'y', [(i, (i + by) % N_Y) for i in range(N_Y)])  3.09 us
  transfers between devices with their start and end apart: 9, of which 4 were waited for; matrix products, arithmetic and copies ran while one was open for 0% of the time, Pallas kernels for 14%

profile of v12, /device:TPU:2, one launch (start us, length us, event | category | flops | bytes accessed | tf_op | source)
XLA Modules:
  0.0 104.2 jit_solution(5601007658819792475)
XLA Ops:
  0.6 0.1 pad_add_fusion.place_ref
  0.7 0.8 dynamic-slice_convert_fusion
  1.6 0.1 broadcast_in_dim.40
  1.6 24.2 %all_to_all.25 = bf16[16,16,1024]{2,1,0:T(8,128)(2,1)S(1)} all-to-all(bf16[16,16,1024]{2,1,0:T(8,128)(2,1)S(1)} %broadcast_in_dim.40), channel_id=1, replica_groups=mesh['xh'=2,'y'=4,'xl'=2,'z'=8,'c'=2] {'xl','z'}, dimensions={0} | all-to-all | bytes 1048576 | tf_op jit(solution)/shard_map/all_to_all | solution.py:244
  25.9 3.1 %collective-permute-start = (bf16[128,1024]{1,0:T(8,128)(2,1)S(1)}, bf16[128,1024]{1,0:T(8,128)(2,1)S(1)}, u32[]{:S(2)}, u32[]{:S(2)}) collective-permute-start(bf16[128,1024]{1,0:T(8,128)(2,1)S(1)} %get-tuple-element.38), channel_id=1, source_target_pairs={{0,96},{32,0},{64,32},{96,64},{1,97},{33,1},{65,33},{97,65},{2,98}... | collective-permute-start | bytes 786440 | tf_op jit(solution)/shard_map/ppermute | solution.py:256
  29.0 0.3 slice-done.1
  29.3 5.6 %inner_products.3 = (bf16[128,32,256]{2,1,0:T(8,128)(2,1)S(1)}, bf16[128,32,256]{2,1,0:T(8,128)(2,1)S(1)}, f32[128,256]{1,0:T(8,128)S(1)}, bf16[128,256]{1,0:T(8,128)(2,1)S(1)}) custom-call(s32[1]{0:T(128)} %bitcast.row_ref, bf16[128,32,1024]{2,1,0:T(8,128)(2,1)S(1)} %bitcast.11, bf16[256,1024]{1,0:T(8,128)(2,1)S(1)} %bitcast.18, ...), custom_call_target="tpu_custom_call" | custom-call | flops 4294967296 | bytes 10485760 | tf_op jit(solution)/shard_map/inner_products/pallas_call | solution.py:72
  34.9 0.3 collective-permute-done.refs_0_
  35.2 3.4 %collective-permute-done.1.refs_1_ = bf16[128,1024]{1,0:T(8,128)(2,1)S(1)} collective-permute-done((bf16[128,1024]{1,0:T(8,128)(2,1)S(1)}, bf16[128,1024]{1,0:T(8,128)(2,1)S(1)}, u32[]{:S(2)}, u32[]{:S(2)}) %collective-permute-start.1) | collective-permute-done | bytes 262176 | tf_op jit(solution)/shard_map/ppermute | solution.py:256
  38.6 0.5 collective-permute-start.4
  39.1 2.8 %inner_products.4 = (bf16[128,32,256]{2,1,0:T(8,128)(2,1)S(1)}, f32[128,256]{1,0:T(8,128)S(1)}) custom-call(s32[1]{0:T(128)} %bitcast.row_ref, bf16[128,32,1024]{2,1,0:T(8,128)(2,1)S(1)} %bitcast.11, bf16[128,1024]{1,0:T(8,128)(2,1)S(1)} %collective-permute-done.refs_0_, bf16[128,1024]{1,0:T(8,128)(2,1)S(1)} %collective-permute-done.1.refs_1_), custom_call_target="tpu_custom_call" | custom-call | flops 2147483648 | bytes 10485760 | tf_op jit(solution)/shard_map/inner_products/pallas_call | solution.py:72
  42.0 0.0 copy-start.1
  42.0 2.9 %inner_products.5 = (bf16[128,32,256]{2,1,0:T(8,128)(2,1)S(1)}, bf16[128,256]{1,0:T(8,128)(2,1)S(1)}) custom-call(s32[1]{0:T(128)} %bitcast.row_ref, bf16[128,32,1024]{2,1,0:T(8,128)(2,1)S(1)} %bitcast.11, bf16[128,1024]{1,0:T(8,128)(2,1)S(1)} %collective-permute-done.3.refs_0_, bf16[128,1024]{1,0:T(8,128)(2,1)S(1)} %collective-permute-done.4.refs_1_), custom_call_target="tpu_custom_call" | custom-call | flops 2147483648 | bytes 10485760 | tf_op jit(solution)/shard_map/inner_products/pallas_call | solution.py:72
  44.9 0.6 collective-permute-start.6
  45.5 0.9 collective-permute-done.6.refs_3_
  46.4 0.1 combine.1
  46.5 13.6 %all_to_all.26.shares_ref = bf16[16,8,512]{2,1,0:T(8,128)(2,1)S(1)} all-to-all(bf16[16,8,512]{2,1,0:T(8,128)(2,1)S(1)} %bitcast.15), channel_id=1, replica_groups=mesh['xh'=2,'y'=4,'xl'=2,'z'=8,'c'=2] {'xl','z'}, dimensions={0} | all-to-all | bytes 262144 | tf_op jit(solution)/shard_map/all_to_all | solution.py:244
  60.1 11.7 %all_to_all.27 = bf16[16,8,512]{2,1,0:T(8,128)(2,1)S(1)} all-to-all(bf16[16,8,512]{2,1,0:T(8,128)(2,1)S(1)} %total_everywhere.1), channel_id=1, replica_groups=mesh['xh'=2,'y'=4,'xl'=2,'z'=8,'c'=2] {'xl','z'}, dimensions={0} | all-to-all | bytes 262144 | tf_op jit(solution)/shard_map/all_to_all | solution.py:244
  71.8 1.8 %forces.2.refs_2_ = bf16[16,8,128]{2,1,0:T(8,128)(2,1)S(1)} custom-call(s32[2]{0:T(128)S(1)} %pad_add_fusion.place_ref, bf16[128,512]{1,0:T(8,128)(2,1)S(1)} %bitcast.13, bf16[128,32,256]{2,1,0:T(8,128)(2,1)S(1)} %get-tuple-element.54.refs_0_, bf16[128,32,256]{2,1,0:T(8,128)(2,1)S(1)} %get-tuple-element.55.refs_1_), custom_call_target="tpu_custom_call" | custom-call | flops 4194304 | bytes 4194304 | tf_op jit(solution)/shard_map/forces/pallas_call | solution.py:182
  73.5 0.0 copy-start.6
  73.6 0.0 copy-start
  73.6 0.0 copy-start.2
  73.6 0.0 copy-start.3
  73.6 0.0 copy-start.5
  73.6 2.4 %forces.3 = bf16[16,2,8,128]{3,2,1,0:T(8,128)(2,1)} custom-call(s32[2]{0:T(128)S(1)} %pad_add_fusion.place_ref, bf16[128,512]{1,0:T(8,128)(2,1)S(1)} %collective-permute-done.7.airy_ref.theirs_ref, bf16[128,32,256]{2,1,0:T(8,128)(2,1)S(1)} %get-tuple-element.52.refs_0_, bf16[128,32,256]{2,1,0:T(8,128)(2,1)S(1)} %get-tuple-element.53.refs_1_, ...), custom_call_target="tpu_custom_call" | custom-call | flops 4194304 | bytes 4194304 | tf_op jit(solution)/shard_map/forces/pallas_call | solution.py:182
  76.1 4.7 %all-to-all-start.3 = ((bf16[32,8,128]{2,1,0:T(8,128)(2,1)}), bf16[32,8,128]{2,1,0:T(8,128)(2,1)S(1)}, u32[]{:S(2)}, u32[]{:S(2)}) async-start(bf16[32,8,128]{2,1,0:T(8,128)(2,1)} %bitcast.7), calls=%async_computation.3 | async-start | bytes 131072 | tf_op jit(solution)/shard_map/all_to_all | solution.py:244
  80.8 1.5 %airy_output.1 = f32[16,2,2,16,128]{4,3,2,1,0:T(8,128)} custom-call(s32[2]{0:T(128)S(1)} %pad_add_fusion.place_ref, bf16[128,512]{1,0:T(8,128)(2,1)S(1)} %bitcast.14, bf16[128,512]{1,0:T(8,128)(2,1)S(1)} %collective-permute-done.7.airy_ref.theirs_ref), custom_call_target="tpu_custom_call" | custom-call | flops 1048576 | bytes 1048576 | tf_op jit(solution)/shard_map/airy_output/pallas_call | solution.py:207
  82.3 0.1 select_add_fusion.base_ref
  82.4 6.2 %all-to-all-done.3 = bf16[32,8,128]{2,1,0:T(8,128)(2,1)S(1)} async-done(((bf16[32,8,128]{2,1,0:T(8,128)(2,1)}), bf16[32,8,128]{2,1,0:T(8,128)(2,1)S(1)}, u32[]{:S(2)}, u32[]{:S(2)}) %all-to-all-start.3) | async-done | bytes 65568 | tf_op jit(solution)/shard_map/all_to_all | solution.py:244
  88.6 0.1 broadcast_in_dim.44
  88.7 14.7 %all_to_all.28.parts_ref = bf16[8,32,8,128]{3,2,1,0:T(8,128)(2,1)S(1)} all-to-all(bf16[8,32,8,128]{3,2,1,0:T(8,128)(2,1)S(1)} %broadcast_in_dim.44), channel_id=1, replica_groups=mesh['xh'=2,'y'=4,'xl'=2,'z'=8,'c'=2] {'xh','y'}, dimensions={0} | all-to-all | bytes 1048576 | tf_op jit(solution)/shard_map/all_to_all | solution.py:244
  103.4 0.9 final_step.1
  (26 shorter events, 0.2 us)
Async XLA Ops:
  25.8 3.1 %slice-start = ((s8[8388608]{0:T(1024)(128)(4,1)}), s8[4194304]{0:T(1024)(128)(4,1)S(1)}, s32[]{:S(2)}) async-start(s8[8388608]{0:T(1024)(128)(4,1)} %bitcast.10), calls=%async_computation.5 | async-start | bytes 8388608
  25.8 3.5 %slice-start.1 = ((s8[8388608]{0:T(1024)(128)(4,1)}), s8[4194304]{0:T(1024)(128)(4,1)S(1)}, s32[]{:S(2)}) async-start(s8[8388608]{0:T(1024)(128)(4,1)} %bitcast.10), calls=%async_computation.6 | async-start | bytes 8388608
  25.8 3.1 %collective-permute-start.2 = (bf16[256,1024]{1,0:T(8,128)(2,1)S(1)}, bf16[256,1024]{1,0:T(8,128)(2,1)S(1)}, u32[]{:S(2)}, u32[]{:S(2)}) collective-permute-start(bf16[256,1024]{1,0:T(8,128)(2,1)S(1)} %bitcast.16), channel_id=1, source_target_pairs={{0,1},{1,0},{2,3},{3,2},{4,5},{5,4},{6,7},{7,6},{8,9},{9,8},{10,11... | collective-permute-start | bytes 1572872 | tf_op jit(solution)/shard_map/ppermute | solution.py:252
  25.9 9.3 %collective-permute-start = (bf16[128,1024]{1,0:T(8,128)(2,1)S(1)}, bf16[128,1024]{1,0:T(8,128)(2,1)S(1)}, u32[]{:S(2)}, u32[]{:S(2)}) collective-permute-start(bf16[128,1024]{1,0:T(8,128)(2,1)S(1)} %get-tuple-element.38), channel_id=1, source_target_pairs={{0,96},{32,0},{64,32},{96,64},{1,97},{33,1},{65,33},{97,65},{2,98}... | collective-permute-start | bytes 786440 | tf_op jit(solution)/shard_map/ppermute | solution.py:256
  29.0 9.6 %collective-permute-start.1 = (bf16[128,1024]{1,0:T(8,128)(2,1)S(1)}, bf16[128,1024]{1,0:T(8,128)(2,1)S(1)}, u32[]{:S(2)}, u32[]{:S(2)}) collective-permute-start(bf16[128,1024]{1,0:T(8,128)(2,1)S(1)} %get-tuple-element.39), channel_id=1, source_target_pairs={{0,32},{32,64},{64,96},{96,0},{1,33},{33,65},{65,97},{97,1},{2,34}... | collective-permute-start | bytes 786440 | tf_op jit(solution)/shard_map/ppermute | solution.py:256
  38.6 3.3 %collective-permute-start.3 = (bf16[128,1024]{1,0:T(8,128)(2,1)S(1)}, bf16[128,1024]{1,0:T(8,128)(2,1)S(1)}, u32[]{:S(2)}, u32[]{:S(2)}) collective-permute-start(bf16[128,1024]{1,0:T(8,128)(2,1)S(1)} %collective-permute-done.refs_0_), channel_id=1, source_target_pairs={{0,1},{1,0},{2,3},{3,2},{4,5},{5,4},{6,7},{7,6},{8,9},{9,8},{10,11... | collective-permute-start | bytes 786440 | tf_op jit(solution)/shard_map/ppermute | solution.py:252
  38.6 3.3 %collective-permute-start.4 = (bf16[128,1024]{1,0:T(8,128)(2,1)S(1)}, bf16[128,1024]{1,0:T(8,128)(2,1)S(1)}, u32[]{:S(2)}, u32[]{:S(2)}) collective-permute-start(bf16[128,1024]{1,0:T(8,128)(2,1)S(1)} %collective-permute-done.1.refs_1_), channel_id=1, source_target_pairs={{0,1},{1,0},{2,3},{3,2},{4,5},{5,4},{6,7},{7,6},{8,9},{9,8},{10,11... | collective-permute-start | bytes 786440 | tf_op jit(solution)/shard_map/ppermute | solution.py:252
  39.1 6.3 %collective-permute-start.5 = (bf16[128,256]{1,0:T(8,128)(2,1)S(1)}, bf16[128,256]{1,0:T(8,128)(2,1)S(1)}, u32[]{:S(2)}, u32[]{:S(2)}) collective-permute-start(bf16[128,256]{1,0:T(8,128)(2,1)S(1)} %get-tuple-element.48), channel_id=1, source_target_pairs={{0,1},{1,0},{2,3},{3,2},{4,5},{5,4},{6,7},{7,6},{8,9},{9,8},{10,11... | collective-permute-start | bytes 196616 | tf_op jit(solution)/shard_map/ppermute | solution.py:252
  42.0 4.4 %copy-start.1 = (f32[128]{0:T(128)S(1)}, f32[128]{0:T(128)}, u32[]{:S(2)}) copy-start(f32[128]{0:T(128)} %param.12) | copy-start | bytes 1540
  44.9 1.5 %collective-permute-start.6 = (bf16[128,256]{1,0:T(8,128)(2,1)S(1)}, bf16[128,256]{1,0:T(8,128)(2,1)S(1)}, u32[]{:S(2)}, u32[]{:S(2)}) collective-permute-start(bf16[128,256]{1,0:T(8,128)(2,1)S(1)} %get-tuple-element.51), channel_id=1, source_target_pairs={{0,1},{1,0},{2,3},{3,2},{4,5},{5,4},{6,7},{7,6},{8,9},{9,8},{10,11... | collective-permute-start | bytes 196616 | tf_op jit(solution)/shard_map/ppermute | solution.py:252
  71.8 1.8 %collective-permute-start.7 = (bf16[128,512]{1,0:T(8,128)(2,1)S(1)}, bf16[128,512]{1,0:T(8,128)(2,1)S(1)}, u32[]{:S(2)}, u32[]{:S(2)}) collective-permute-start(bf16[128,512]{1,0:T(8,128)(2,1)S(1)} %bitcast.12), channel_id=1, source_target_pairs={{0,1},{1,0},{2,3},{3,2},{4,5},{5,4},{6,7},{7,6},{8,9},{9,8},{10,11... | collective-permute-start | bytes 393224 | tf_op jit(solution)/shard_map/ppermute | solution.py:252
  73.5 2.5 %copy-start.6 = (s32[32]{0:T(128)S(1)}, s32[32]{0:T(128)}, u32[]{:S(2)}) copy-start(s32[32]{0:T(128)} %param.15) | copy-start | bytes 388
  73.6 2.5 %copy-start = (f32[1024]{0:T(1024)S(1)}, f32[1024]{0:T(1024)}, u32[]{:S(2)}) copy-start(f32[1024]{0:T(1024)} %param.13) | copy-start | bytes 12292
  73.6 8.7 %copy-start.2 = (f32[32,1024]{1,0:T(8,128)S(1)}, f32[32,1024]{1,0:T(8,128)}, u32[]{:S(2)}) copy-start(f32[32,1024]{1,0:T(8,128)} %param.8) | copy-start | bytes 393220
  73.6 8.7 %copy-start.3 = (f32[32,1024]{1,0:T(8,128)S(1)}, f32[32,1024]{1,0:T(8,128)}, u32[]{:S(2)}) copy-start(f32[32,1024]{1,0:T(8,128)} %param.9) | copy-start | bytes 393220
  73.6 8.7 %copy-start.4 = (f32[1024]{0:T(1024)S(1)}, f32[1024]{0:T(1024)}, u32[]{:S(2)}) copy-start(f32[1024]{0:T(1024)} %param.11) | copy-start | bytes 12292
  73.6 8.7 %copy-start.5 = (s32[32]{0:T(128)S(1)}, s32[32]{0:T(128)}, u32[]{:S(2)}) copy-start(s32[32]{0:T(128)} %param.14) | copy-start | bytes 388
  76.1 12.5 %all-to-all-start.3 = ((bf16[32,8,128]{2,1,0:T(8,128)(2,1)}), bf16[32,8,128]{2,1,0:T(8,128)(2,1)S(1)}, u32[]{:S(2)}, u32[]{:S(2)}) async-start(bf16[32,8,128]{2,1,0:T(8,128)(2,1)} %bitcast.7), calls=%async_computation.3 | async-start | bytes 131072 | tf_op jit(solution)/shard_map/all_to_all | solution.py:244
